TPU v7x, 32 devices: a whole 2x2x4 slice. The times are simulated.
32 devices in a mesh: grp: 8 (over y, x, core), mem: 4 (over z).
Axes of the slice: x: 2, y: 2, z: 4, core: 2. Of those that a mesh axis runs over, the one named last changes fastest.
Arguments:
- stem: bfloat16 [2, 8, 4, 1024, 256], P(None, 'grp', 'mem'), may hold values from -6 to 6
- branches: bfloat16 [3, 2, 256, 256], replicated, may hold values from -0.25 to 0.25
- mode_order: int32 [3, 256], replicated, may hold values from 0 to 255, each once within a row
Outputs:
- contracted: bfloat16 [2, 8, 4, 1024, 256], P(None, 'grp', 'mem')
Inputs may be any that keep to these rules, and one draw needn't show every extreme that they name: Each row of mode_order names every number below 256 once.
All inputs are finite; a program needn't handle non-finite values.
Results may differ from a plain program's by a relative error of at most 0.0057.
Values may be sent and summed in bfloat16 or wider, within the bound.
No kernel may reach another device: no remote copies, remote signals or barrier semaphores. Data moves between devices by JAX's collectives and lax.ppermute only.
A program may use at most 64 MiB of HBM per device.

v0:
```python
import jax
import jax.numpy as jnp
from jax import lax
from jax.sharding import PartitionSpec as P


def real_matrix(branches, mode_order, section_no):
    weight = jnp.take(branches[section_no], mode_order[section_no], axis=1)
    upper = jnp.concatenate([weight[0], weight[1]], axis=1)
    lower = jnp.concatenate([-weight[1], weight[0]], axis=1)
    return jnp.concatenate([upper, lower], axis=0)


def contract_columns(arrived, real_form):
    row_count = arrived.shape[-1]
    half = real_form.shape[1] // 2
    joined = arrived.reshape(2 * half, row_count)
    result = lax.dot_general(
        real_form, joined, (((0,), (0,)), ((), ())), preferred_element_type=jnp.float32
    )
    return result.astype(jnp.bfloat16).reshape(2, half, row_count)


def local(stem, branches, mode_order):
    forms = [real_matrix(branches, mode_order, section_no) for section_no in range(3)]
    row_count = stem.shape[3]
    width = stem.shape[4]
    inner_count = lax.axis_size("mem")
    outer_count = lax.axis_size("grp")
    local_stem = stem[:, 0, 0]
    joined = jnp.concatenate([local_stem[0], local_stem[1]], axis=-1)
    first_full = lax.dot_general(
        forms[0], joined, (((0,), (1,)), ((), ())), preferred_element_type=jnp.float32
    )
    first = first_full.astype(jnp.bfloat16).reshape(2, width, row_count)
    inner_pieces = first.reshape(2, inner_count, width // inner_count, row_count)
    arrived_inner = lax.all_to_all(inner_pieces, "mem", split_axis=1, concat_axis=1, tiled=True)
    second = contract_columns(arrived_inner, forms[1])
    outer_pieces = second.reshape(2, outer_count, width // outer_count, row_count)
    arrived_outer = lax.all_to_all(outer_pieces, "grp", split_axis=1, concat_axis=1, tiled=True)
    final = contract_columns(arrived_outer, forms[2])
    return jnp.transpose(final, (0, 2, 1)).reshape(2, 1, 1, row_count, width)


def solution(mesh):
    in_specs = (P(None, "grp", "mem", None, None), P(), P())
    out_specs = P(None, "grp", "mem", None, None)
    return jax.shard_map(local, mesh=mesh, in_specs=in_specs, out_specs=out_specs, check_vma=False)
```

profile of v0, /device:TPU:0, one launch (start us, length us, event | category | flops | bytes accessed | tf_op | source)
XLA Modules:
  0.0 63.1 jit_solution(9508452276522880496)
XLA Ops:
  0.0 0.8 %fusion.37 = (s32[1,256]{1,0:T(1,128)S(1)}, s32[1,256]{1,0:T(1,128)S(1)}, s32[1,256]{1,0:T(1,128)S(1)}) fusion(s32[3,256]{1,0:T(4,128)} %param.7), kind=kLoop, calls=%fused_computation.66 | loop fusion | bytes 6144 | tf_op jit(solution)/shard_map/slice | solution.py:8
  0.8 1.2 %fusion.33 = (bf16[1,2,256,256]{3,2,1,0:T(8,128)(2,1)S(1)}, bf16[1,2,256,256]{3,2,1,0:T(8,128)(2,1)S(1)}, bf16[1,2,256,256]{3,2,1,0:T(8,128)(2,1)S(1)}) fusion(bf16[3,2,256,256]{3,2,1,0:T(8,128)(2,1)} %param.6), kind=kLoop, calls=%fused_computation.62 | loop fusion | bytes 1572864 | tf_op jit(solution)/shard_map/slice | solution.py:8
  2.0 0.5 copy_bitcast_fusion
  2.5 1.2 %gather_fusion.2 = bf16[256,2,256]{2,1,0:T(2,128)(2,1)S(1)} fusion(bf16[2,256,256]{2,0,1:T(2,128)(2,1)S(1)} %get-tuple-element.26, s32[1024]{0:T(1024)S(1)} %pad_clamp_fusion), kind=kCustom, calls=%fused_computation.2.clone | custom fusion | bytes 525312 | tf_op jit(solution)/shard_map/jit(_take)/gather | solution.py:8
  3.8 0.9 %fusion.26 = bf16[2,256,256]{2,0,1:T(2,128)(2,1)S(1)} fusion(bf16[256,2,256]{2,1,0:T(2,128)(2,1)S(1)} %gather_fusion.2, pred[256]{0:T(512)(128)(4,1)S(1)} %compare_and_fusion), kind=kLoop, calls=%fused_computation.40 | loop fusion | flops 131072 | bytes 524544 | tf_op jit(solution)/shard_map/jit(_take)/select_n | solution.py:8
  4.7 0.0 copy-start
  4.8 0.4 fusion.36
  5.2 0.8 %copy-done = bf16[2,1,1,1024,256]{4,3,2,1,0:T(8,128)(2,1)S(1)} copy-done((bf16[2,1,1,1024,256]{4,3,2,1,0:T(8,128)(2,1)S(1)}, bf16[2,1,1,1024,256]{4,3,2,1,0:T(8,128)(2,1)}, u32[]{:S(2)}) %copy-start) | copy-done | bytes 1048600
  6.0 0.1 slice_bitcast_fusion.1
  6.0 0.8 %convolution_convert_fusion.2 = bf16[512,1024]{1,0:T(8,128)(2,1)S(1)} fusion(bf16[1024,256]{1,0:T(8,128)(2,1)S(1)} %get-tuple-element.13, bf16[1024,256]{1,0:T(8,128)(2,1)S(1)} %get-tuple-element.12, bf16[256,256]{1,0:T(8,128)(2,1)S(1)} %bitcast.56, bf16[256,256]{1,0:T(8,128)(2,1)S(1)} %get-tuple-element.10, bf16[256,256]{1,0:T(8,128)(2,1)S(1)} %get-tuple-element.11), kind=kOutput, calls=%fused_computation.5 | convolution fusion | flops 541589504 | bytes 2490368 | tf_op jit(solution)/shard_map/dot_general | solution.py:32
  6.8 1.1 %copy.29 = bf16[2,4,64,1024]{3,2,0,1:T(8,128)(2,1)} copy(bf16[2,4,64,1024]{3,2,1,0:T(8,128)(2,1)S(1)} %bitcast.48) | data formatting | bytes 2097152 | tf_op jit(solution)/shard_map/reshape;reshape | solution.py:36
  7.9 6.3 %all-to-all-start = ((bf16[2,4,64,1024]{3,2,0,1:T(8,128)(2,1)}), bf16[2,4,64,1024]{3,2,0,1:T(8,128)(2,1)S(1)}, u32[]{:S(2)}, u32[]{:S(2)}) async-start(bf16[2,4,64,1024]{3,2,0,1:T(8,128)(2,1)} %copy.29), calls=%async_computation | async-start | bytes 2097152 | tf_op jit(solution)/shard_map/all_to_all | solution.py:37
  14.2 1.2 %gather_fusion.1 = bf16[256,2,256]{2,1,0:T(2,128)(2,1)S(1)} fusion(bf16[2,256,256]{2,0,1:T(2,128)(2,1)S(1)} %get-tuple-element.27, s32[1024]{0:T(1024)S(1)} %pad_clamp_fusion.1), kind=kCustom, calls=%fused_computation.1.clone | custom fusion | bytes 525312 | tf_op jit(solution)/shard_map/jit(_take)/gather | solution.py:8
  15.5 0.9 %fusion.25 = bf16[2,256,256]{2,0,1:T(2,128)(2,1)S(1)} fusion(bf16[256,2,256]{2,1,0:T(2,128)(2,1)S(1)} %gather_fusion.1, pred[256]{0:T(512)(128)(4,1)S(1)} %compare_and_fusion.1), kind=kLoop, calls=%fused_computation.39 | loop fusion | flops 131072 | bytes 524544 | tf_op jit(solution)/shard_map/jit(_take)/select_n | solution.py:8
  16.4 0.4 fusion.35
  16.8 0.3 copy.55
  17.1 1.2 %gather_fusion = bf16[256,2,256]{2,1,0:T(2,128)(2,1)S(1)} fusion(bf16[2,256,256]{2,0,1:T(2,128)(2,1)S(1)} %bitcast.53, s32[1024]{0:T(1024)S(1)} %pad_clamp_fusion.2), kind=kCustom, calls=%fused_computation.clone | custom fusion | bytes 525312 | tf_op jit(solution)/shard_map/jit(_take)/gather | solution.py:8
  18.4 21.5 %all-to-all-done = bf16[2,4,64,1024]{3,2,0,1:T(8,128)(2,1)S(1)} async-done(((bf16[2,4,64,1024]{3,2,0,1:T(8,128)(2,1)}), bf16[2,4,64,1024]{3,2,0,1:T(8,128)(2,1)S(1)}, u32[]{:S(2)}, u32[]{:S(2)}) %all-to-all-start) | async-done | bytes 1048608 | tf_op jit(solution)/shard_map/all_to_all | solution.py:37
  39.9 0.1 copy.30
  40.0 0.7 %convolution_convert_fusion.1 = bf16[512,1024]{1,0:T(8,128)(2,1)S(1)} fusion(bf16[512,1024]{1,0:T(8,128)(2,1)S(1)} %bitcast.49, bf16[256,256]{1,0:T(8,128)(2,1)S(1)} %bitcast.54, bf16[256,256]{1,0:T(8,128)(2,1)S(1)} %get-tuple-element.8, bf16[256,256]{1,0:T(8,128)(2,1)S(1)} %get-tuple-element.9), kind=kOutput, calls=%fused_computation.4 | convolution fusion | flops 539492352 | bytes 2490368 | tf_op jit(solution)/shard_map/dot_general | solution.py:18
  40.7 1.1 %copy.31 = bf16[2,8,32,1024]{3,2,0,1:T(8,128)(2,1)} copy(bf16[2,8,32,1024]{3,2,1,0:T(8,128)(2,1)S(1)} %bitcast.51) | data formatting | bytes 2097152 | tf_op jit(solution)/shard_map/reshape;reshape | solution.py:39
  41.8 3.7 %all-to-all-start.1 = ((bf16[2,8,32,1024]{3,2,0,1:T(8,128)(2,1)}), bf16[2,8,32,1024]{3,2,0,1:T(8,128)(2,1)S(1)}, u32[]{:S(2)}, u32[]{:S(2)}) async-start(bf16[2,8,32,1024]{3,2,0,1:T(8,128)(2,1)} %copy.31), calls=%async_computation.1 | async-start | bytes 2097152 | tf_op jit(solution)/shard_map/all_to_all | solution.py:40
  45.5 0.9 %fusion.24 = bf16[2,256,256]{2,0,1:T(2,128)(2,1)S(1)} fusion(bf16[256,2,256]{2,1,0:T(2,128)(2,1)S(1)} %gather_fusion, pred[256]{0:T(512)(128)(4,1)S(1)} %compare_and_fusion.2), kind=kLoop, calls=%fused_computation.38 | loop fusion | flops 131072 | bytes 524544 | tf_op jit(solution)/shard_map/jit(_take)/select_n | solution.py:8
  46.5 0.4 fusion.34
  46.9 14.0 %all-to-all-done.1 = bf16[2,8,32,1024]{3,2,0,1:T(8,128)(2,1)S(1)} async-done(((bf16[2,8,32,1024]{3,2,0,1:T(8,128)(2,1)}), bf16[2,8,32,1024]{3,2,0,1:T(8,128)(2,1)S(1)}, u32[]{:S(2)}, u32[]{:S(2)}) %all-to-all-start.1) | async-done | bytes 1048608 | tf_op jit(solution)/shard_map/all_to_all | solution.py:40
  60.9 0.1 copy.32
  61.0 0.7 %convolution_convert_fusion = bf16[512,1024]{1,0:T(8,128)(2,1)S(1)} fusion(bf16[512,1024]{1,0:T(8,128)(2,1)S(1)} %bitcast.50, bf16[256,256]{1,0:T(8,128)(2,1)S(1)} %bitcast.55, bf16[256,256]{1,0:T(8,128)(2,1)S(1)} %get-tuple-element.6, bf16[256,256]{1,0:T(8,128)(2,1)S(1)} %get-tuple-element.7), kind=kOutput, calls=%fused_computation.3 | convolution fusion | flops 539492352 | bytes 2490368 | tf_op jit(solution)/shard_map/dot_general | solution.py:18
  61.8 1.3 %copy.33 = bf16[2,256,1024]{1,2,0:T(8,128)(2,1)} copy(bf16[2,256,1024]{2,1,0:T(8,128)(2,1)S(1)} %bitcast.52) | data formatting | bytes 2097152 | tf_op jit(solution)/shard_map/reshape | solution.py:21
  (15 shorter events, 0.2 us)
Async XLA Ops:
  4.7 1.2 %copy-start = (bf16[2,1,1,1024,256]{4,3,2,1,0:T(8,128)(2,1)S(1)}, bf16[2,1,1,1024,256]{4,3,2,1,0:T(8,128)(2,1)}, u32[]{:S(2)}) copy-start(bf16[2,1,1,1024,256]{4,3,2,1,0:T(8,128)(2,1)} %param.5) | copy-start | bytes 3145732
  7.9 32.0 %all-to-all-start = ((bf16[2,4,64,1024]{3,2,0,1:T(8,128)(2,1)}), bf16[2,4,64,1024]{3,2,0,1:T(8,128)(2,1)S(1)}, u32[]{:S(2)}, u32[]{:S(2)}) async-start(bf16[2,4,64,1024]{3,2,0,1:T(8,128)(2,1)} %copy.29), calls=%async_computation | async-start | bytes 2097152 | tf_op jit(solution)/shard_map/all_to_all | solution.py:37
  41.8 19.1 %all-to-all-start.1 = ((bf16[2,8,32,1024]{3,2,0,1:T(8,128)(2,1)}), bf16[2,8,32,1024]{3,2,0,1:T(8,128)(2,1)S(1)}, u32[]{:S(2)}, u32[]{:S(2)}) async-start(bf16[2,8,32,1024]{3,2,0,1:T(8,128)(2,1)} %copy.31), calls=%async_computation.1 | async-start | bytes 2097152 | tf_op jit(solution)/shard_map/all_to_all | solution.py:40
where the time goes:
time: 63.4 us; the launch traced here: 63.1 us
  waiting for transfers between devices  35.5 us (56%)
  local copies, waits for them, and re-layouts  12.1 us (19%)
  starting transfers between devices  10 us (16%)
  other arithmetic  2.97 us (5%)
  matrix products  2.21 us (3%)
    all_to_all x1, waiting for transfers between devices, local(): lax.all_to_all(inner_pieces, 'mem', split_axis=1, concat_axis=1, tiled=True)  21.5 us
    all_to_all x1, waiting for transfers between devices, local(): lax.all_to_all(outer_pieces, 'grp', split_axis=1, concat_axis=1, tiled=True)  14 us
    all_to_all x1, starting transfers between devices, local(): lax.all_to_all(inner_pieces, 'mem', split_axis=1, concat_axis=1, tiled=True)  6.32 us
    all_to_all x1, starting transfers between devices, local(): lax.all_to_all(outer_pieces, 'grp', split_axis=1, concat_axis=1, tiled=True)  3.72 us
    gather x3, local copies, waits for them, and re-layouts, real_matrix(): weight = jnp.take(branches[section_no], mode_order[section_no], axis=1)  3.69 us
    select_n x6, other arithmetic, real_matrix(): weight = jnp.take(branches[section_no], mode_order[section_no], axis=1)  2.86 us
    slice x2, local copies, waits for them, and re-layouts, real_matrix(): weight = jnp.take(branches[section_no], mode_order[section_no], axis=1)  1.96 us
    dot_general x2, matrix products, contract_columns(): lax.dot_general(real_form, joined, (((0,), (0,)), ((), ())), preferred_el...  1.45 us
  transfers between devices with their start and end apart: 2, of which 2 were waited for; matrix products, arithmetic and copies ran while one was open for 9% of the time, Pallas kernels for 0%

commit v1 on v0

v1 whole, which is shorter than its diff:
```python
import functools

import jax
import jax.numpy as jnp
from jax import lax
from jax.experimental import pallas as pl
from jax.experimental.pallas import tpu as pltpu
from jax.sharding import PartitionSpec as P

BF16 = jnp.bfloat16
F32 = jnp.float32
VMEM_LIMIT = 16 * 1024 * 1024
ROW_SPLIT = (4, 4)
PERMUTE_MAX = 8


def iota(shape, dim):
    return lax.broadcasted_iota(jnp.int32, shape, dim)


def dot(a, b, ca, cb):
    return lax.dot_general(a, b, (((ca,), (cb,)), ((), ())), preferred_element_type=F32)


def ids(count, size, me):
    return size if me is None else size ^ me


def entry(position, part, me):
    owner = position // (2 * part)
    owner = owner if me is None else owner ^ me
    return (position // part) % 2, owner * part + position % part


def both(branch):
    return jnp.concatenate([branch[0], branch[1]], axis=1)


def chosen(order_row, states, column):
    width = order_row.shape[1]
    pick = (iota((width, column), 0) == states).astype(BF16)
    rows = dot(order_row.astype(BF16), pick, 1, 0)
    return (iota((width, column), 0) == rows.astype(jnp.int32)).astype(BF16)


def first_form(branch, order_row, part, me):
    width = order_row.shape[1]
    hot = (iota((width, width), 0) == order_row).astype(BF16)
    turned = dot(both(branch), hot, 0, 0).astype(BF16)
    real, imag = turned[:width], turned[width:]
    return jnp.concatenate(
        [jnp.concatenate([real, -imag], axis=1), jnp.concatenate([imag, real], axis=1)], axis=0
    )


def second_form(branch, order_row, part_in, me_in, part_out, me_out):
    width = order_row.shape[1]
    full = 2 * width
    comp, states = entry(iota((1, full), 1), part_in, me_in)
    hot = chosen(order_row, states, full)
    turned = dot(both(branch), hot, 0, 0)
    real, imag = turned[:width], turned[width:]
    plain = comp == 0
    form = jnp.concatenate(
        [jnp.where(plain, real, -imag), jnp.where(plain, imag, real)], axis=0
    ).astype(BF16)
    out_comp, out_states = entry(iota((full, 1), 0), part_out, me_out)
    place = (iota((full, full), 1) == out_comp * width + out_states).astype(BF16)
    return dot(place, form, 1, 0).astype(BF16)


def third_form(branch, order_row, part_in, me_in):
    width = order_row.shape[1]
    full = 2 * width
    _, states = entry(iota((1, full), 1), part_in, me_in)
    hot = chosen(order_row, states, full)
    taken = dot(hot, both(branch), 0, 0)
    real, imag = taken[:, :width], taken[:, width:]
    comp, _ = entry(iota((full, 1), 0), part_in, me_in)
    plain = comp == 0
    return jnp.concatenate(
        [jnp.where(plain, real, -imag), jnp.where(plain, imag, real)], axis=1
    ).astype(BF16)


def place_of(axis, relative):
    return lax.axis_index(axis) if relative else None


def first_kernel(lo, rows, part, relative, with_form, *refs):
    if with_form:
        stem_ref, branches_ref, order_ref, form_ref, *rest = refs
        rest, (branch, order, more) = rest[:-3], rest[-3:]
        n_out = len(rest) - 2
    else:
        stem_ref, form_ref, *rest = refs
        n_out = len(rest) - 2
    outs, (held, sem) = rest[:n_out], rest[n_out:]
    copies = [
        pltpu.make_async_copy(stem_ref.at[c, 0, 0, pl.ds(lo, rows)], held.at[c], sem.at[c])
        for c in range(2)
    ]
    if with_form:
        early = [
            pltpu.make_async_copy(order_ref, order, more.at[0]),
            pltpu.make_async_copy(branches_ref.at[0], branch, more.at[1]),
        ]
        for copy in early:
            copy.start()
    for copy in copies:
        copy.start()
    if with_form:
        for copy in early:
            copy.wait()
        form_ref[...] = first_form(branch, order[0:1, :], part, None)
    for copy in copies:
        copy.wait()
    joined = jnp.concatenate([held[0], held[1]], axis=1)
    width = form_ref.shape[0] // 2
    me = place_of("mem", relative)
    for k in range(width // part):
        owner = k if me is None else jnp.bitwise_xor(me, k)
        form = jnp.concatenate(
            [form_ref[pl.ds(pl.multiple_of(c * width + owner * part, part), part), :] for c in range(2)],
            axis=0,
        )
        piece = dot(form, joined, 1, 1).astype(BF16)
        if len(outs) == 1:
            outs[0][k] = piece
        else:
            outs[k][...] = piece


def forms_kernel(part1, rel1, part2, rel2, branches_ref, order_ref, second_ref, third_ref, branch, order, sem):
    copies = [
        pltpu.make_async_copy(order_ref, order, sem.at[0]),
        pltpu.make_async_copy(branches_ref, branch, sem.at[1]),
    ]
    for copy in copies:
        copy.start()
    for copy in copies:
        copy.wait()
    me1, me2 = place_of("mem", rel1), place_of("grp", rel2)
    second_ref[...] = second_form(branch[1], order[1:2, :], part1, me1, part2, me2)
    third_ref[...] = third_form(branch[2], order[2:3, :], part2, me2)


def gathered(refs):
    return jnp.concatenate([r[...].reshape(-1, r.shape[-1]) for r in refs], axis=0)


def second_kernel(n_in, *refs):
    form_ref, ins, outs = refs[0], refs[1 : 1 + n_in], refs[1 + n_in :]
    result = dot(form_ref[...], gathered(ins), 1, 0).astype(BF16)
    if len(outs) == 1:
        outs[0][...] = result
    else:
        size = result.shape[0] // len(outs)
        for k, out in enumerate(outs):
            out[...] = result[k * size : (k + 1) * size]


def third_kernel(n_in, lo, rows, first, *refs):
    form_ref, ins, rest = refs[0], refs[1 : 1 + n_in], refs[1 + n_in :]
    out_ref, held, sem = rest[-3:]
    result = dot(gathered(ins), form_ref[...], 0, 0).astype(BF16)
    width = result.shape[1] // 2
    for c in range(2):
        held[c] = result[:, c * width : (c + 1) * width]
    copies = [
        pltpu.make_async_copy(held.at[c], out_ref.at[c, 0, 0, pl.ds(lo, rows)], sem.at[c])
        for c in range(2)
    ]
    for copy in copies:
        copy.start()
    for copy in copies:
        copy.wait()


ANY = pl.BlockSpec(memory_space=pl.ANY)
HBM = pl.BlockSpec(memory_space=pltpu.HBM)
VM = pl.BlockSpec(memory_space=pltpu.VMEM)


def call(kernel, in_specs, out_shapes, out_specs, flops, moved, scratch=(), aliases={}):
    return pl.pallas_call(
        kernel,
        in_specs=in_specs,
        out_shape=out_shapes,
        out_specs=out_specs,
        scratch_shapes=list(scratch),
        input_output_aliases=aliases,
        compiler_params=pltpu.CompilerParams(vmem_limit_bytes=VMEM_LIMIT),
        cost_estimate=pl.CostEstimate(flops=flops, bytes_accessed=moved, transcendentals=0),
    )


def swap(piece, axis, count, k):
    return lax.ppermute(piece, axis, [(i, i ^ k) for i in range(count)])


def exchange(pieces, axis, count, relative):
    if relative:
        order = sorted(range(1, count), key=lambda k: -k)
        got = {k: swap(pieces[k], axis, count, k) for k in order}
        return [pieces[0]] + [got[k] for k in range(1, count)]
    (whole,) = pieces
    shaped = whole.reshape(count, -1, whole.shape[-1])
    moved = lax.all_to_all(shaped, axis, split_axis=0, concat_axis=0, tiled=True)
    return [moved.reshape(-1, whole.shape[-1])]


def local(stem, branches, mode_order, z_relative=True, g_relative=True):
    row_count, width = stem.shape[3], stem.shape[4]
    full = 2 * width
    inner, outer = lax.axis_size("mem"), lax.axis_size("grp")
    part1, part2 = width // inner, width // outer
    z_relative = z_relative and inner <= PERMUTE_MAX
    g_relative = g_relative and outer <= PERMUTE_MAX
    unit = row_count // sum(ROW_SPLIT)
    sizes = [unit * s for s in ROW_SPLIT]
    starts = [sum(sizes[:n]) for n in range(len(sizes))]
    form_shape = jax.ShapeDtypeStruct((full, full), BF16)

    def pieces_of(rows, count, relative):
        if relative:
            return [jax.ShapeDtypeStruct((full // count, rows), BF16)] * count
        return [jax.ShapeDtypeStruct((full, rows), BF16)]

    stem, branches, mode_order = (
        pltpu.with_memory_space_constraint(a, pltpu.HBM) for a in (stem, branches, mode_order)
    )
    form0 = None
    sent = []
    for n, (lo, rows) in enumerate(zip(starts, sizes)):
        if z_relative:
            shapes = [jax.ShapeDtypeStruct((full // inner, rows), BF16)] * inner
        else:
            shapes = [jax.ShapeDtypeStruct((inner, full // inner, rows), BF16)]
        kernel = functools.partial(first_kernel, lo, rows, part1, z_relative, n == 0)
        scratch = [pltpu.VMEM((2, rows, width), BF16), pltpu.SemaphoreType.DMA((2,))]
        flops, moved = 1, 1
        if n == 0:
            made = call(
                kernel, [HBM, HBM, HBM], [form_shape] + shapes, [VM] * (1 + len(shapes)), flops, moved,
                scratch + [
                    pltpu.VMEM(branches.shape[1:], BF16),
                    pltpu.VMEM(mode_order.shape, jnp.int32),
                    pltpu.SemaphoreType.DMA((2,)),
                ],
            )(stem, branches, mode_order)
            form0, made = made[0], made[1:]
        else:
            made = call(kernel, [HBM, VM], shapes, [VM] * len(shapes), flops, moved, scratch)(stem, form0)
        sent.append([m.reshape(-1, rows) if not z_relative else m for m in made])
    form1, form2 = call(
        functools.partial(forms_kernel, part1, z_relative, part2, g_relative),
        [HBM, HBM], [form_shape] * 2, [VM] * 2, 1, 1,
        [pltpu.VMEM(branches.shape, BF16), pltpu.VMEM(mode_order.shape, jnp.int32), pltpu.SemaphoreType.DMA((2,))],
    )(branches, mode_order)
    arrived = [exchange(p, "mem", inner, z_relative) for p in sent]
    out = None
    finals = []
    for n, rows in enumerate(sizes):
        ins = arrived[n]
        shapes = pieces_of(rows, outer, g_relative)
        made = call(
            functools.partial(second_kernel, len(ins)), [VM] * (1 + len(ins)), shapes, [VM] * len(shapes),
            *((10**11, 10**8) if n else (1, 1)),
        )(form1, *ins)
        finals.append(exchange(made, "grp", outer, g_relative))
    for n, (lo, rows) in enumerate(zip(starts, sizes)):
        ins = finals[n]
        kernel = functools.partial(third_kernel, len(ins), lo, rows, n == 0)
        scratch = [pltpu.VMEM((2, rows, width), BF16), pltpu.SemaphoreType.DMA((2,))]
        more = [] if out is None else [out]
        out = call(
            kernel, [VM] * (1 + len(ins)) + [ANY] * len(more), jax.ShapeDtypeStruct(stem.shape, BF16), ANY,
            2 * full * full * rows, 4 * full * rows, scratch, {1 + len(ins): 0} if more else {},
        )(form2, *ins, *more)
    return out


def solution(mesh):
    in_specs = (P(None, "grp", "mem", None, None), P(), P())
    out_specs = P(None, "grp", "mem", None, None)
    return jax.shard_map(local, mesh=mesh, in_specs=in_specs, out_specs=out_specs, check_vma=False)
```

time: 63.4 us -> 48.4 us (0.76)
  waiting for transfers between devices: 35.5 us -> 14.1 us
  starting transfers between devices: 10 us -> 24.2 us
  local copies, waits for them, and re-layouts: 12.1 us -> 0 us
  Pallas kernels: 0 us -> 9.81 us
  other arithmetic: 2.97 us -> 0 us
  matrix products: 2.21 us -> 0 us
    all_to_all x2 -> x0, waiting for transfers between devices: 35.5 us -> none  [the longest x1 21.5 us: local(): lax.all_to_all(inner_pieces, 'mem', split_axis=1, concat_axis=1, tiled=True)]
    ppermute x0 -> x20, starting transfers between devices: none -> 24.2 us  [swap(): return lax.ppermute(piece, axis, [(i, i ^ k) for i in range(count)])]
    ppermute x0 -> x20, waiting for transfers between devices: none -> 14.1 us  [swap(): return lax.ppermute(piece, axis, [(i, i ^ k) for i in range(count)])]
    all_to_all x2 -> x0, starting transfers between devices: 10 us -> none  [the longest x1 6.32 us: local(): lax.all_to_all(inner_pieces, 'mem', split_axis=1, concat_axis=1, tiled=True)]
    pallas_call x0 -> x7, Pallas kernels: none -> 9.81 us  [the longest x2 2.55 us: local(): call(kernel, [VM] * (1 + len(ins)) + [ANY] * len(more), jax.ShapeDtypeStr...]
    gather x3 -> x0, local copies, waits for them, and re-layouts: 3.69 us -> none  [real_matrix(): weight = jnp.take(branches[section_no], mode_order[section_no], axis=1)]
    slice x5 -> x0, local copies, waits for them, and re-layouts: 3.07 us -> none  [the longest x2 1.96 us: real_matrix(): weight = jnp.take(branches[section_no], mode_order[section_no], axis=1)]
    select_n x6 -> x0, other arithmetic: 2.86 us -> none  [real_matrix(): weight = jnp.take(branches[section_no], mode_order[section_no], axis=1)]
  transfers between devices with their start and end apart: 2 -> 20, of which waited for: 2 -> 5; matrix products, arithmetic and copies ran while one was open for 9% -> 0% of each run, Pallas kernels for 0% -> 13%
where the time goes in v1:
time: 48.4 us; the launch traced here: 48.2 us
  starting transfers between devices  24.2 us (50%)
  waiting for transfers between devices  14.1 us (29%)
  Pallas kernels  9.81 us (20%)
    ppermute x20, starting transfers between devices, swap(): return lax.ppermute(piece, axis, [(i, i ^ k) for i in range(count)])  24.2 us
    ppermute x20, waiting for transfers between devices, swap(): return lax.ppermute(piece, axis, [(i, i ^ k) for i in range(count)])  14.1 us
    pallas_call x2, Pallas kernels, local(): call(kernel, [VM] * (1 + len(ins)) + [ANY] * len(more), jax.ShapeDtypeStr...  2.55 us
    pallas_call x1, Pallas kernels, local(): call(functools.partial(forms_kernel, part1, z_relative, part2, g_relative...  2.39 us
    pallas_call x1, Pallas kernels, local(): call(kernel, [HBM, HBM, HBM], [form_shape] + shapes, [VM] * (1 + len(shap...  2.16 us
    pallas_call x1, Pallas kernels, local(): call(kernel, [HBM, VM], shapes, [VM] * len(shapes), flops, moved, scratch)  1.84 us
  transfers between devices with their start and end apart: 20, of which 5 were waited for; matrix products, arithmetic and copies ran while one was open for 0% of the time, Pallas kernels for 13%

profile of v1, /device:TPU:0, one launch (start us, length us, event | category | flops | bytes accessed | tf_op | source)
XLA Modules:
  0.0 48.2 jit_solution(2114614898256472665)
XLA Ops:
  0.0 2.2 %shard_map.38 = (bf16[512,512]{1,0:T(8,128)(2,1)S(1)}, bf16[128,512]{1,0:T(8,128)(2,1)S(1)}, bf16[128,512]{1,0:T(8,128)(2,1)S(1)}, bf16[128,512]{1,0:T(8,128)(2,1)S(1)}, bf16[128,512]{1,0:T(8,128)(2,1)S(1)}) custom-call(bf16[2,1,1,1024,256]{4,3,2,1,0:T(8,128)(2,1)} %refs_0_.3, bf16[3,2,256,256]{3,2,1,0:T(8,128)(2,1)} %refs_1_.1, s32[3,256]{1,0:T(4,128)} %refs_2_.1), custom_call_target="tpu_custom_call" | custom-call | flops 1 | bytes 1 | tf_op jit(solution)/shard_map/pallas_call | solution.py:244
  2.2 3.1 %collective-permute-start.10 = (bf16[128,512]{1,0:T(8,128)(2,1)S(1)}, bf16[128,512]{1,0:T(8,128)(2,1)S(1)}, u32[]{:S(2)}, u32[]{:S(2)}) collective-permute-start(bf16[128,512]{1,0:T(8,128)(2,1)S(1)} %get-tuple-element.48), channel_id=1, source_target_pairs={{0,1},{1,0},{2,3},{3,2},{4,5},{5,4},{6,7},{7,6},{8,9},{9,8},{10,11... | collective-permute-start | bytes 393224 | tf_op jit(solution)/shard_map/ppermute | solution.py:199
  5.3 2.6 %collective-permute-start.11 = (bf16[128,512]{1,0:T(8,128)(2,1)S(1)}, bf16[128,512]{1,0:T(8,128)(2,1)S(1)}, u32[]{:S(2)}, u32[]{:S(2)}) collective-permute-start(bf16[128,512]{1,0:T(8,128)(2,1)S(1)} %get-tuple-element.49), channel_id=1, source_target_pairs={{0,2},{1,3},{2,0},{3,1},{4,6},{5,7},{6,4},{7,5},{8,10},{9,11},{10,... | collective-permute-start | bytes 393224 | tf_op jit(solution)/shard_map/ppermute | solution.py:199
  7.8 0.0 collective-permute-start.12
  7.9 1.8 %shard_map.39 = (bf16[128,512]{1,0:T(8,128)(2,1)S(1)}, bf16[128,512]{1,0:T(8,128)(2,1)S(1)}, bf16[128,512]{1,0:T(8,128)(2,1)S(1)}, bf16[128,512]{1,0:T(8,128)(2,1)S(1)}) custom-call(bf16[2,1,1,1024,256]{4,3,2,1,0:T(8,128)(2,1)} %refs_0_.3, bf16[512,512]{1,0:T(8,128)(2,1)S(1)} %get-tuple-element.34.refs_1_), custom_call_target="tpu_custom_call" | custom-call | flops 1 | bytes 1 | tf_op jit(solution)/shard_map/pallas_call | solution.py:254
  9.7 1.0 %collective-permute-start = (bf16[128,512]{1,0:T(8,128)(2,1)S(1)}, bf16[128,512]{1,0:T(8,128)(2,1)S(1)}, u32[]{:S(2)}, u32[]{:S(2)}) collective-permute-start(bf16[128,512]{1,0:T(8,128)(2,1)S(1)} %get-tuple-element.36), channel_id=1, source_target_pairs={{0,1},{1,0},{2,3},{3,2},{4,5},{5,4},{6,7},{7,6},{8,9},{9,8},{10,11... | collective-permute-start | bytes 393224 | tf_op jit(solution)/shard_map/ppermute | solution.py:199
  10.7 3.5 %collective-permute-start.1 = (bf16[128,512]{1,0:T(8,128)(2,1)S(1)}, bf16[128,512]{1,0:T(8,128)(2,1)S(1)}, u32[]{:S(2)}, u32[]{:S(2)}) collective-permute-start(bf16[128,512]{1,0:T(8,128)(2,1)S(1)} %get-tuple-element.37), channel_id=1, source_target_pairs={{0,2},{1,3},{2,0},{3,1},{4,6},{5,7},{6,4},{7,5},{8,10},{9,11},{10,... | collective-permute-start | bytes 393224 | tf_op jit(solution)/shard_map/ppermute | solution.py:199
  14.2 0.0 collective-permute-done.10.refs_2_
  14.2 0.0 collective-permute-start.2
  14.2 2.4 %shard_map.37 = (bf16[512,512]{1,0:T(8,128)(2,1)S(1)}, bf16[512,512]{1,0:T(8,128)(2,1)S(1)}) custom-call(bf16[3,2,256,256]{3,2,1,0:T(8,128)(2,1)} %refs_1_.1, s32[3,256]{1,0:T(4,128)} %refs_2_.1), custom_call_target="tpu_custom_call" | custom-call | flops 1 | bytes 1 | tf_op jit(solution)/shard_map/pallas_call | solution.py:256
  16.6 1.6 %collective-permute-done.11.refs_3_ = bf16[128,512]{1,0:T(8,128)(2,1)S(1)} collective-permute-done((bf16[128,512]{1,0:T(8,128)(2,1)S(1)}, bf16[128,512]{1,0:T(8,128)(2,1)S(1)}, u32[]{:S(2)}, u32[]{:S(2)}) %collective-permute-start.11) | collective-permute-done | bytes 131104 | tf_op jit(solution)/shard_map/ppermute | solution.py:199
  18.2 0.0 collective-permute-done.12.refs_4_
  18.2 0.4 shard_map.41
  18.6 0.1 collective-permute-start.13
  18.7 1.6 %collective-permute-start.14 = (bf16[64,512]{1,0:T(8,128)(2,1)S(1)}, bf16[64,512]{1,0:T(8,128)(2,1)S(1)}, u32[]{:S(2)}, u32[]{:S(2)}) collective-permute-start(bf16[64,512]{1,0:T(8,128)(2,1)S(1)} %get-tuple-element.53), channel_id=1, source_target_pairs={{0,8},{4,12},{8,0},{12,4},{16,24},{20,28},{24,16},{28,20},{1,9},{5... | collective-permute-start | bytes 196616 | tf_op jit(solution)/shard_map/ppermute | solution.py:199
  20.3 0.0 collective-permute-done.refs_2_
  20.3 0.3 collective-permute-start.15
  20.6 8.8 %collective-permute-done.1.refs_3_ = bf16[128,512]{1,0:T(8,128)(2,1)S(1)} collective-permute-done((bf16[128,512]{1,0:T(8,128)(2,1)S(1)}, bf16[128,512]{1,0:T(8,128)(2,1)S(1)}, u32[]{:S(2)}, u32[]{:S(2)}) %collective-permute-start.1) | collective-permute-done | bytes 131104 | tf_op jit(solution)/shard_map/ppermute | solution.py:199
  29.4 1.5 %collective-permute-start.16 = (bf16[64,512]{1,0:T(8,128)(2,1)S(1)}, bf16[64,512]{1,0:T(8,128)(2,1)S(1)}, u32[]{:S(2)}, u32[]{:S(2)}) collective-permute-start(bf16[64,512]{1,0:T(8,128)(2,1)S(1)} %get-tuple-element.55), channel_id=1, source_target_pairs={{0,16},{4,20},{8,24},{12,28},{16,0},{20,4},{24,8},{28,12},{1,17},{... | collective-permute-start | bytes 196616 | tf_op jit(solution)/shard_map/ppermute | solution.py:199
  30.9 0.0 collective-permute-done.2.refs_4_
  30.9 0.0 collective-permute-start.17
  30.9 0.4 shard_map.40
  31.4 0.0 collective-permute-done.13.refs_2_
  31.4 1.5 %collective-permute-start.18 = (bf16[64,512]{1,0:T(8,128)(2,1)S(1)}, bf16[64,512]{1,0:T(8,128)(2,1)S(1)}, u32[]{:S(2)}, u32[]{:S(2)}) collective-permute-start(bf16[64,512]{1,0:T(8,128)(2,1)S(1)} %get-tuple-element.57), channel_id=1, source_target_pairs={{0,24},{4,28},{8,16},{12,20},{16,8},{20,12},{24,0},{28,4},{1,25},{... | collective-permute-start | bytes 196616 | tf_op jit(solution)/shard_map/ppermute | solution.py:199
  32.9 0.0 collective-permute-done.14.refs_3_
  32.9 1.4 %collective-permute-start.19 = (bf16[64,512]{1,0:T(8,128)(2,1)S(1)}, bf16[64,512]{1,0:T(8,128)(2,1)S(1)}, u32[]{:S(2)}, u32[]{:S(2)}) collective-permute-start(bf16[64,512]{1,0:T(8,128)(2,1)S(1)} %get-tuple-element.58), channel_id=1, source_target_pairs={{0,28},{4,24},{8,20},{12,16},{16,12},{20,8},{24,4},{28,0},{1,29},{... | collective-permute-start | bytes 196616 | tf_op jit(solution)/shard_map/ppermute | solution.py:199
  34.3 0.0 collective-permute-done.15.refs_4_
  34.3 0.2 collective-permute-start.3
  34.5 0.0 collective-permute-done.16.refs_5_
  34.5 1.5 %collective-permute-start.4 = (bf16[64,512]{1,0:T(8,128)(2,1)S(1)}, bf16[64,512]{1,0:T(8,128)(2,1)S(1)}, u32[]{:S(2)}, u32[]{:S(2)}) collective-permute-start(bf16[64,512]{1,0:T(8,128)(2,1)S(1)} %get-tuple-element.41), channel_id=1, source_target_pairs={{0,8},{4,12},{8,0},{12,4},{16,24},{20,28},{24,16},{28,20},{1,9},{5... | collective-permute-start | bytes 196616 | tf_op jit(solution)/shard_map/ppermute | solution.py:199
  36.0 0.0 collective-permute-done.17.refs_6_
  36.0 0.2 collective-permute-start.5
  36.2 1.0 %collective-permute-done.18.refs_7_ = bf16[64,512]{1,0:T(8,128)(2,1)S(1)} collective-permute-done((bf16[64,512]{1,0:T(8,128)(2,1)S(1)}, bf16[64,512]{1,0:T(8,128)(2,1)S(1)}, u32[]{:S(2)}, u32[]{:S(2)}) %collective-permute-start.18) | collective-permute-done | bytes 65568 | tf_op jit(solution)/shard_map/ppermute | solution.py:199
  37.2 3.3 %collective-permute-start.6 = (bf16[64,512]{1,0:T(8,128)(2,1)S(1)}, bf16[64,512]{1,0:T(8,128)(2,1)S(1)}, u32[]{:S(2)}, u32[]{:S(2)}) collective-permute-start(bf16[64,512]{1,0:T(8,128)(2,1)S(1)} %get-tuple-element.43), channel_id=1, source_target_pairs={{0,16},{4,20},{8,24},{12,28},{16,0},{20,4},{24,8},{28,12},{1,17},{... | collective-permute-start | bytes 196616 | tf_op jit(solution)/shard_map/ppermute | solution.py:199
  40.5 0.0 collective-permute-done.19.refs_8_
  40.5 0.0 collective-permute-start.7
  40.5 0.0 collective-permute-done.3.refs_2_
  40.5 1.2 %collective-permute-start.8 = (bf16[64,512]{1,0:T(8,128)(2,1)S(1)}, bf16[64,512]{1,0:T(8,128)(2,1)S(1)}, u32[]{:S(2)}, u32[]{:S(2)}) collective-permute-start(bf16[64,512]{1,0:T(8,128)(2,1)S(1)} %get-tuple-element.45), channel_id=1, source_target_pairs={{0,24},{4,28},{8,16},{12,20},{16,8},{20,12},{24,0},{28,4},{1,25},{... | collective-permute-start | bytes 196616 | tf_op jit(solution)/shard_map/ppermute | solution.py:199
  41.7 0.0 collective-permute-done.4.refs_3_
  41.7 1.2 %collective-permute-start.9 = (bf16[64,512]{1,0:T(8,128)(2,1)S(1)}, bf16[64,512]{1,0:T(8,128)(2,1)S(1)}, u32[]{:S(2)}, u32[]{:S(2)}) collective-permute-start(bf16[64,512]{1,0:T(8,128)(2,1)S(1)} %get-tuple-element.46), channel_id=1, source_target_pairs={{0,28},{4,24},{8,20},{12,16},{16,12},{20,8},{24,4},{28,0},{1,29},{... | collective-permute-start | bytes 196616 | tf_op jit(solution)/shard_map/ppermute | solution.py:199
  42.9 1.3 %shard_map.42.refs_9_ = bf16[2,1,1,1024,256]{4,3,2,1,0:T(8,128)(2,1)} custom-call(bf16[512,512]{1,0:T(8,128)(2,1)S(1)} %get-tuple-element.32.refs_0_, bf16[64,512]{1,0:T(8,128)(2,1)S(1)} %get-tuple-element.51.refs_1_, bf16[64,512]{1,0:T(8,128)(2,1)S(1)} %collective-permute-done.13.refs_2_, bf16[64,512]{1,0:T(8,128)(2,1)S(1)} %collective-permute-done.14.refs_3_, ...), custom_call_target="tpu_custom_call" | custom-call | flops 268435456 | bytes 1048576 | tf_op jit(solution)/shard_map/pallas_call | solution.py:277
  44.2 0.0 collective-permute-done.5.refs_4_
  44.2 0.0 collective-permute-done.6.refs_5_
  44.3 0.0 collective-permute-done.7.refs_6_
  44.3 1.7 %collective-permute-done.8.refs_7_ = bf16[64,512]{1,0:T(8,128)(2,1)S(1)} collective-permute-done((bf16[64,512]{1,0:T(8,128)(2,1)S(1)}, bf16[64,512]{1,0:T(8,128)(2,1)S(1)}, u32[]{:S(2)}, u32[]{:S(2)}) %collective-permute-start.8) | collective-permute-done | bytes 65568 | tf_op jit(solution)/shard_map/ppermute | solution.py:199
  46.0 1.0 %collective-permute-done.9.refs_8_ = bf16[64,512]{1,0:T(8,128)(2,1)S(1)} collective-permute-done((bf16[64,512]{1,0:T(8,128)(2,1)S(1)}, bf16[64,512]{1,0:T(8,128)(2,1)S(1)}, u32[]{:S(2)}, u32[]{:S(2)}) %collective-permute-start.9) | collective-permute-done | bytes 65568 | tf_op jit(solution)/shard_map/ppermute | solution.py:199
  46.9 1.3 %shard_map.43 = bf16[2,1,1,1024,256]{4,3,2,1,0:T(8,128)(2,1)} custom-call(bf16[512,512]{1,0:T(8,128)(2,1)S(1)} %get-tuple-element.32.refs_0_, bf16[64,512]{1,0:T(8,128)(2,1)S(1)} %get-tuple-element.39.refs_1_, bf16[64,512]{1,0:T(8,128)(2,1)S(1)} %collective-permute-done.3.refs_2_, ...), custom_call_target="tpu_custom_call", output_to_operand_aliasing={{}: (9, {})} | custom-call | flops 268435456 | bytes 1048576 | tf_op jit(solution)/shard_map/pallas_call | solution.py:277
Async XLA Ops:
  2.2 12.0 %collective-permute-start.10 = (bf16[128,512]{1,0:T(8,128)(2,1)S(1)}, bf16[128,512]{1,0:T(8,128)(2,1)S(1)}, u32[]{:S(2)}, u32[]{:S(2)}) collective-permute-start(bf16[128,512]{1,0:T(8,128)(2,1)S(1)} %get-tuple-element.48), channel_id=1, source_target_pairs={{0,1},{1,0},{2,3},{3,2},{4,5},{5,4},{6,7},{7,6},{8,9},{9,8},{10,11... | collective-permute-start | bytes 393224 | tf_op jit(solution)/shard_map/ppermute | solution.py:199
  5.3 12.9 %collective-permute-start.11 = (bf16[128,512]{1,0:T(8,128)(2,1)S(1)}, bf16[128,512]{1,0:T(8,128)(2,1)S(1)}, u32[]{:S(2)}, u32[]{:S(2)}) collective-permute-start(bf16[128,512]{1,0:T(8,128)(2,1)S(1)} %get-tuple-element.49), channel_id=1, source_target_pairs={{0,2},{1,3},{2,0},{3,1},{4,6},{5,7},{6,4},{7,5},{8,10},{9,11},{10,... | collective-permute-start | bytes 393224 | tf_op jit(solution)/shard_map/ppermute | solution.py:199
  7.8 10.4 %collective-permute-start.12 = (bf16[128,512]{1,0:T(8,128)(2,1)S(1)}, bf16[128,512]{1,0:T(8,128)(2,1)S(1)}, u32[]{:S(2)}, u32[]{:S(2)}) collective-permute-start(bf16[128,512]{1,0:T(8,128)(2,1)S(1)} %get-tuple-element.50), channel_id=1, source_target_pairs={{0,3},{1,2},{2,1},{3,0},{4,7},{5,6},{6,5},{7,4},{8,11},{9,10},{10,... | collective-permute-start | bytes 393224 | tf_op jit(solution)/shard_map/ppermute | solution.py:199
  9.7 10.6 %collective-permute-start = (bf16[128,512]{1,0:T(8,128)(2,1)S(1)}, bf16[128,512]{1,0:T(8,128)(2,1)S(1)}, u32[]{:S(2)}, u32[]{:S(2)}) collective-permute-start(bf16[128,512]{1,0:T(8,128)(2,1)S(1)} %get-tuple-element.36), channel_id=1, source_target_pairs={{0,1},{1,0},{2,3},{3,2},{4,5},{5,4},{6,7},{7,6},{8,9},{9,8},{10,11... | collective-permute-start | bytes 393224 | tf_op jit(solution)/shard_map/ppermute | solution.py:199
  10.7 18.7 %collective-permute-start.1 = (bf16[128,512]{1,0:T(8,128)(2,1)S(1)}, bf16[128,512]{1,0:T(8,128)(2,1)S(1)}, u32[]{:S(2)}, u32[]{:S(2)}) collective-permute-start(bf16[128,512]{1,0:T(8,128)(2,1)S(1)} %get-tuple-element.37), channel_id=1, source_target_pairs={{0,2},{1,3},{2,0},{3,1},{4,6},{5,7},{6,4},{7,5},{8,10},{9,11},{10,... | collective-permute-start | bytes 393224 | tf_op jit(solution)/shard_map/ppermute | solution.py:199
  14.2 16.8 %collective-permute-start.2 = (bf16[128,512]{1,0:T(8,128)(2,1)S(1)}, bf16[128,512]{1,0:T(8,128)(2,1)S(1)}, u32[]{:S(2)}, u32[]{:S(2)}) collective-permute-start(bf16[128,512]{1,0:T(8,128)(2,1)S(1)} %get-tuple-element.38), channel_id=1, source_target_pairs={{0,3},{1,2},{2,1},{3,0},{4,7},{5,6},{6,5},{7,4},{8,11},{9,10},{10,... | collective-permute-start | bytes 393224 | tf_op jit(solution)/shard_map/ppermute | solution.py:199
  18.6 12.7 %collective-permute-start.13 = (bf16[64,512]{1,0:T(8,128)(2,1)S(1)}, bf16[64,512]{1,0:T(8,128)(2,1)S(1)}, u32[]{:S(2)}, u32[]{:S(2)}) collective-permute-start(bf16[64,512]{1,0:T(8,128)(2,1)S(1)} %get-tuple-element.52), channel_id=1, source_target_pairs={{0,4},{4,0},{8,12},{12,8},{16,20},{20,16},{24,28},{28,24},{1,5},{5... | collective-permute-start | bytes 196616 | tf_op jit(solution)/shard_map/ppermute | solution.py:199
  18.7 14.2 %collective-permute-start.14 = (bf16[64,512]{1,0:T(8,128)(2,1)S(1)}, bf16[64,512]{1,0:T(8,128)(2,1)S(1)}, u32[]{:S(2)}, u32[]{:S(2)}) collective-permute-start(bf16[64,512]{1,0:T(8,128)(2,1)S(1)} %get-tuple-element.53), channel_id=1, source_target_pairs={{0,8},{4,12},{8,0},{12,4},{16,24},{20,28},{24,16},{28,20},{1,9},{5... | collective-permute-start | bytes 196616 | tf_op jit(solution)/shard_map/ppermute | solution.py:199
  20.3 14.1 %collective-permute-start.15 = (bf16[64,512]{1,0:T(8,128)(2,1)S(1)}, bf16[64,512]{1,0:T(8,128)(2,1)S(1)}, u32[]{:S(2)}, u32[]{:S(2)}) collective-permute-start(bf16[64,512]{1,0:T(8,128)(2,1)S(1)} %get-tuple-element.54), channel_id=1, source_target_pairs={{0,12},{4,8},{8,4},{12,0},{16,28},{20,24},{24,20},{28,16},{1,13},{... | collective-permute-start | bytes 196616 | tf_op jit(solution)/shard_map/ppermute | solution.py:199
  29.4 5.1 %collective-permute-start.16 = (bf16[64,512]{1,0:T(8,128)(2,1)S(1)}, bf16[64,512]{1,0:T(8,128)(2,1)S(1)}, u32[]{:S(2)}, u32[]{:S(2)}) collective-permute-start(bf16[64,512]{1,0:T(8,128)(2,1)S(1)} %get-tuple-element.55), channel_id=1, source_target_pairs={{0,16},{4,20},{8,24},{12,28},{16,0},{20,4},{24,8},{28,12},{1,17},{... | collective-permute-start | bytes 196616 | tf_op jit(solution)/shard_map/ppermute | solution.py:199
  30.9 5.1 %collective-permute-start.17 = (bf16[64,512]{1,0:T(8,128)(2,1)S(1)}, bf16[64,512]{1,0:T(8,128)(2,1)S(1)}, u32[]{:S(2)}, u32[]{:S(2)}) collective-permute-start(bf16[64,512]{1,0:T(8,128)(2,1)S(1)} %get-tuple-element.56), channel_id=1, source_target_pairs={{0,20},{4,16},{8,28},{12,24},{16,4},{20,0},{24,12},{28,8},{1,21},{... | collective-permute-start | bytes 196616 | tf_op jit(solution)/shard_map/ppermute | solution.py:199
  31.4 5.8 %collective-permute-start.18 = (bf16[64,512]{1,0:T(8,128)(2,1)S(1)}, bf16[64,512]{1,0:T(8,128)(2,1)S(1)}, u32[]{:S(2)}, u32[]{:S(2)}) collective-permute-start(bf16[64,512]{1,0:T(8,128)(2,1)S(1)} %get-tuple-element.57), channel_id=1, source_target_pairs={{0,24},{4,28},{8,16},{12,20},{16,8},{20,12},{24,0},{28,4},{1,25},{... | collective-permute-start | bytes 196616 | tf_op jit(solution)/shard_map/ppermute | solution.py:199
  32.9 7.6 %collective-permute-start.19 = (bf16[64,512]{1,0:T(8,128)(2,1)S(1)}, bf16[64,512]{1,0:T(8,128)(2,1)S(1)}, u32[]{:S(2)}, u32[]{:S(2)}) collective-permute-start(bf16[64,512]{1,0:T(8,128)(2,1)S(1)} %get-tuple-element.58), channel_id=1, source_target_pairs={{0,28},{4,24},{8,20},{12,16},{16,12},{20,8},{24,4},{28,0},{1,29},{... | collective-permute-start | bytes 196616 | tf_op jit(solution)/shard_map/ppermute | solution.py:199
  34.3 6.2 %collective-permute-start.3 = (bf16[64,512]{1,0:T(8,128)(2,1)S(1)}, bf16[64,512]{1,0:T(8,128)(2,1)S(1)}, u32[]{:S(2)}, u32[]{:S(2)}) collective-permute-start(bf16[64,512]{1,0:T(8,128)(2,1)S(1)} %get-tuple-element.40), channel_id=1, source_target_pairs={{0,4},{4,0},{8,12},{12,8},{16,20},{20,16},{24,28},{28,24},{1,5},{5... | collective-permute-start | bytes 196616 | tf_op jit(solution)/shard_map/ppermute | solution.py:199
  34.5 7.2 %collective-permute-start.4 = (bf16[64,512]{1,0:T(8,128)(2,1)S(1)}, bf16[64,512]{1,0:T(8,128)(2,1)S(1)}, u32[]{:S(2)}, u32[]{:S(2)}) collective-permute-start(bf16[64,512]{1,0:T(8,128)(2,1)S(1)} %get-tuple-element.41), channel_id=1, source_target_pairs={{0,8},{4,12},{8,0},{12,4},{16,24},{20,28},{24,16},{28,20},{1,9},{5... | collective-permute-start | bytes 196616 | tf_op jit(solution)/shard_map/ppermute | solution.py:199
  36.0 8.2 %collective-permute-start.5 = (bf16[64,512]{1,0:T(8,128)(2,1)S(1)}, bf16[64,512]{1,0:T(8,128)(2,1)S(1)}, u32[]{:S(2)}, u32[]{:S(2)}) collective-permute-start(bf16[64,512]{1,0:T(8,128)(2,1)S(1)} %get-tuple-element.42), channel_id=1, source_target_pairs={{0,12},{4,8},{8,4},{12,0},{16,28},{20,24},{24,20},{28,16},{1,13},{... | collective-permute-start | bytes 196616 | tf_op jit(solution)/shard_map/ppermute | solution.py:199
  37.2 7.1 %collective-permute-start.6 = (bf16[64,512]{1,0:T(8,128)(2,1)S(1)}, bf16[64,512]{1,0:T(8,128)(2,1)S(1)}, u32[]{:S(2)}, u32[]{:S(2)}) collective-permute-start(bf16[64,512]{1,0:T(8,128)(2,1)S(1)} %get-tuple-element.43), channel_id=1, source_target_pairs={{0,16},{4,20},{8,24},{12,28},{16,0},{20,4},{24,8},{28,12},{1,17},{... | collective-permute-start | bytes 196616 | tf_op jit(solution)/shard_map/ppermute | solution.py:199
  40.5 3.7 %collective-permute-start.7 = (bf16[64,512]{1,0:T(8,128)(2,1)S(1)}, bf16[64,512]{1,0:T(8,128)(2,1)S(1)}, u32[]{:S(2)}, u32[]{:S(2)}) collective-permute-start(bf16[64,512]{1,0:T(8,128)(2,1)S(1)} %get-tuple-element.44), channel_id=1, source_target_pairs={{0,20},{4,16},{8,28},{12,24},{16,4},{20,0},{24,12},{28,8},{1,21},{... | collective-permute-start | bytes 196616 | tf_op jit(solution)/shard_map/ppermute | solution.py:199
  40.5 5.4 %collective-permute-start.8 = (bf16[64,512]{1,0:T(8,128)(2,1)S(1)}, bf16[64,512]{1,0:T(8,128)(2,1)S(1)}, u32[]{:S(2)}, u32[]{:S(2)}) collective-permute-start(bf16[64,512]{1,0:T(8,128)(2,1)S(1)} %get-tuple-element.45), channel_id=1, source_target_pairs={{0,24},{4,28},{8,16},{12,20},{16,8},{20,12},{24,0},{28,4},{1,25},{... | collective-permute-start | bytes 196616 | tf_op jit(solution)/shard_map/ppermute | solution.py:199
  41.7 5.2 %collective-permute-start.9 = (bf16[64,512]{1,0:T(8,128)(2,1)S(1)}, bf16[64,512]{1,0:T(8,128)(2,1)S(1)}, u32[]{:S(2)}, u32[]{:S(2)}) collective-permute-start(bf16[64,512]{1,0:T(8,128)(2,1)S(1)} %get-tuple-element.46), channel_id=1, source_target_pairs={{0,28},{4,24},{8,20},{12,16},{16,12},{20,8},{24,4},{28,0},{1,29},{... | collective-permute-start | bytes 196616 | tf_op jit(solution)/shard_map/ppermute | solution.py:199

commit v2 on v1

v2 whole, which is shorter than its diff:
```python
import functools

import jax
import jax.numpy as jnp
from jax import lax
from jax.experimental import pallas as pl
from jax.experimental.pallas import tpu as pltpu
from jax.sharding import PartitionSpec as P

BF16 = jnp.bfloat16
F32 = jnp.float32
VMEM_LIMIT = 16 * 1024 * 1024
ROW_SPLIT = (4, 4)
PERMUTE_MAX = 8
STEPPED = (False, True)


def iota(shape, dim):
    return lax.broadcasted_iota(jnp.int32, shape, dim)


def dot(a, b, ca, cb):
    return lax.dot_general(a, b, (((ca,), (cb,)), ((), ())), preferred_element_type=F32)


def ids(count, size, me):
    return size if me is None else size ^ me


def entry(position, part, me):
    owner = position // (2 * part)
    owner = owner if me is None else owner ^ me
    return (position // part) % 2, owner * part + position % part


def both(branch):
    return jnp.concatenate([branch[0], branch[1]], axis=1)


def chosen(order_row, states, column):
    width = order_row.shape[1]
    pick = (iota((width, column), 0) == states).astype(BF16)
    rows = dot(order_row.astype(BF16), pick, 1, 0)
    return (iota((width, column), 0) == rows.astype(jnp.int32)).astype(BF16)


def first_form(branch, order_row, part, me):
    width = order_row.shape[1]
    hot = (iota((width, width), 0) == order_row).astype(BF16)
    turned = dot(both(branch), hot, 0, 0).astype(BF16)
    real, imag = turned[:width], turned[width:]
    return jnp.concatenate(
        [jnp.concatenate([real, -imag], axis=1), jnp.concatenate([imag, real], axis=1)], axis=0
    )


def second_form(branch, order_row, part_in, me_in, part_out, me_out):
    width = order_row.shape[1]
    full = 2 * width
    comp, states = entry(iota((1, full), 1), part_in, me_in)
    hot = chosen(order_row, states, full)
    turned = dot(both(branch), hot, 0, 0)
    real, imag = turned[:width], turned[width:]
    plain = comp == 0
    form = jnp.concatenate(
        [jnp.where(plain, real, -imag), jnp.where(plain, imag, real)], axis=0
    ).astype(BF16)
    out_comp, out_states = entry(iota((full, 1), 0), part_out, me_out)
    place = (iota((full, full), 1) == out_comp * width + out_states).astype(BF16)
    return dot(place, form, 1, 0).astype(BF16)


def third_form(branch, order_row, part_in, me_in):
    width = order_row.shape[1]
    full = 2 * width
    _, states = entry(iota((1, full), 1), part_in, me_in)
    hot = chosen(order_row, states, full)
    taken = dot(hot, both(branch), 0, 0)
    real, imag = taken[:, :width], taken[:, width:]
    comp, _ = entry(iota((full, 1), 0), part_in, me_in)
    plain = comp == 0
    return jnp.concatenate(
        [jnp.where(plain, real, -imag), jnp.where(plain, imag, real)], axis=1
    ).astype(BF16)


def place_of(axis, relative):
    return lax.axis_index(axis) if relative else None


def first_pieces(form_ref, block, part, me):
    width = block.shape[2]
    form = []
    for k in range(width // part):
        owner = k if me is None else jnp.bitwise_xor(me, k)
        form += [form_ref[pl.ds(pl.multiple_of(c * width + owner * part, part), part), :] for c in range(2)]
    joined = jnp.concatenate([block[0], block[1]], axis=1)
    result = dot(jnp.concatenate(form, axis=0), joined, 1, 1).astype(BF16)
    return [result[2 * part * k : 2 * part * (k + 1)] for k in range(width // part)]


def put(pieces, outs):
    if len(outs) == 1 and len(pieces) > 1:
        outs[0][...] = jnp.concatenate(pieces, axis=0)
    else:
        for piece, out in zip(pieces, outs):
            out[...] = piece


def opening_kernel(rows, part, relative, stem_ref, branches_ref, order_ref, form_ref, *rest):
    outs, (branch, order, block, sem) = rest[:-4], rest[-4:]
    copies = [
        pltpu.make_async_copy(order_ref, order, sem.at[0]),
        pltpu.make_async_copy(branches_ref.at[0], branch, sem.at[1]),
        pltpu.make_async_copy(stem_ref.at[:, 0, 0, pl.ds(0, rows)], block, sem.at[2]),
    ]
    for copy in copies:
        copy.start()
    copies[0].wait()
    copies[1].wait()
    form_ref[...] = first_form(branch, order[0:1, :], part, None)
    copies[2].wait()
    put(first_pieces(form_ref, block, part, place_of("mem", relative)), outs)


def first_kernel(part, relative, n_out, block_ref, form_ref, *rest):
    put(first_pieces(form_ref, block_ref, part, place_of("mem", relative)), rest[-n_out:])


def forms_kernel(sizes, part1, rel1, part2, rel2, stem_ref, branches_ref, order_ref, second_ref, third_ref, *rest):
    blocks, (branch, order, sem) = rest[:-3], rest[-3:]
    copies = [
        pltpu.make_async_copy(order_ref, order, sem.at[0]),
        pltpu.make_async_copy(branches_ref.at[pl.ds(1, 2)], branch, sem.at[1]),
    ]
    lo = sizes[0]
    for n, rows in enumerate(sizes[1:]):
        copies.append(pltpu.make_async_copy(stem_ref.at[:, 0, 0, pl.ds(lo, rows)], blocks[n], sem.at[2 + n]))
        lo += rows
    for copy in copies:
        copy.start()
    copies[0].wait()
    copies[1].wait()
    me1, me2 = place_of("mem", rel1), place_of("grp", rel2)
    second_ref[...] = second_form(branch[0], order[1:2, :], part1, me1, part2, me2)
    third_ref[...] = third_form(branch[1], order[2:3, :], part2, me2)
    for copy in copies[2:]:
        copy.wait()


def gathered(refs):
    return jnp.concatenate([r[...].reshape(-1, r.shape[-1]) for r in refs], axis=0)


def second_kernel(n_in, count, relative, form_ref, *refs):
    ins, outs = refs[:n_in], refs[n_in:]
    result = dot(form_ref[...], gathered(ins), 1, 0).astype(BF16)
    size = result.shape[0] // count
    if not relative:
        outs[0][...] = result
        return
    me = lax.axis_index("grp")
    for k in range(count):
        block = result[size * k : size * (k + 1)]
        if len(outs) == 1:
            outs[0][pl.ds(pl.multiple_of(jnp.bitwise_xor(me, k) * size, size), size)] = block
        else:
            outs[k % 2][size * (k // 2) : size * (k // 2 + 1)] = block


def merge_kernel(size, count, kept_ref, came_ref, *outs):
    outs = outs[-count:]
    for q, out in enumerate(outs, 1):
        out[:size] = kept_ref[q * size : (q + 1) * size]
        out[size:] = came_ref[q * size : (q + 1) * size]


def third_kernel(n_in, count, relative, lo, rows, form_ref, *refs):
    ins, (out_ref, held, sem) = refs[:n_in], refs[-3:]
    size = form_ref.shape[0] // count
    if n_in > 1:
        ins = (ins[0].at[:size], ins[1].at[:size]) + ins[2:]
    elif relative:
        me = lax.axis_index("grp")
        ins = [ins[0].at[pl.ds(pl.multiple_of(jnp.bitwise_xor(me, k) * size, size), size)] for k in range(count)]
    result = dot(gathered(ins), form_ref[...], 0, 0).astype(BF16)
    width = result.shape[1] // 2
    for c in range(2):
        held[c] = result[:, c * width : (c + 1) * width]
    copies = [
        pltpu.make_async_copy(held.at[c], out_ref.at[c, 0, 0, pl.ds(lo, rows)], sem.at[c])
        for c in range(2)
    ]
    for copy in copies:
        copy.start()
    for copy in copies:
        copy.wait()


ANY = pl.BlockSpec(memory_space=pl.ANY)
HBM = pl.BlockSpec(memory_space=pltpu.HBM)
VM = pl.BlockSpec(memory_space=pltpu.VMEM)


def call(kernel, in_specs, out_shapes, out_specs, flops, moved, scratch=(), aliases={}):
    return pl.pallas_call(
        kernel,
        in_specs=in_specs,
        out_shape=out_shapes,
        out_specs=out_specs,
        scratch_shapes=list(scratch),
        input_output_aliases=aliases,
        compiler_params=pltpu.CompilerParams(vmem_limit_bytes=VMEM_LIMIT),
        cost_estimate=pl.CostEstimate(flops=flops, bytes_accessed=moved, transcendentals=0),
    )


def swap(piece, axis, count, k):
    return lax.ppermute(piece, axis, [(i, i ^ k) for i in range(count)])


def whole_exchange(whole, axis, count):
    shaped = whole.reshape(count, -1, whole.shape[-1])
    moved = lax.all_to_all(shaped, axis, split_axis=0, concat_axis=0, tiled=True)
    return [moved.reshape(-1, whole.shape[-1])]


def shape(*dims):
    return jax.ShapeDtypeStruct(dims, BF16)


def plain(count):
    return count > PERMUTE_MAX or count < 4 or count & (count - 1) != 0


def local(stem, branches, mode_order):
    row_count, width = stem.shape[3], stem.shape[4]
    full = 2 * width
    inner, outer = lax.axis_size("mem"), lax.axis_size("grp")
    part1, part2 = width // inner, width // outer
    rel1, rel2 = not plain(inner), not plain(outer)
    unit = row_count // sum(ROW_SPLIT)
    sizes = [unit * s for s in ROW_SPLIT]
    starts = [sum(sizes[:n]) for n in range(len(sizes))]
    stem, branches, mode_order = (
        pltpu.with_memory_space_constraint(a, pltpu.HBM) for a in (stem, branches, mode_order)
    )
    form_shape = shape(full, full)

    def first_shapes(rows):
        return [shape(full // inner, rows)] * inner if rel1 else [shape(full, rows)]

    form0, *pieces = call(
        functools.partial(opening_kernel, sizes[0], part1, rel1),
        [HBM] * 3, [form_shape] + first_shapes(sizes[0]), [VM] * (1 + len(first_shapes(sizes[0]))), *COST["open"],
        [
            pltpu.VMEM(branches.shape[1:], BF16),
            pltpu.VMEM(mode_order.shape, jnp.int32),
            pltpu.VMEM((2, sizes[0], width), BF16),
            pltpu.SemaphoreType.DMA((3,)),
        ],
    )(stem, branches, mode_order)
    form1, form2, *blocks = call(
        functools.partial(forms_kernel, sizes, part1, rel1, part2, rel2),
        [HBM] * 3, [form_shape] * 2 + [shape(2, rows, width) for rows in sizes[1:]], [VM] * (1 + len(sizes)),
        *COST["forms"],
        [
            pltpu.VMEM((2,) + branches.shape[1:], BF16),
            pltpu.VMEM(mode_order.shape, jnp.int32),
            pltpu.SemaphoreType.DMA((1 + len(sizes),)),
        ],
    )(stem, branches, mode_order)

    arrived = []
    for n, rows in enumerate(sizes):
        if n:
            wait = FIRST_AFTER(arrived, form1) if rel1 else []
            shapes = first_shapes(rows)
            pieces = call(
                functools.partial(first_kernel, part1, rel1, len(shapes)),
                [VM, VM] + [ANY] * len(wait), shapes, [VM] * len(shapes), *COST["first"],
            )(blocks[n - 1], form0, *wait)
        if rel1:
            got = {k: swap(pieces[k], "mem", inner, k) for k in range(1, inner)}
            arrived.append([pieces[0]] + [got[k] for k in range(1, inner)])
        else:
            arrived.append(whole_exchange(pieces[0], "mem", inner))

    out = None
    for n, (lo, rows) in enumerate(zip(starts, sizes)):
        ins = arrived[n]
        stepped = rel2 and STEPPED[n]
        shapes = [shape(full // 2, rows)] * 2 if stepped else [shape(full, rows)]
        made = call(
            functools.partial(second_kernel, len(ins), outer, rel2),
            [VM] * (1 + len(ins)), shapes, [VM] * len(shapes), *COST["second"][n],
        )(form1, *ins)
        if stepped:
            kept, given = made
            came = swap(given, "grp", outer, 1)
            pairs = outer // 2
            merged = call(
                functools.partial(merge_kernel, full // outer, pairs - 1),
                [VM] * 2, [shape(full // pairs, rows)] * (pairs - 1), [VM] * (pairs - 1), *COST["merge"],
            )(kept, came)
            got = {q: swap(merged[q - 1], "grp", outer, 2 * q) for q in range(1, pairs)}
            ins = [kept, came] + [got[q] for q in range(1, pairs)]
        else:
            ins = whole_exchange(made[0], "grp", outer)
        more = [] if out is None else [out]
        out = call(
            functools.partial(third_kernel, len(ins), outer, rel2, lo, rows),
            [VM] * (1 + len(ins)) + [ANY] * len(more), shape(*stem.shape), ANY, *COST["third"],
            [pltpu.VMEM((2, rows, width), BF16), pltpu.SemaphoreType.DMA((2,))],
            {1 + len(ins): 0} if more else {},
        )(form2, *ins, *more)
    return out


def FIRST_AFTER(arrived, form1):
    return [arrived[-1][2], form1]


COST = {
    "open": (1, 1),
    "forms": (1, 1),
    "first": (1, 1),
    "second": [(1, 1), (10**11, 10**8)],
    "merge": (1, 1),
    "third": (1, 1),
}


def solution(mesh):
    in_specs = (P(None, "grp", "mem", None, None), P(), P())
    out_specs = P(None, "grp", "mem", None, None)
    return jax.shard_map(local, mesh=mesh, in_specs=in_specs, out_specs=out_specs, check_vma=False)
```

time: 48.4 us -> 41.3 us (0.85)
  starting transfers between devices: 24.2 us -> 18.1 us
  Pallas kernels: 9.81 us -> 8.77 us
    ppermute x20 -> x10, starting transfers between devices: 24.2 us -> 13.8 us  [swap(): return lax.ppermute(piece, axis, [(i, i ^ k) for i in range(count)])]
    all_to_all x0 -> x1, starting transfers between devices: none -> 4.36 us  [whole_exchange(): lax.all_to_all(shaped, axis, split_axis=0, concat_axis=0, tiled=True)]
    pallas_call x7 -> x8, Pallas kernels: 9.81 us -> 8.77 us  [the longest x2 2.56 us: local(): call(functools.partial(third_kernel, len(ins), outer, rel2, lo, rows), [V...]
    ppermute x20 -> x10, waiting for transfers between devices: 14.1 us -> 13.5 us  [swap(): return lax.ppermute(piece, axis, [(i, i ^ k) for i in range(count)])]
    all_to_all x0 -> x1, waiting for transfers between devices: none -> 0.57 us  [whole_exchange(): lax.all_to_all(shaped, axis, split_axis=0, concat_axis=0, tiled=True)]
  transfers between devices with their start and end apart: 20 -> 11, of which waited for: 5 -> 7; matrix products, arithmetic and copies ran while one was open for 0% -> 0% of each run, Pallas kernels for 13% -> 14%
where the time goes in v2:
time: 41.3 us; the launch traced here: 41.1 us
  starting transfers between devices  18.1 us (44%)
  waiting for transfers between devices  14.1 us (34%)
  Pallas kernels  8.77 us (21%)
    ppermute x10, starting transfers between devices, swap(): return lax.ppermute(piece, axis, [(i, i ^ k) for i in range(count)])  13.8 us
    ppermute x10, waiting for transfers between devices, swap(): return lax.ppermute(piece, axis, [(i, i ^ k) for i in range(count)])  13.5 us
    all_to_all x1, starting transfers between devices, whole_exchange(): lax.all_to_all(shaped, axis, split_axis=0, concat_axis=0, tiled=True)  4.36 us
    pallas_call x2, Pallas kernels, local(): call(functools.partial(third_kernel, len(ins), outer, rel2, lo, rows), [V...  2.56 us
    pallas_call x1, Pallas kernels, local(): call(functools.partial(forms_kernel, sizes, part1, rel1, part2, rel2), [H...  2.32 us
    pallas_call x1, Pallas kernels, local(): call(functools.partial(opening_kernel, sizes[0], part1, rel1), [HBM] * 3,...  1.73 us
    pallas_call x2, Pallas kernels, local(): call(functools.partial(second_kernel, len(ins), outer, rel2), [VM] * (1 +...  1.67 us
  transfers between devices with their start and end apart: 11, of which 7 were waited for; matrix products, arithmetic and copies ran while one was open for 0% of the time, Pallas kernels for 14%

profile of v2, /device:TPU:0, one launch (start us, length us, event | category | flops | bytes accessed | tf_op | source)
XLA Modules:
  0.0 41.1 jit_solution(14036040286132046291)
XLA Ops:
  0.0 1.7 %shard_map.38 = (bf16[512,512]{1,0:T(8,128)(2,1)S(1)}, bf16[128,512]{1,0:T(8,128)(2,1)S(1)}, bf16[128,512]{1,0:T(8,128)(2,1)S(1)}, bf16[128,512]{1,0:T(8,128)(2,1)S(1)}, bf16[128,512]{1,0:T(8,128)(2,1)S(1)}) custom-call(bf16[2,1,1,1024,256]{4,3,2,1,0:T(8,128)(2,1)} %stem_ref.3, bf16[3,2,256,256]{3,2,1,0:T(8,128)(2,1)} %branches_ref.3, s32[3,256]{1,0:T(4,128)} %order_ref.3), custom_call_target="tpu_custom_call" | custom-call | flops 1 | bytes 1 | tf_op jit(solution)/shard_map/pallas_call | solution.py:253
  1.7 4.1 %collective-permute-start = (bf16[128,512]{1,0:T(8,128)(2,1)S(1)}, bf16[128,512]{1,0:T(8,128)(2,1)S(1)}, u32[]{:S(2)}, u32[]{:S(2)}) collective-permute-start(bf16[128,512]{1,0:T(8,128)(2,1)S(1)} %get-tuple-element.26), channel_id=1, source_target_pairs={{0,2},{1,3},{2,0},{3,1},{4,6},{5,7},{6,4},{7,5},{8,10},{9,11},{10,... | collective-permute-start | bytes 393224 | tf_op jit(solution)/shard_map/ppermute | solution.py:219
  5.8 1.6 %collective-permute-start.8 = (bf16[128,512]{1,0:T(8,128)(2,1)S(1)}, bf16[128,512]{1,0:T(8,128)(2,1)S(1)}, u32[]{:S(2)}, u32[]{:S(2)}) collective-permute-start(bf16[128,512]{1,0:T(8,128)(2,1)S(1)} %get-tuple-element.37), channel_id=1, source_target_pairs={{0,1},{1,0},{2,3},{3,2},{4,5},{5,4},{6,7},{7,6},{8,9},{9,8},{10,11... | collective-permute-start | bytes 393224 | tf_op jit(solution)/shard_map/ppermute | solution.py:219
  7.4 0.0 collective-permute-start.9
  7.4 2.3 %shard_map.37 = (bf16[512,512]{1,0:T(8,128)(2,1)S(1)}, bf16[512,512]{1,0:T(8,128)(2,1)S(1)}, bf16[2,512,256]{2,1,0:T(8,128)(2,1)S(1)}) custom-call(bf16[2,1,1,1024,256]{4,3,2,1,0:T(8,128)(2,1)} %stem_ref.3, bf16[3,2,256,256]{3,2,1,0:T(8,128)(2,1)} %branches_ref.3, s32[3,256]{1,0:T(4,128)} %order_ref.3), custom_call_target="tpu_custom_call" | custom-call | flops 1 | bytes 1 | tf_op jit(solution)/shard_map/pallas_call | solution.py:263
  9.7 4.1 %collective-permute-done.rest_0_.refs_2_ = bf16[128,512]{1,0:T(8,128)(2,1)S(1)} collective-permute-done((bf16[128,512]{1,0:T(8,128)(2,1)S(1)}, bf16[128,512]{1,0:T(8,128)(2,1)S(1)}, u32[]{:S(2)}, u32[]{:S(2)}) %collective-permute-start) | collective-permute-done | bytes 131104 | tf_op jit(solution)/shard_map/ppermute | solution.py:219
  13.8 0.5 %shard_map.39 = (bf16[128,512]{1,0:T(8,128)(2,1)S(1)}, bf16[128,512]{1,0:T(8,128)(2,1)S(1)}, bf16[128,512]{1,0:T(8,128)(2,1)S(1)}, bf16[128,512]{1,0:T(8,128)(2,1)S(1)}) custom-call(bf16[2,512,256]{2,1,0:T(8,128)(2,1)S(1)} %get-tuple-element.24.block_ref, bf16[512,512]{1,0:T(8,128)(2,1)S(1)} %get-tuple-element.25.form_ref, ...), custom_call_target="tpu_custom_call" | custom-call | flops 1 | bytes 1 | tf_op jit(solution)/shard_map/pallas_call | solution.py:279
  14.3 0.1 collective-permute-start.1
  14.4 3.6 %collective-permute-start.2 = (bf16[128,512]{1,0:T(8,128)(2,1)S(1)}, bf16[128,512]{1,0:T(8,128)(2,1)S(1)}, u32[]{:S(2)}, u32[]{:S(2)}) collective-permute-start(bf16[128,512]{1,0:T(8,128)(2,1)S(1)} %get-tuple-element.29), channel_id=1, source_target_pairs={{0,2},{1,3},{2,0},{3,1},{4,6},{5,7},{6,4},{7,5},{8,10},{9,11},{10,... | collective-permute-start | bytes 393224 | tf_op jit(solution)/shard_map/ppermute | solution.py:219
  18.0 0.7 %collective-permute-start.3 = (bf16[128,512]{1,0:T(8,128)(2,1)S(1)}, bf16[128,512]{1,0:T(8,128)(2,1)S(1)}, u32[]{:S(2)}, u32[]{:S(2)}) collective-permute-start(bf16[128,512]{1,0:T(8,128)(2,1)S(1)} %get-tuple-element.30), channel_id=1, source_target_pairs={{0,3},{1,2},{2,1},{3,0},{4,7},{5,6},{6,5},{7,4},{8,11},{9,10},{10,... | collective-permute-start | bytes 393224 | tf_op jit(solution)/shard_map/ppermute | solution.py:219
  18.7 0.0 collective-permute-done.8.refs_1_
  18.7 0.0 collective-permute-done.9.refs_3_
  18.7 1.2 %shard_map.42 = bf16[512,512]{1,0:T(8,128)(2,1)} custom-call(bf16[512,512]{1,0:T(8,128)(2,1)S(1)} %get-tuple-element.23.rest_1_.form_ref, bf16[128,512]{1,0:T(8,128)(2,1)S(1)} %get-tuple-element.36.refs_0_, bf16[128,512]{1,0:T(8,128)(2,1)S(1)} %collective-permute-done.8.refs_1_, bf16[128,512]{1,0:T(8,128)(2,1)S(1)} %collective-permute-done.rest_0_.refs_2_, ...), custom_call_target="tpu_custom_call" | custom-call | flops 1 | bytes 1 | tf_op jit(solution)/shard_map/pallas_call | solution.py:294
  20.0 4.4 %all-to-all-start = ((bf16[8,64,512]{2,1,0:T(8,128)(2,1)}), bf16[8,64,512]{2,1,0:T(8,128)(2,1)S(1)}, u32[]{:S(2)}, u32[]{:S(2)}) async-start(bf16[8,64,512]{2,1,0:T(8,128)(2,1)} %bitcast), calls=%async_computation | async-start | bytes 1048576 | tf_op jit(solution)/shard_map/all_to_all | solution.py:224
  24.3 0.0 collective-permute-done.1.refs_1_
  24.3 3.7 %collective-permute-done.2.refs_2_ = bf16[128,512]{1,0:T(8,128)(2,1)S(1)} collective-permute-done((bf16[128,512]{1,0:T(8,128)(2,1)S(1)}, bf16[128,512]{1,0:T(8,128)(2,1)S(1)}, u32[]{:S(2)}, u32[]{:S(2)}) %collective-permute-start.2) | collective-permute-done | bytes 131104 | tf_op jit(solution)/shard_map/ppermute | solution.py:219
  28.0 0.0 collective-permute-done.3.refs_3_
  28.0 0.4 %shard_map.40 = (bf16[256,512]{1,0:T(8,128)(2,1)S(1)}, bf16[256,512]{1,0:T(8,128)(2,1)S(1)}) custom-call(bf16[512,512]{1,0:T(8,128)(2,1)S(1)} %get-tuple-element.23.rest_1_.form_ref, bf16[128,512]{1,0:T(8,128)(2,1)S(1)} %get-tuple-element.27.refs_0_, bf16[128,512]{1,0:T(8,128)(2,1)S(1)} %collective-permute-done.1.refs_1_, ...), custom_call_target="tpu_custom_call" | custom-call | flops 99999997952 | bytes 100000000 | tf_op jit(solution)/shard_map/pallas_call | solution.py:294
  28.5 0.1 collective-permute-start.4
  28.5 1.5 %collective-permute-done.4.came_ref.refs_1_ = bf16[256,512]{1,0:T(8,128)(2,1)S(1)} collective-permute-done((bf16[256,512]{1,0:T(8,128)(2,1)S(1)}, bf16[256,512]{1,0:T(8,128)(2,1)S(1)}, u32[]{:S(2)}, u32[]{:S(2)}) %collective-permute-start.4) | collective-permute-done | bytes 262176 | tf_op jit(solution)/shard_map/ppermute | solution.py:219
  30.1 1.6 %collective-permute-start.5 = (bf16[128,512]{1,0:T(8,128)(2,1)S(1)}, bf16[128,512]{1,0:T(8,128)(2,1)S(1)}, u32[]{:S(2)}, u32[]{:S(2)}) collective-permute-start(bf16[128,512]{1,0:T(8,128)(2,1)S(1)} %get-tuple-element.33), channel_id=1, source_target_pairs={{0,8},{4,12},{8,0},{12,4},{16,24},{20,28},{24,16},{28,20},{1,9},{5... | collective-permute-start | bytes 393224 | tf_op jit(solution)/shard_map/ppermute | solution.py:219
  31.7 1.5 %collective-permute-start.6 = (bf16[128,512]{1,0:T(8,128)(2,1)S(1)}, bf16[128,512]{1,0:T(8,128)(2,1)S(1)}, u32[]{:S(2)}, u32[]{:S(2)}) collective-permute-start(bf16[128,512]{1,0:T(8,128)(2,1)S(1)} %get-tuple-element.34), channel_id=1, source_target_pairs={{0,16},{4,20},{8,24},{12,28},{16,0},{20,4},{24,8},{28,12},{1,17},{... | collective-permute-start | bytes 393224 | tf_op jit(solution)/shard_map/ppermute | solution.py:219
  33.2 0.5 %collective-permute-start.7 = (bf16[128,512]{1,0:T(8,128)(2,1)S(1)}, bf16[128,512]{1,0:T(8,128)(2,1)S(1)}, u32[]{:S(2)}, u32[]{:S(2)}) collective-permute-start(bf16[128,512]{1,0:T(8,128)(2,1)S(1)} %get-tuple-element.35), channel_id=1, source_target_pairs={{0,24},{4,28},{8,16},{12,20},{16,8},{20,12},{24,0},{28,4},{1,25},{... | collective-permute-start | bytes 393224 | tf_op jit(solution)/shard_map/ppermute | solution.py:219
  33.7 0.6 %all-to-all-done = bf16[8,64,512]{2,1,0:T(8,128)(2,1)S(1)} async-done(((bf16[8,64,512]{2,1,0:T(8,128)(2,1)}), bf16[8,64,512]{2,1,0:T(8,128)(2,1)S(1)}, u32[]{:S(2)}, u32[]{:S(2)}) %all-to-all-start) | async-done | bytes 524320 | tf_op jit(solution)/shard_map/all_to_all | solution.py:224
  34.2 1.3 %shard_map.43.refs_5_ = bf16[2,1,1,1024,256]{4,3,2,1,0:T(8,128)(2,1)} custom-call(bf16[512,512]{1,0:T(8,128)(2,1)S(1)} %get-tuple-element.22.form_ref, bf16[512,512]{1,0:T(8,128)(2,1)S(1)} %bitcast.2), custom_call_target="tpu_custom_call" | custom-call | flops 1 | bytes 1 | tf_op jit(solution)/shard_map/pallas_call | solution.py:311
  35.5 1.0 %collective-permute-done.5.refs_2_ = bf16[128,512]{1,0:T(8,128)(2,1)S(1)} collective-permute-done((bf16[128,512]{1,0:T(8,128)(2,1)S(1)}, bf16[128,512]{1,0:T(8,128)(2,1)S(1)}, u32[]{:S(2)}, u32[]{:S(2)}) %collective-permute-start.5) | collective-permute-done | bytes 131104 | tf_op jit(solution)/shard_map/ppermute | solution.py:219
  36.5 2.3 %collective-permute-done.6.refs_3_ = bf16[128,512]{1,0:T(8,128)(2,1)S(1)} collective-permute-done((bf16[128,512]{1,0:T(8,128)(2,1)S(1)}, bf16[128,512]{1,0:T(8,128)(2,1)S(1)}, u32[]{:S(2)}, u32[]{:S(2)}) %collective-permute-start.6) | collective-permute-done | bytes 131104 | tf_op jit(solution)/shard_map/ppermute | solution.py:219
  38.8 1.0 %collective-permute-done.7.refs_4_ = bf16[128,512]{1,0:T(8,128)(2,1)S(1)} collective-permute-done((bf16[128,512]{1,0:T(8,128)(2,1)S(1)}, bf16[128,512]{1,0:T(8,128)(2,1)S(1)}, u32[]{:S(2)}, u32[]{:S(2)}) %collective-permute-start.7) | collective-permute-done | bytes 131104 | tf_op jit(solution)/shard_map/ppermute | solution.py:219
  39.8 1.3 %shard_map.44 = bf16[2,1,1,1024,256]{4,3,2,1,0:T(8,128)(2,1)} custom-call(bf16[512,512]{1,0:T(8,128)(2,1)S(1)} %get-tuple-element.22.form_ref, bf16[256,512]{1,0:T(8,128)(2,1)S(1)} %get-tuple-element.31.kept_ref.refs_0_, bf16[256,512]{1,0:T(8,128)(2,1)S(1)} %collective-permute-done.4.came_ref.refs_1_, ...), custom_call_target="tpu_custom_call", output_to_operand_aliasing={{}: (6, {})} | custom-call | flops 1 | bytes 1 | tf_op jit(solution)/shard_map/pallas_call | solution.py:311
  (1 shorter events, 0.0 us)
Async XLA Ops:
  1.7 12.1 %collective-permute-start = (bf16[128,512]{1,0:T(8,128)(2,1)S(1)}, bf16[128,512]{1,0:T(8,128)(2,1)S(1)}, u32[]{:S(2)}, u32[]{:S(2)}) collective-permute-start(bf16[128,512]{1,0:T(8,128)(2,1)S(1)} %get-tuple-element.26), channel_id=1, source_target_pairs={{0,2},{1,3},{2,0},{3,1},{4,6},{5,7},{6,4},{7,5},{8,10},{9,11},{10,... | collective-permute-start | bytes 393224 | tf_op jit(solution)/shard_map/ppermute | solution.py:219
  5.8 12.9 %collective-permute-start.8 = (bf16[128,512]{1,0:T(8,128)(2,1)S(1)}, bf16[128,512]{1,0:T(8,128)(2,1)S(1)}, u32[]{:S(2)}, u32[]{:S(2)}) collective-permute-start(bf16[128,512]{1,0:T(8,128)(2,1)S(1)} %get-tuple-element.37), channel_id=1, source_target_pairs={{0,1},{1,0},{2,3},{3,2},{4,5},{5,4},{6,7},{7,6},{8,9},{9,8},{10,11... | collective-permute-start | bytes 393224 | tf_op jit(solution)/shard_map/ppermute | solution.py:219
  7.4 11.3 %collective-permute-start.9 = (bf16[128,512]{1,0:T(8,128)(2,1)S(1)}, bf16[128,512]{1,0:T(8,128)(2,1)S(1)}, u32[]{:S(2)}, u32[]{:S(2)}) collective-permute-start(bf16[128,512]{1,0:T(8,128)(2,1)S(1)} %get-tuple-element.38), channel_id=1, source_target_pairs={{0,3},{1,2},{2,1},{3,0},{4,7},{5,6},{6,5},{7,4},{8,11},{9,10},{10,... | collective-permute-start | bytes 393224 | tf_op jit(solution)/shard_map/ppermute | solution.py:219
  14.3 10.1 %collective-permute-start.1 = (bf16[128,512]{1,0:T(8,128)(2,1)S(1)}, bf16[128,512]{1,0:T(8,128)(2,1)S(1)}, u32[]{:S(2)}, u32[]{:S(2)}) collective-permute-start(bf16[128,512]{1,0:T(8,128)(2,1)S(1)} %get-tuple-element.28), channel_id=1, source_target_pairs={{0,1},{1,0},{2,3},{3,2},{4,5},{5,4},{6,7},{7,6},{8,9},{9,8},{10,11... | collective-permute-start | bytes 393224 | tf_op jit(solution)/shard_map/ppermute | solution.py:219
  14.4 13.6 %collective-permute-start.2 = (bf16[128,512]{1,0:T(8,128)(2,1)S(1)}, bf16[128,512]{1,0:T(8,128)(2,1)S(1)}, u32[]{:S(2)}, u32[]{:S(2)}) collective-permute-start(bf16[128,512]{1,0:T(8,128)(2,1)S(1)} %get-tuple-element.29), channel_id=1, source_target_pairs={{0,2},{1,3},{2,0},{3,1},{4,6},{5,7},{6,4},{7,5},{8,10},{9,11},{10,... | collective-permute-start | bytes 393224 | tf_op jit(solution)/shard_map/ppermute | solution.py:219
  18.0 10.0 %collective-permute-start.3 = (bf16[128,512]{1,0:T(8,128)(2,1)S(1)}, bf16[128,512]{1,0:T(8,128)(2,1)S(1)}, u32[]{:S(2)}, u32[]{:S(2)}) collective-permute-start(bf16[128,512]{1,0:T(8,128)(2,1)S(1)} %get-tuple-element.30), channel_id=1, source_target_pairs={{0,3},{1,2},{2,1},{3,0},{4,7},{5,6},{6,5},{7,4},{8,11},{9,10},{10,... | collective-permute-start | bytes 393224 | tf_op jit(solution)/shard_map/ppermute | solution.py:219
  20.0 14.3 %all-to-all-start = ((bf16[8,64,512]{2,1,0:T(8,128)(2,1)}), bf16[8,64,512]{2,1,0:T(8,128)(2,1)S(1)}, u32[]{:S(2)}, u32[]{:S(2)}) async-start(bf16[8,64,512]{2,1,0:T(8,128)(2,1)} %bitcast), calls=%async_computation | async-start | bytes 1048576 | tf_op jit(solution)/shard_map/all_to_all | solution.py:224
  28.5 1.6 %collective-permute-start.4 = (bf16[256,512]{1,0:T(8,128)(2,1)S(1)}, bf16[256,512]{1,0:T(8,128)(2,1)S(1)}, u32[]{:S(2)}, u32[]{:S(2)}) collective-permute-start(bf16[256,512]{1,0:T(8,128)(2,1)S(1)} %get-tuple-element.32), channel_id=1, source_target_pairs={{0,4},{4,0},{8,12},{12,8},{16,20},{20,16},{24,28},{28,24},{1,5},{5... | collective-permute-start | bytes 786440 | tf_op jit(solution)/shard_map/ppermute | solution.py:219
  30.1 6.4 %collective-permute-start.5 = (bf16[128,512]{1,0:T(8,128)(2,1)S(1)}, bf16[128,512]{1,0:T(8,128)(2,1)S(1)}, u32[]{:S(2)}, u32[]{:S(2)}) collective-permute-start(bf16[128,512]{1,0:T(8,128)(2,1)S(1)} %get-tuple-element.33), channel_id=1, source_target_pairs={{0,8},{4,12},{8,0},{12,4},{16,24},{20,28},{24,16},{28,20},{1,9},{5... | collective-permute-start | bytes 393224 | tf_op jit(solution)/shard_map/ppermute | solution.py:219
  31.7 7.1 %collective-permute-start.6 = (bf16[128,512]{1,0:T(8,128)(2,1)S(1)}, bf16[128,512]{1,0:T(8,128)(2,1)S(1)}, u32[]{:S(2)}, u32[]{:S(2)}) collective-permute-start(bf16[128,512]{1,0:T(8,128)(2,1)S(1)} %get-tuple-element.34), channel_id=1, source_target_pairs={{0,16},{4,20},{8,24},{12,28},{16,0},{20,4},{24,8},{28,12},{1,17},{... | collective-permute-start | bytes 393224 | tf_op jit(solution)/shard_map/ppermute | solution.py:219
  33.2 6.6 %collective-permute-start.7 = (bf16[128,512]{1,0:T(8,128)(2,1)S(1)}, bf16[128,512]{1,0:T(8,128)(2,1)S(1)}, u32[]{:S(2)}, u32[]{:S(2)}) collective-permute-start(bf16[128,512]{1,0:T(8,128)(2,1)S(1)} %get-tuple-element.35), channel_id=1, source_target_pairs={{0,24},{4,28},{8,16},{12,20},{16,8},{20,12},{24,0},{28,4},{1,25},{... | collective-permute-start | bytes 393224 | tf_op jit(solution)/shard_map/ppermute | solution.py:219

commit v3 on v2

v3 whole, which is shorter than its diff:
```python
import functools

import jax
import jax.numpy as jnp
from jax import lax
from jax.experimental import pallas as pl
from jax.experimental.pallas import tpu as pltpu
from jax.sharding import PartitionSpec as P

BF16 = jnp.bfloat16
F32 = jnp.float32
VMEM_LIMIT = 16 * 1024 * 1024
ROW_SPLIT = (1, 1)
PERMUTE_MAX = 8
WRITE_CUT = 2
FREE, LONG = 1, 10**11


def iota(shape, dim):
    return lax.broadcasted_iota(jnp.int32, shape, dim)


def dot(a, b, ca, cb):
    return lax.dot_general(a, b, (((ca,), (cb,)), ((), ())), preferred_element_type=F32)


def entry(position, part, me):
    owner = position // (2 * part)
    owner = owner if me is None else owner ^ me
    return (position // part) % 2, owner * part + position % part


def both(branch):
    return jnp.concatenate([branch[0], branch[1]], axis=1)


def chosen(order_row, states, column):
    width = order_row.shape[1]
    pick = (iota((width, column), 0) == states).astype(BF16)
    rows = dot(order_row.astype(BF16), pick, 1, 0)
    return (iota((width, column), 0) == rows.astype(jnp.int32)).astype(BF16)


def first_form(branch, order_row):
    width = order_row.shape[1]
    hot = (iota((width, width), 0) == order_row).astype(BF16)
    taken = dot(both(branch), hot, 0, 0).astype(BF16)
    real, imag = taken[:width], taken[width:]
    return jnp.concatenate(
        [jnp.concatenate([real, -imag], axis=1), jnp.concatenate([imag, real], axis=1)], axis=0
    )


def second_form(branch, order_row, part_in, me_in, part_out, me_out):
    width = order_row.shape[1]
    full = 2 * width
    comp, states = entry(iota((1, full), 1), part_in, me_in)
    hot = chosen(order_row, states, full)
    taken = dot(both(branch), hot, 0, 0)
    real, imag = taken[:width], taken[width:]
    plain = comp == 0
    form = jnp.concatenate(
        [jnp.where(plain, real, -imag), jnp.where(plain, imag, real)], axis=0
    ).astype(BF16)
    out_comp, out_states = entry(iota((full, 1), 0), part_out, me_out)
    place = (iota((full, full), 1) == out_comp * width + out_states).astype(BF16)
    return dot(place, form, 1, 0).astype(BF16)


def third_form(branch, order_row, part_in, me_in):
    width = order_row.shape[1]
    full = 2 * width
    _, states = entry(iota((1, full), 1), part_in, me_in)
    hot = chosen(order_row, states, full)
    taken = dot(hot, both(branch), 0, 0)
    real, imag = taken[:, :width], taken[:, width:]
    comp, _ = entry(iota((full, 1), 0), part_in, me_in)
    plain = comp == 0
    return jnp.concatenate(
        [jnp.where(plain, real, -imag), jnp.where(plain, imag, real)], axis=1
    ).astype(BF16)


def place_of(axis, relative):
    return lax.axis_index(axis) if relative else None


def put_first(form_ref, block, part, me, owners, outs):
    width = block.shape[2]
    form = []
    for k in owners:
        owner = k if me is None else jnp.bitwise_xor(me, k)
        form += [form_ref[pl.ds(pl.multiple_of(c * width + owner * part, part), part), :] for c in range(2)]
    joined = jnp.concatenate([block[0], block[1]], axis=1)
    result = dot(jnp.concatenate(form, axis=0), joined, 1, 1).astype(BF16)
    size = result.shape[0] // len(outs)
    for n, out in enumerate(outs):
        out[...] = result[size * n : size * (n + 1)]


def opening_kernel(part, relative, owners, stem_ref, branches_ref, order_ref, form_ref, block_ref, *rest):
    outs, (branch, order, sem) = rest[:-3], rest[-3:]
    copies = [
        pltpu.make_async_copy(order_ref, order, sem.at[0]),
        pltpu.make_async_copy(branches_ref.at[0], branch, sem.at[1]),
        pltpu.make_async_copy(stem_ref.at[:, 0, 0, pl.ds(0, block_ref.shape[1])], block_ref, sem.at[2]),
    ]
    for copy in copies:
        copy.start()
    copies[0].wait()
    copies[1].wait()
    form_ref[...] = first_form(branch, order[0:1, :])
    copies[2].wait()
    put_first(form_ref, block_ref, part, place_of("mem", relative), owners, outs)


def first_kernel(part, relative, owners, n_out, block_ref, form_ref, *rest):
    put_first(form_ref, block_ref, part, place_of("mem", relative), owners, rest[-n_out:])


def forms_kernel(sizes, part1, rel1, part2, rel2, stem_ref, branches_ref, order_ref, second_ref, third_ref, *rest):
    blocks, (branch, order, sem) = rest[:-3], rest[-3:]
    copies = [
        pltpu.make_async_copy(order_ref, order, sem.at[0]),
        pltpu.make_async_copy(branches_ref.at[pl.ds(1, 2)], branch, sem.at[1]),
    ]
    lo = sizes[0]
    for n, rows in enumerate(sizes[1:]):
        copies.append(pltpu.make_async_copy(stem_ref.at[:, 0, 0, pl.ds(lo, rows)], blocks[n], sem.at[2 + n]))
        lo += rows
    for copy in copies:
        copy.start()
    copies[0].wait()
    copies[1].wait()
    me1, me2 = place_of("mem", rel1), place_of("grp", rel2)
    second_ref[...] = second_form(branch[0], order[1:2, :], part1, me1, part2, me2)
    third_ref[...] = third_form(branch[1], order[2:3, :], part2, me2)
    for copy in copies[2:]:
        copy.wait()


def gathered(refs):
    return jnp.concatenate([ref[...] for ref in refs], axis=0)


def second_kernel(n_in, slots, form_ref, *refs):
    ins, outs = refs[:n_in], refs[n_in:]
    joined = gathered(ins)
    for slot, out in zip(slots, outs):
        rows = out.shape[0]
        out[...] = dot(form_ref[rows * slot : rows * (slot + 1)], joined, 1, 0).astype(BF16)


def pass_kernel(*refs):
    size = refs[0].shape[0] // 2
    for slot, ref in enumerate(refs[:-1]):
        refs[-1][slot * size : (slot + 1) * size] = ref[size:]


def third_kernel(n_in, lo, form_ref, *refs):
    ins, (out_ref, held, sem) = refs[:n_in], refs[-3:]
    if n_in > 1:
        size = ins[0].shape[0] // 2
        ins = sum(
            [[ref.at[:size], ins[-1].at[slot * size : (slot + 1) * size]] for slot, ref in enumerate(ins[:-1])], []
        )
    joined, form = gathered(ins), form_ref[...]
    width, rows = form.shape[1] // 2, held.shape[1]
    cut = rows // WRITE_CUT
    copies = []
    for n in range(WRITE_CUT):
        result = dot(joined[:, n * cut : (n + 1) * cut], form, 0, 0).astype(BF16)
        for c in range(2):
            held[c, n * cut : (n + 1) * cut] = result[:, c * width : (c + 1) * width]
            there = out_ref.at[c, 0, 0, pl.ds(lo + n * cut, cut)]
            copies.append(pltpu.make_async_copy(held.at[c, pl.ds(n * cut, cut)], there, sem.at[2 * n + c]))
            copies[-1].start()
    for copy in copies:
        copy.wait()


ANY = pl.BlockSpec(memory_space=pl.ANY)
HBM = pl.BlockSpec(memory_space=pltpu.HBM)
VM = pl.BlockSpec(memory_space=pltpu.VMEM)


def call(kernel, in_specs, out_shapes, out_specs, cost=FREE, scratch=(), aliases={}):
    return pl.pallas_call(
        kernel,
        in_specs=in_specs,
        out_shape=out_shapes,
        out_specs=out_specs,
        scratch_shapes=list(scratch),
        input_output_aliases=aliases,
        compiler_params=pltpu.CompilerParams(vmem_limit_bytes=VMEM_LIMIT),
        cost_estimate=pl.CostEstimate(flops=cost, bytes_accessed=max(1, cost // 1000), transcendentals=0),
    )


def swap(piece, axis, count, k):
    return lax.ppermute(piece, axis, [(i, i ^ k) for i in range(count)])


def whole_exchange(whole, axis, count):
    shaped = whole.reshape(count, -1, whole.shape[-1])
    moved = lax.all_to_all(shaped, axis, split_axis=0, concat_axis=0, tiled=True)
    return moved.reshape(whole.shape)


def shape(*dims):
    return jax.ShapeDtypeStruct(dims, BF16)


def by_permutes(count):
    return 4 <= count <= PERMUTE_MAX and count & (count - 1) == 0


def local(stem, branches, mode_order):
    row_count, width = stem.shape[3], stem.shape[4]
    full = 2 * width
    inner, outer = lax.axis_size("mem"), lax.axis_size("grp")
    part1, part2 = width // inner, width // outer
    rel1, rel2 = by_permutes(inner), by_permutes(outer)
    sizes = [row_count * share // sum(ROW_SPLIT) for share in ROW_SPLIT]
    starts = [sum(sizes[:n]) for n in range(len(sizes))]
    last = len(sizes) - 1
    stem, branches, mode_order = (
        pltpu.with_memory_space_constraint(a, pltpu.HBM) for a in (stem, branches, mode_order)
    )
    form_shape = shape(full, full)
    order_scratch = pltpu.VMEM(mode_order.shape, jnp.int32)
    half = inner // 2

    def first_shapes(rows, owners):
        return [shape(full // inner, rows)] * len(owners) if rel1 else [shape(full, rows)]

    def first_pieces(block, owners, after=()):
        shapes = first_shapes(block.shape[1], owners)
        made = call(
            functools.partial(first_kernel, part1, rel1, owners, len(shapes)),
            [VM, VM] + [ANY] * len(after), shapes, [VM] * len(shapes),
        )(block, form0, *after)
        return dict(zip(owners, made))

    def inner_exchange(pieces):
        if not rel1:
            return [whole_exchange(pieces[0], "mem", inner)]
        return [pieces[0]] + [swap(pieces[k], "mem", inner, k) for k in range(1, inner)]

    everything = tuple(range(inner))
    opening = (half,) if rel1 else everything
    shapes = first_shapes(sizes[0], opening)
    form0, block, *made = call(
        functools.partial(opening_kernel, part1, rel1, opening),
        [HBM] * 3, [form_shape, shape(2, sizes[0], width)] + shapes, [VM] * (2 + len(shapes)), FREE,
        [pltpu.VMEM(branches.shape[1:], BF16), order_scratch, pltpu.SemaphoreType.DMA((3,))],
    )(stem, branches, mode_order)
    pieces = dict(zip(opening, made))
    if rel1:
        pieces.update(first_pieces(block, tuple(k for k in everything if k != half)))
    arrived = [inner_exchange(pieces)]
    form1, form2, *blocks = call(
        functools.partial(forms_kernel, sizes, part1, rel1, part2, rel2),
        [HBM] * 3, [form_shape] * 2 + [shape(2, rows, width) for rows in sizes[1:]], [VM] * (1 + len(sizes)), FREE,
        [pltpu.VMEM((2,) + branches.shape[1:], BF16), order_scratch, pltpu.SemaphoreType.DMA((1 + len(sizes),))],
    )(stem, branches, mode_order)
    for block in blocks:
        after = (form1, arrived[-1][half]) if rel1 else ()
        arrived.append(inner_exchange(first_pieces(block, everything, after)))

    pairs = outer // 2

    def second(n, slots, rows_each, cost):
        ins = arrived[n]
        shapes = [shape(rows_each, sizes[n])] * len(slots)
        made = call(
            functools.partial(second_kernel, len(ins), slots), [VM] * (1 + len(ins)), shapes, [VM] * len(slots), cost
        )(form1, *ins)
        return dict(zip(slots, made))

    def outer_exchange(n):
        cost = LONG if n == last else FREE
        if not rel2:
            return [whole_exchange(second(n, (0,), full, cost)[0], "grp", outer)]
        slots = tuple(range(pairs))
        early = slots[:1] + slots[2:] if n == last else slots
        made = second(n, early, full // pairs, cost)
        if n == last:
            made.update(second(n, slots[1:2], full // pairs, FREE))
        came = [made[0]] + [swap(made[q], "grp", outer, 2 * q) for q in slots[1:]]
        passed = call(pass_kernel, [VM] * pairs, shape(full // 2, sizes[n]), VM)(*came)
        return came + [swap(passed, "grp", outer, 1)]

    out = ()
    for n, rows in enumerate(sizes):
        ins = outer_exchange(n)
        out = (
            call(
                functools.partial(third_kernel, len(ins), starts[n]),
                [VM] * (1 + len(ins)) + [ANY] * len(out), shape(*stem.shape), ANY, FREE,
                [pltpu.VMEM((2, rows, width), BF16), pltpu.SemaphoreType.DMA((2 * WRITE_CUT,))],
                {1 + len(ins): 0} if out else {},
            )(form2, *ins, *out),
        )
    return out[0]


def solution(mesh):
    in_specs = (P(None, "grp", "mem", None, None), P(), P())
    out_specs = P(None, "grp", "mem", None, None)
    return jax.shard_map(local, mesh=mesh, in_specs=in_specs, out_specs=out_specs, check_vma=False)
```

time: 41.3 us -> 40.2 us (0.973)
  the two profiles are of different devices: /device:TPU:0 before, /device:TPU:21 now
where the time goes in v3:
time: 40.2 us; the launch traced here: 40 us
  starting transfers between devices  19.6 us (49%)
  waiting for transfers between devices  12.1 us (30%)
  Pallas kernels  8.23 us (20%)
    ppermute x14, starting transfers between devices, swap(): return lax.ppermute(piece, axis, [(i, i ^ k) for i in range(count)])  19.6 us
    ppermute x14, waiting for transfers between devices, swap(): return lax.ppermute(piece, axis, [(i, i ^ k) for i in range(count)])  12.1 us
    pallas_call x2, Pallas kernels, local(): call(functools.partial(third_kernel, len(ins), starts[n]), [VM] * (1 + le...  2.41 us
    pallas_call x1, Pallas kernels, local(): call(functools.partial(forms_kernel, sizes, part1, rel1, part2, rel2), [H...  2.31 us
    pallas_call x1, Pallas kernels, local(): call(functools.partial(opening_kernel, part1, rel1, opening), [HBM] * 3,...  1.56 us
    pallas_call x3, Pallas kernels, second(): call(functools.partial(second_kernel, len(ins), slots), [VM] * (1 + len(i...  1.05 us
    pallas_call x2, Pallas kernels, first_pieces(): call(functools.partial(first_kernel, part1, rel1, owners, len(shapes)), [...  0.86 us
  transfers between devices with their start and end apart: 14, of which 4 were waited for; matrix products, arithmetic and copies ran while one was open for 0% of the time, Pallas kernels for 14%

profile of v3, /device:TPU:21, one launch (start us, length us, event | category | flops | bytes accessed | tf_op | source)
XLA Modules:
  0.0 40.0 jit_solution(15711105562986585450)
XLA Ops:
  0.0 1.6 %shard_map.38 = (bf16[512,512]{1,0:T(8,128)(2,1)S(1)}, bf16[2,512,256]{2,1,0:T(8,128)(2,1)S(1)}, bf16[128,512]{1,0:T(8,128)(2,1)S(1)}) custom-call(bf16[2,1,1,1024,256]{4,3,2,1,0:T(8,128)(2,1)} %stem_ref.3, bf16[3,2,256,256]{3,2,1,0:T(8,128)(2,1)} %branches_ref.3, s32[3,256]{1,0:T(4,128)} %order_ref.3), custom_call_target="tpu_custom_call" | custom-call | flops 1 | bytes 1 | tf_op jit(solution)/shard_map/pallas_call | solution.py:253
  1.6 0.1 collective-permute-start
  1.7 0.4 shard_map.43
  2.1 1.4 %collective-permute-start.8 = (bf16[128,512]{1,0:T(8,128)(2,1)S(1)}, bf16[128,512]{1,0:T(8,128)(2,1)S(1)}, u32[]{:S(2)}, u32[]{:S(2)}) collective-permute-start(bf16[128,512]{1,0:T(8,128)(2,1)S(1)} %get-tuple-element.39), channel_id=1, source_target_pairs={{0,1},{1,0},{2,3},{3,2},{4,5},{5,4},{6,7},{7,6},{8,9},{9,8},{10,11... | collective-permute-start | bytes 393224 | tf_op jit(solution)/shard_map/ppermute | solution.py:201
  3.5 1.3 %collective-permute-start.9 = (bf16[128,512]{1,0:T(8,128)(2,1)S(1)}, bf16[128,512]{1,0:T(8,128)(2,1)S(1)}, u32[]{:S(2)}, u32[]{:S(2)}) collective-permute-start(bf16[128,512]{1,0:T(8,128)(2,1)S(1)} %get-tuple-element.40), channel_id=1, source_target_pairs={{0,3},{1,2},{2,1},{3,0},{4,7},{5,6},{6,5},{7,4},{8,11},{9,10},{10,... | collective-permute-start | bytes 393224 | tf_op jit(solution)/shard_map/ppermute | solution.py:201
  4.8 2.3 %shard_map.37 = (bf16[512,512]{1,0:T(8,128)(2,1)S(1)}, bf16[512,512]{1,0:T(8,128)(2,1)S(1)}, bf16[2,512,256]{2,1,0:T(8,128)(2,1)S(1)}) custom-call(bf16[2,1,1,1024,256]{4,3,2,1,0:T(8,128)(2,1)} %stem_ref.3, bf16[3,2,256,256]{3,2,1,0:T(8,128)(2,1)} %branches_ref.3, s32[3,256]{1,0:T(4,128)} %order_ref.3), custom_call_target="tpu_custom_call" | custom-call | flops 1 | bytes 1 | tf_op jit(solution)/shard_map/pallas_call | solution.py:262
  7.1 0.0 collective-permute-done.rest_1_.refs_2_
  7.1 0.5 %shard_map.39 = (bf16[128,512]{1,0:T(8,128)(2,1)S(1)}, bf16[128,512]{1,0:T(8,128)(2,1)S(1)}, bf16[128,512]{1,0:T(8,128)(2,1)S(1)}, bf16[128,512]{1,0:T(8,128)(2,1)S(1)}) custom-call(bf16[2,512,256]{2,1,0:T(8,128)(2,1)S(1)} %get-tuple-element.27.block_ref, bf16[512,512]{1,0:T(8,128)(2,1)S(1)} %get-tuple-element.28.form_ref, ...), custom_call_target="tpu_custom_call" | custom-call | flops 1 | bytes 1 | tf_op jit(solution)/shard_map/pallas_call | solution.py:239
  7.6 5.9 %collective-permute-start.1 = (bf16[128,512]{1,0:T(8,128)(2,1)S(1)}, bf16[128,512]{1,0:T(8,128)(2,1)S(1)}, u32[]{:S(2)}, u32[]{:S(2)}) collective-permute-start(bf16[128,512]{1,0:T(8,128)(2,1)S(1)} %get-tuple-element.31), channel_id=1, source_target_pairs={{0,1},{1,0},{2,3},{3,2},{4,5},{5,4},{6,7},{7,6},{8,9},{9,8},{10,11... | collective-permute-start | bytes 393224 | tf_op jit(solution)/shard_map/ppermute | solution.py:201
  13.5 0.0 collective-permute-start.2
  13.5 1.3 %collective-permute-start.3 = (bf16[128,512]{1,0:T(8,128)(2,1)S(1)}, bf16[128,512]{1,0:T(8,128)(2,1)S(1)}, u32[]{:S(2)}, u32[]{:S(2)}) collective-permute-start(bf16[128,512]{1,0:T(8,128)(2,1)S(1)} %get-tuple-element.33), channel_id=1, source_target_pairs={{0,3},{1,2},{2,1},{3,0},{4,7},{5,6},{6,5},{7,4},{8,11},{9,10},{10,... | collective-permute-start | bytes 393224 | tf_op jit(solution)/shard_map/ppermute | solution.py:201
  14.7 0.0 collective-permute-done.8.refs_1_
  14.7 1.6 %collective-permute-done.9.refs_3_ = bf16[128,512]{1,0:T(8,128)(2,1)S(1)} collective-permute-done((bf16[128,512]{1,0:T(8,128)(2,1)S(1)}, bf16[128,512]{1,0:T(8,128)(2,1)S(1)}, u32[]{:S(2)}, u32[]{:S(2)}) %collective-permute-start.9) | collective-permute-done | bytes 131104 | tf_op jit(solution)/shard_map/ppermute | solution.py:201
  16.4 0.4 %shard_map.44 = (bf16[128,512]{1,0:T(8,128)(2,1)S(1)}, bf16[128,512]{1,0:T(8,128)(2,1)S(1)}, bf16[128,512]{1,0:T(8,128)(2,1)S(1)}, bf16[128,512]{1,0:T(8,128)(2,1)S(1)}) custom-call(bf16[512,512]{1,0:T(8,128)(2,1)S(1)} %get-tuple-element.26.rest_0_.form_ref, bf16[128,512]{1,0:T(8,128)(2,1)S(1)} %get-tuple-element.38.refs_0_, ...), custom_call_target="tpu_custom_call" | custom-call | flops 1 | bytes 1 | tf_op jit(solution)/shard_map/pallas_call | solution.py:276
  16.8 1.3 %collective-permute-start.10 = (bf16[128,512]{1,0:T(8,128)(2,1)S(1)}, bf16[128,512]{1,0:T(8,128)(2,1)S(1)}, u32[]{:S(2)}, u32[]{:S(2)}) collective-permute-start(bf16[128,512]{1,0:T(8,128)(2,1)S(1)} %get-tuple-element.42), channel_id=1, source_target_pairs={{0,8},{4,12},{8,0},{12,4},{16,24},{20,28},{24,16},{28,20},{1,9},{5... | collective-permute-start | bytes 393224 | tf_op jit(solution)/shard_map/ppermute | solution.py:201
  18.1 0.2 collective-permute-start.11
  18.3 0.0 collective-permute-done.1.refs_1_
  18.3 1.2 %collective-permute-start.12 = (bf16[128,512]{1,0:T(8,128)(2,1)S(1)}, bf16[128,512]{1,0:T(8,128)(2,1)S(1)}, u32[]{:S(2)}, u32[]{:S(2)}) collective-permute-start(bf16[128,512]{1,0:T(8,128)(2,1)S(1)} %get-tuple-element.44), channel_id=1, source_target_pairs={{0,24},{4,28},{8,16},{12,20},{16,8},{20,12},{24,0},{28,4},{1,25},{... | collective-permute-start | bytes 393224 | tf_op jit(solution)/shard_map/ppermute | solution.py:201
  19.6 0.0 collective-permute-done.2.refs_2_
  19.6 7.4 %collective-permute-done.3.refs_3_ = bf16[128,512]{1,0:T(8,128)(2,1)S(1)} collective-permute-done((bf16[128,512]{1,0:T(8,128)(2,1)S(1)}, bf16[128,512]{1,0:T(8,128)(2,1)S(1)}, u32[]{:S(2)}, u32[]{:S(2)}) %collective-permute-start.3) | collective-permute-done | bytes 131104 | tf_op jit(solution)/shard_map/ppermute | solution.py:201
  27.0 0.4 shard_map.40
  27.4 0.3 collective-permute-start.5
  27.7 2.2 %collective-permute-start.6 = (bf16[128,512]{1,0:T(8,128)(2,1)S(1)}, bf16[128,512]{1,0:T(8,128)(2,1)S(1)}, u32[]{:S(2)}, u32[]{:S(2)}) collective-permute-start(bf16[128,512]{1,0:T(8,128)(2,1)S(1)} %get-tuple-element.36), channel_id=1, source_target_pairs={{0,24},{4,28},{8,16},{12,20},{16,8},{20,12},{24,0},{28,4},{1,25},{... | collective-permute-start | bytes 393224 | tf_op jit(solution)/shard_map/ppermute | solution.py:201
  29.9 0.2 shard_map.41
  30.1 0.0 collective-permute-done.10.refs_1_
  30.1 0.3 collective-permute-start.4
  30.4 0.0 collective-permute-done.11.refs_2_
  30.4 0.0 collective-permute-done.12.refs_3_
  30.4 2.0 %collective-permute-start.13 = (bf16[256,512]{1,0:T(8,128)(2,1)S(1)}, bf16[256,512]{1,0:T(8,128)(2,1)S(1)}, u32[]{:S(2)}, u32[]{:S(2)}) collective-permute-start(bf16[256,512]{1,0:T(8,128)(2,1)S(1)} %shard_map.45), channel_id=1, source_target_pairs={{0,4},{4,0},{8,12},{12,8},{16,20},{20,16},{24,28},{28,24},{1,5},{5... | collective-permute-start | bytes 786440 | tf_op jit(solution)/shard_map/ppermute | solution.py:201
  32.4 0.6 %collective-permute-done.5.refs_2_ = bf16[128,512]{1,0:T(8,128)(2,1)S(1)} collective-permute-done((bf16[128,512]{1,0:T(8,128)(2,1)S(1)}, bf16[128,512]{1,0:T(8,128)(2,1)S(1)}, u32[]{:S(2)}, u32[]{:S(2)}) %collective-permute-start.5) | collective-permute-done | bytes 131104 | tf_op jit(solution)/shard_map/ppermute | solution.py:201
  33.0 0.0 collective-permute-done.6.refs_3_
  33.0 2.4 %collective-permute-done.4.refs_1_ = bf16[128,512]{1,0:T(8,128)(2,1)S(1)} collective-permute-done((bf16[128,512]{1,0:T(8,128)(2,1)S(1)}, bf16[128,512]{1,0:T(8,128)(2,1)S(1)}, u32[]{:S(2)}, u32[]{:S(2)}) %collective-permute-start.4) | collective-permute-done | bytes 131104 | tf_op jit(solution)/shard_map/ppermute | solution.py:201
  35.4 2.2 %collective-permute-start.7 = (bf16[256,512]{1,0:T(8,128)(2,1)S(1)}, bf16[256,512]{1,0:T(8,128)(2,1)S(1)}, u32[]{:S(2)}, u32[]{:S(2)}) collective-permute-start(bf16[256,512]{1,0:T(8,128)(2,1)S(1)} %shard_map.42), channel_id=1, source_target_pairs={{0,4},{4,0},{8,12},{12,8},{16,20},{20,16},{24,28},{28,24},{1,5},{5... | collective-permute-start | bytes 786440 | tf_op jit(solution)/shard_map/ppermute | solution.py:201
  37.6 0.0 collective-permute-done.13.refs_4_
  37.6 1.2 %shard_map.46.refs_5_ = bf16[2,1,1,1024,256]{4,3,2,1,0:T(8,128)(2,1)} custom-call(bf16[512,512]{1,0:T(8,128)(2,1)S(1)} %get-tuple-element.25.form_ref, bf16[128,512]{1,0:T(8,128)(2,1)S(1)} %get-tuple-element.41.refs_0_, bf16[128,512]{1,0:T(8,128)(2,1)S(1)} %collective-permute-done.10.refs_1_, bf16[128,512]{1,0:T(8,128)(2,1)S(1)} %collective-permute-done.11.refs_2_, ...), custom_call_target="tpu_custom_call" | custom-call | flops 1 | bytes 1 | tf_op jit(solution)/shard_map/pallas_call | solution.py:298
  38.8 0.0 collective-permute-done.7.refs_4_
  38.8 1.2 %shard_map.47 = bf16[2,1,1,1024,256]{4,3,2,1,0:T(8,128)(2,1)} custom-call(bf16[512,512]{1,0:T(8,128)(2,1)S(1)} %get-tuple-element.25.form_ref, bf16[128,512]{1,0:T(8,128)(2,1)S(1)} %get-tuple-element.34.refs_0_, bf16[128,512]{1,0:T(8,128)(2,1)S(1)} %collective-permute-done.4.refs_1_, ...), custom_call_target="tpu_custom_call", output_to_operand_aliasing={{}: (6, {})} | custom-call | flops 1 | bytes 1 | tf_op jit(solution)/shard_map/pallas_call | solution.py:298
  (2 shorter events, 0.0 us)
Async XLA Ops:
  1.6 5.5 %collective-permute-start = (bf16[128,512]{1,0:T(8,128)(2,1)S(1)}, bf16[128,512]{1,0:T(8,128)(2,1)S(1)}, u32[]{:S(2)}, u32[]{:S(2)}) collective-permute-start(bf16[128,512]{1,0:T(8,128)(2,1)S(1)} %get-tuple-element.29), channel_id=1, source_target_pairs={{0,2},{1,3},{2,0},{3,1},{4,6},{5,7},{6,4},{7,5},{8,10},{9,11},{10,... | collective-permute-start | bytes 393224 | tf_op jit(solution)/shard_map/ppermute | solution.py:201
  2.1 12.6 %collective-permute-start.8 = (bf16[128,512]{1,0:T(8,128)(2,1)S(1)}, bf16[128,512]{1,0:T(8,128)(2,1)S(1)}, u32[]{:S(2)}, u32[]{:S(2)}) collective-permute-start(bf16[128,512]{1,0:T(8,128)(2,1)S(1)} %get-tuple-element.39), channel_id=1, source_target_pairs={{0,1},{1,0},{2,3},{3,2},{4,5},{5,4},{6,7},{7,6},{8,9},{9,8},{10,11... | collective-permute-start | bytes 393224 | tf_op jit(solution)/shard_map/ppermute | solution.py:201
  3.5 12.9 %collective-permute-start.9 = (bf16[128,512]{1,0:T(8,128)(2,1)S(1)}, bf16[128,512]{1,0:T(8,128)(2,1)S(1)}, u32[]{:S(2)}, u32[]{:S(2)}) collective-permute-start(bf16[128,512]{1,0:T(8,128)(2,1)S(1)} %get-tuple-element.40), channel_id=1, source_target_pairs={{0,3},{1,2},{2,1},{3,0},{4,7},{5,6},{6,5},{7,4},{8,11},{9,10},{10,... | collective-permute-start | bytes 393224 | tf_op jit(solution)/shard_map/ppermute | solution.py:201
  7.6 10.8 %collective-permute-start.1 = (bf16[128,512]{1,0:T(8,128)(2,1)S(1)}, bf16[128,512]{1,0:T(8,128)(2,1)S(1)}, u32[]{:S(2)}, u32[]{:S(2)}) collective-permute-start(bf16[128,512]{1,0:T(8,128)(2,1)S(1)} %get-tuple-element.31), channel_id=1, source_target_pairs={{0,1},{1,0},{2,3},{3,2},{4,5},{5,4},{6,7},{7,6},{8,9},{9,8},{10,11... | collective-permute-start | bytes 393224 | tf_op jit(solution)/shard_map/ppermute | solution.py:201
  13.5 6.1 %collective-permute-start.2 = (bf16[128,512]{1,0:T(8,128)(2,1)S(1)}, bf16[128,512]{1,0:T(8,128)(2,1)S(1)}, u32[]{:S(2)}, u32[]{:S(2)}) collective-permute-start(bf16[128,512]{1,0:T(8,128)(2,1)S(1)} %get-tuple-element.32), channel_id=1, source_target_pairs={{0,2},{1,3},{2,0},{3,1},{4,6},{5,7},{6,4},{7,5},{8,10},{9,11},{10,... | collective-permute-start | bytes 393224 | tf_op jit(solution)/shard_map/ppermute | solution.py:201
  13.5 13.5 %collective-permute-start.3 = (bf16[128,512]{1,0:T(8,128)(2,1)S(1)}, bf16[128,512]{1,0:T(8,128)(2,1)S(1)}, u32[]{:S(2)}, u32[]{:S(2)}) collective-permute-start(bf16[128,512]{1,0:T(8,128)(2,1)S(1)} %get-tuple-element.33), channel_id=1, source_target_pairs={{0,3},{1,2},{2,1},{3,0},{4,7},{5,6},{6,5},{7,4},{8,11},{9,10},{10,... | collective-permute-start | bytes 393224 | tf_op jit(solution)/shard_map/ppermute | solution.py:201
  16.8 13.3 %collective-permute-start.10 = (bf16[128,512]{1,0:T(8,128)(2,1)S(1)}, bf16[128,512]{1,0:T(8,128)(2,1)S(1)}, u32[]{:S(2)}, u32[]{:S(2)}) collective-permute-start(bf16[128,512]{1,0:T(8,128)(2,1)S(1)} %get-tuple-element.42), channel_id=1, source_target_pairs={{0,8},{4,12},{8,0},{12,4},{16,24},{20,28},{24,16},{28,20},{1,9},{5... | collective-permute-start | bytes 393224 | tf_op jit(solution)/shard_map/ppermute | solution.py:201
  18.1 12.3 %collective-permute-start.11 = (bf16[128,512]{1,0:T(8,128)(2,1)S(1)}, bf16[128,512]{1,0:T(8,128)(2,1)S(1)}, u32[]{:S(2)}, u32[]{:S(2)}) collective-permute-start(bf16[128,512]{1,0:T(8,128)(2,1)S(1)} %get-tuple-element.43), channel_id=1, source_target_pairs={{0,16},{4,20},{8,24},{12,28},{16,0},{20,4},{24,8},{28,12},{1,17},{... | collective-permute-start | bytes 393224 | tf_op jit(solution)/shard_map/ppermute | solution.py:201
  18.3 12.1 %collective-permute-start.12 = (bf16[128,512]{1,0:T(8,128)(2,1)S(1)}, bf16[128,512]{1,0:T(8,128)(2,1)S(1)}, u32[]{:S(2)}, u32[]{:S(2)}) collective-permute-start(bf16[128,512]{1,0:T(8,128)(2,1)S(1)} %get-tuple-element.44), channel_id=1, source_target_pairs={{0,24},{4,28},{8,16},{12,20},{16,8},{20,12},{24,0},{28,4},{1,25},{... | collective-permute-start | bytes 393224 | tf_op jit(solution)/shard_map/ppermute | solution.py:201
  27.4 5.6 %collective-permute-start.5 = (bf16[128,512]{1,0:T(8,128)(2,1)S(1)}, bf16[128,512]{1,0:T(8,128)(2,1)S(1)}, u32[]{:S(2)}, u32[]{:S(2)}) collective-permute-start(bf16[128,512]{1,0:T(8,128)(2,1)S(1)} %get-tuple-element.35), channel_id=1, source_target_pairs={{0,16},{4,20},{8,24},{12,28},{16,0},{20,4},{24,8},{28,12},{1,17},{... | collective-permute-start | bytes 393224 | tf_op jit(solution)/shard_map/ppermute | solution.py:201
  27.7 5.3 %collective-permute-start.6 = (bf16[128,512]{1,0:T(8,128)(2,1)S(1)}, bf16[128,512]{1,0:T(8,128)(2,1)S(1)}, u32[]{:S(2)}, u32[]{:S(2)}) collective-permute-start(bf16[128,512]{1,0:T(8,128)(2,1)S(1)} %get-tuple-element.36), channel_id=1, source_target_pairs={{0,24},{4,28},{8,16},{12,20},{16,8},{20,12},{24,0},{28,4},{1,25},{... | collective-permute-start | bytes 393224 | tf_op jit(solution)/shard_map/ppermute | solution.py:201
  30.1 5.3 %collective-permute-start.4 = (bf16[128,512]{1,0:T(8,128)(2,1)S(1)}, bf16[128,512]{1,0:T(8,128)(2,1)S(1)}, u32[]{:S(2)}, u32[]{:S(2)}) collective-permute-start(bf16[128,512]{1,0:T(8,128)(2,1)S(1)} %shard_map.41), channel_id=1, source_target_pairs={{0,8},{4,12},{8,0},{12,4},{16,24},{20,28},{24,16},{28,20},{1,9},{5... | collective-permute-start | bytes 393224 | tf_op jit(solution)/shard_map/ppermute | solution.py:201
  30.4 7.2 %collective-permute-start.13 = (bf16[256,512]{1,0:T(8,128)(2,1)S(1)}, bf16[256,512]{1,0:T(8,128)(2,1)S(1)}, u32[]{:S(2)}, u32[]{:S(2)}) collective-permute-start(bf16[256,512]{1,0:T(8,128)(2,1)S(1)} %shard_map.45), channel_id=1, source_target_pairs={{0,4},{4,0},{8,12},{12,8},{16,20},{20,16},{24,28},{28,24},{1,5},{5... | collective-permute-start | bytes 786440 | tf_op jit(solution)/shard_map/ppermute | solution.py:201
  35.4 3.4 %collective-permute-start.7 = (bf16[256,512]{1,0:T(8,128)(2,1)S(1)}, bf16[256,512]{1,0:T(8,128)(2,1)S(1)}, u32[]{:S(2)}, u32[]{:S(2)}) collective-permute-start(bf16[256,512]{1,0:T(8,128)(2,1)S(1)} %shard_map.42), channel_id=1, source_target_pairs={{0,4},{4,0},{8,12},{12,8},{16,20},{20,16},{24,28},{28,24},{1,5},{5... | collective-permute-start | bytes 786440 | tf_op jit(solution)/shard_map/ppermute | solution.py:201

commit v4 on v3

--- a/solution.py
+++ b/solution.py
@@ -151,30 +151,56 @@
         out[...] = dot(form_ref[rows * slot : rows * (slot + 1)], joined, 1, 0).astype(BF16)
 
 
-def pass_kernel(*refs):
+def pass_kernel(count, *refs):
     size = refs[0].shape[0] // 2
-    for slot, ref in enumerate(refs[:-1]):
+    for slot, ref in enumerate(refs[:count]):
         refs[-1][slot * size : (slot + 1) * size] = ref[size:]
 
 
-def third_kernel(n_in, lo, form_ref, *refs):
-    ins, (out_ref, held, sem) = refs[:n_in], refs[-3:]
+def form_rows(form_ref, size, places):
+    return jnp.concatenate([form_ref[size * k : size * (k + 1)] for k in places], axis=0)
+
+
+def third_part_kernel(places, size, form_ref, *refs):
+    joined = jnp.concatenate([ref[:size] for ref in refs[:-1]], axis=0)
+    refs[-1][...] = dot(joined, form_rows(form_ref, size, places), 0, 0)
+
+
+def third_block_kernel(n_in, form_ref, *refs):
+    ins, out_ref = refs[:n_in], refs[-1]
     if n_in > 1:
         size = ins[0].shape[0] // 2
         ins = sum(
             [[ref.at[:size], ins[-1].at[slot * size : (slot + 1) * size]] for slot, ref in enumerate(ins[:-1])], []
         )
-    joined, form = gathered(ins), form_ref[...]
-    width, rows = form.shape[1] // 2, held.shape[1]
+    result = dot(gathered(ins), form_ref[...], 0, 0).astype(BF16)
+    width = out_ref.shape[2]
+    for c in range(2):
+        out_ref[c] = result[:, c * width : (c + 1) * width]
+
+
+def closing_kernel(n_done, places, form_ref, *refs):
+    done, ins, (out_ref, held, sem) = refs[:n_done], refs[n_done:-3], refs[-3:]
+    width, rows = held.shape[2], held.shape[1]
+    copies, lo = [], 0
+
+    def write(source, lo, rows):
+        copies.append(pltpu.make_async_copy(source, out_ref.at[:, 0, 0, pl.ds(lo, rows)], sem.at[len(copies)]))
+        copies[-1].start()
+
+    for ref in done:
+        write(ref, lo, ref.shape[1])
+        lo += ref.shape[1]
+    joined, form = ins[-1][...], form_ref[...]
+    if places:
+        form = form_rows(form_ref, joined.shape[0] // len(places), places)
     cut = rows // WRITE_CUT
-    copies = []
-    for n in range(WRITE_CUT):
-        result = dot(joined[:, n * cut : (n + 1) * cut], form, 0, 0).astype(BF16)
+    for at in range(0, rows, cut):
+        result = dot(joined[:, at : at + cut], form, 0, 0)
+        result = (result + ins[0][at : at + cut] if places else result).astype(BF16)
         for c in range(2):
-            held[c, n * cut : (n + 1) * cut] = result[:, c * width : (c + 1) * width]
-            there = out_ref.at[c, 0, 0, pl.ds(lo + n * cut, cut)]
-            copies.append(pltpu.make_async_copy(held.at[c, pl.ds(n * cut, cut)], there, sem.at[2 * n + c]))
-            copies[-1].start()
+            held[c, at : at + cut] = result[:, c * width : (c + 1) * width]
+        write(held.at[:, pl.ds(at, cut)], lo + at, cut)
     for copy in copies:
         copy.wait()
 
@@ -279,30 +305,47 @@
         return dict(zip(slots, made))
 
     def outer_exchange(n):
-        cost = LONG if n == last else FREE
         if not rel2:
-            return [whole_exchange(second(n, (0,), full, cost)[0], "grp", outer)]
+            return [whole_exchange(second(n, (0,), full, LONG if n == last else FREE)[0], "grp", outer)]
         slots = tuple(range(pairs))
-        early = slots[:1] + slots[2:] if n == last else slots
-        made = second(n, early, full // pairs, cost)
-        if n == last:
-            made.update(second(n, slots[1:2], full // pairs, FREE))
+        made = second(n, slots, full // pairs, FREE)
         came = [made[0]] + [swap(made[q], "grp", outer, 2 * q) for q in slots[1:]]
-        passed = call(pass_kernel, [VM] * pairs, shape(full // 2, sizes[n]), VM)(*came)
+        passed = call(functools.partial(pass_kernel, pairs), [VM] * pairs, shape(full // 2, sizes[n]), VM)(*came)
         return came + [swap(passed, "grp", outer, 1)]
 
-    out = ()
-    for n, rows in enumerate(sizes):
+    def last_exchange(done):
+        slots = (0,) + tuple(range(2, pairs))
+        made = second(last, slots, full // pairs, LONG)
+        came = {q: swap(made[q], "grp", outer, 2 * q) if q else made[q] for q in slots}
+        direct = second(last, (2, 3), full // outer, FREE)
+        direct = {k: swap(direct[k], "grp", outer, k) for k in direct}
+        passed = call(
+            functools.partial(pass_kernel, len(slots)),
+            [VM] * len(slots), shape(len(slots) * full // outer, sizes[last]), VM,
+        )(*[came[q] for q in slots])
+        passed = swap(passed, "grp", outer, 1)
+        ins = {2 * q: came[q] for q in slots} | direct
+        total = call(
+            functools.partial(third_part_kernel, tuple(ins), full // outer),
+            [VM] * (1 + len(ins)), jax.ShapeDtypeStruct((sizes[last], full), F32), VM, LONG,
+        )(form2, *ins.values())
+        return [total, passed], tuple(2 * q + 1 for q in slots)
+
+    done = []
+    for n, rows in enumerate(sizes[:-1]):
         ins = outer_exchange(n)
-        out = (
+        done.append(
             call(
-                functools.partial(third_kernel, len(ins), starts[n]),
-                [VM] * (1 + len(ins)) + [ANY] * len(out), shape(*stem.shape), ANY, FREE,
-                [pltpu.VMEM((2, rows, width), BF16), pltpu.SemaphoreType.DMA((2 * WRITE_CUT,))],
-                {1 + len(ins): 0} if out else {},
-            )(form2, *ins, *out),
+                functools.partial(third_block_kernel, len(ins)),
+                [VM] * (1 + len(ins)), shape(2, rows, width), VM,
+            )(form2, *ins)
         )
-    return out[0]
+    ins, places = last_exchange(done) if rel2 else (outer_exchange(last), ())
+    return call(
+        functools.partial(closing_kernel, last, places),
+        [VM] * (1 + last + len(ins)), shape(*stem.shape), ANY, FREE,
+        [pltpu.VMEM((2, sizes[-1], width), BF16), pltpu.SemaphoreType.DMA((last + WRITE_CUT,))],
+    )(form2, *done, *ins)
 
 
 def solution(mesh):

time: 40.2 us -> 39.1 us (0.973)
  the two profiles are of different devices: /device:TPU:21 before, /device:TPU:0 now
where the time goes in v4:
time: 39.1 us; the launch traced here: 38.5 us
  starting transfers between devices  20.7 us (53%)
  waiting for transfers between devices  9.85 us (25%)
  Pallas kernels  7.89 us (20%)
    ppermute x15, starting transfers between devices, swap(): return lax.ppermute(piece, axis, [(i, i ^ k) for i in range(count)])  20.7 us
    ppermute x15, waiting for transfers between devices, swap(): return lax.ppermute(piece, axis, [(i, i ^ k) for i in range(count)])  9.85 us
    pallas_call x1, Pallas kernels, local(): call(functools.partial(forms_kernel, sizes, part1, rel1, part2, rel2), [H...  2.31 us
    pallas_call x1, Pallas kernels, local(): call(functools.partial(opening_kernel, part1, rel1, opening), [HBM] * 3,...  1.57 us
    pallas_call x3, Pallas kernels, second(): call(functools.partial(second_kernel, len(ins), slots), [VM] * (1 + len(i...  1.11 us
    pallas_call x1, Pallas kernels, local(): call(functools.partial(closing_kernel, last, places), [VM] * (1 + last +...  1.08 us
    pallas_call x2, Pallas kernels, first_pieces(): call(functools.partial(first_kernel, part1, rel1, owners, len(shapes)), [...  0.86 us
  transfers between devices with their start and end apart: 15, of which 4 were waited for; matrix products, arithmetic and copies ran while one was open for 0% of the time, Pallas kernels for 14%

profile of v4, /device:TPU:0, one launch (start us, length us, event | category | flops | bytes accessed | tf_op | source)
XLA Modules:
  0.0 38.5 jit_solution(12655901610928358793)
XLA Ops:
  0.0 1.6 %shard_map.38 = (bf16[512,512]{1,0:T(8,128)(2,1)S(1)}, bf16[2,512,256]{2,1,0:T(8,128)(2,1)S(1)}, bf16[128,512]{1,0:T(8,128)(2,1)S(1)}) custom-call(bf16[2,1,1,1024,256]{4,3,2,1,0:T(8,128)(2,1)} %stem_ref.3, bf16[3,2,256,256]{3,2,1,0:T(8,128)(2,1)} %branches_ref.3, s32[3,256]{1,0:T(4,128)} %order_ref.3), custom_call_target="tpu_custom_call" | custom-call | flops 1 | bytes 1 | tf_op jit(solution)/shard_map/pallas_call | solution.py:279
  1.6 4.1 %collective-permute-start.1 = (bf16[128,512]{1,0:T(8,128)(2,1)S(1)}, bf16[128,512]{1,0:T(8,128)(2,1)S(1)}, u32[]{:S(2)}, u32[]{:S(2)}) collective-permute-start(bf16[128,512]{1,0:T(8,128)(2,1)S(1)} %get-tuple-element.33), channel_id=1, source_target_pairs={{0,2},{1,3},{2,0},{3,1},{4,6},{5,7},{6,4},{7,5},{8,10},{9,11},{10,... | collective-permute-start | bytes 393224 | tf_op jit(solution)/shard_map/ppermute | solution.py:227
  5.7 0.4 %shard_map.39 = (bf16[128,512]{1,0:T(8,128)(2,1)S(1)}, bf16[128,512]{1,0:T(8,128)(2,1)S(1)}, bf16[128,512]{1,0:T(8,128)(2,1)S(1)}) custom-call(bf16[2,512,256]{2,1,0:T(8,128)(2,1)S(1)} %get-tuple-element.29.block_ref, bf16[512,512]{1,0:T(8,128)(2,1)S(1)} %get-tuple-element.30.form_ref), custom_call_target="tpu_custom_call" | custom-call | flops 1 | bytes 1 | tf_op jit(solution)/shard_map/pallas_call | solution.py:265
  6.1 1.7 %collective-permute-start = (bf16[128,512]{1,0:T(8,128)(2,1)S(1)}, bf16[128,512]{1,0:T(8,128)(2,1)S(1)}, u32[]{:S(2)}, u32[]{:S(2)}) collective-permute-start(bf16[128,512]{1,0:T(8,128)(2,1)S(1)} %get-tuple-element.32), channel_id=1, source_target_pairs={{0,1},{1,0},{2,3},{3,2},{4,5},{5,4},{6,7},{7,6},{8,9},{9,8},{10,11... | collective-permute-start | bytes 393224 | tf_op jit(solution)/shard_map/ppermute | solution.py:227
  7.7 0.0 collective-permute-start.2
  7.7 2.3 %shard_map.37 = (bf16[512,512]{1,0:T(8,128)(2,1)S(1)}, bf16[512,512]{1,0:T(8,128)(2,1)S(1)}, bf16[2,512,256]{2,1,0:T(8,128)(2,1)S(1)}) custom-call(bf16[2,1,1,1024,256]{4,3,2,1,0:T(8,128)(2,1)} %stem_ref.3, bf16[3,2,256,256]{3,2,1,0:T(8,128)(2,1)} %branches_ref.3, s32[3,256]{1,0:T(4,128)} %order_ref.3), custom_call_target="tpu_custom_call" | custom-call | flops 1 | bytes 1 | tf_op jit(solution)/shard_map/pallas_call | solution.py:288
  10.1 3.6 %collective-permute-done.1.refs_2_.rest_1_ = bf16[128,512]{1,0:T(8,128)(2,1)S(1)} collective-permute-done((bf16[128,512]{1,0:T(8,128)(2,1)S(1)}, bf16[128,512]{1,0:T(8,128)(2,1)S(1)}, u32[]{:S(2)}, u32[]{:S(2)}) %collective-permute-start.1) | collective-permute-done | bytes 131104 | tf_op jit(solution)/shard_map/ppermute | solution.py:227
  13.6 0.5 %shard_map.43 = (bf16[128,512]{1,0:T(8,128)(2,1)S(1)}, bf16[128,512]{1,0:T(8,128)(2,1)S(1)}, bf16[128,512]{1,0:T(8,128)(2,1)S(1)}, bf16[128,512]{1,0:T(8,128)(2,1)S(1)}) custom-call(bf16[2,512,256]{2,1,0:T(8,128)(2,1)S(1)} %get-tuple-element.39.block_ref, bf16[512,512]{1,0:T(8,128)(2,1)S(1)} %get-tuple-element.30.form_ref, ...), custom_call_target="tpu_custom_call" | custom-call | flops 1 | bytes 1 | tf_op jit(solution)/shard_map/pallas_call | solution.py:265
  14.1 0.1 collective-permute-start.7
  14.2 3.6 %collective-permute-start.8 = (bf16[128,512]{1,0:T(8,128)(2,1)S(1)}, bf16[128,512]{1,0:T(8,128)(2,1)S(1)}, u32[]{:S(2)}, u32[]{:S(2)}) collective-permute-start(bf16[128,512]{1,0:T(8,128)(2,1)S(1)} %get-tuple-element.42), channel_id=1, source_target_pairs={{0,2},{1,3},{2,0},{3,1},{4,6},{5,7},{6,4},{7,5},{8,10},{9,11},{10,... | collective-permute-start | bytes 393224 | tf_op jit(solution)/shard_map/ppermute | solution.py:227
  17.8 0.8 %collective-permute-start.9 = (bf16[128,512]{1,0:T(8,128)(2,1)S(1)}, bf16[128,512]{1,0:T(8,128)(2,1)S(1)}, u32[]{:S(2)}, u32[]{:S(2)}) collective-permute-start(bf16[128,512]{1,0:T(8,128)(2,1)S(1)} %get-tuple-element.43), channel_id=1, source_target_pairs={{0,3},{1,2},{2,1},{3,0},{4,7},{5,6},{6,5},{7,4},{8,11},{9,10},{10,... | collective-permute-start | bytes 393224 | tf_op jit(solution)/shard_map/ppermute | solution.py:227
  18.6 0.0 collective-permute-done.refs_1_
  18.6 0.0 collective-permute-done.2.refs_3_
  18.6 0.4 %shard_map.40 = (bf16[128,512]{1,0:T(8,128)(2,1)S(1)}, bf16[128,512]{1,0:T(8,128)(2,1)S(1)}, bf16[128,512]{1,0:T(8,128)(2,1)S(1)}, bf16[128,512]{1,0:T(8,128)(2,1)S(1)}) custom-call(bf16[512,512]{1,0:T(8,128)(2,1)S(1)} %get-tuple-element.28.form_ref.rest_0_, bf16[128,512]{1,0:T(8,128)(2,1)S(1)} %get-tuple-element.31.refs_0_, ...), custom_call_target="tpu_custom_call" | custom-call | flops 1 | bytes 1 | tf_op jit(solution)/shard_map/pallas_call | solution.py:302
  19.0 2.2 %collective-permute-start.3 = (bf16[128,512]{1,0:T(8,128)(2,1)S(1)}, bf16[128,512]{1,0:T(8,128)(2,1)S(1)}, u32[]{:S(2)}, u32[]{:S(2)}) collective-permute-start(bf16[128,512]{1,0:T(8,128)(2,1)S(1)} %get-tuple-element.36), channel_id=1, source_target_pairs={{0,8},{4,12},{8,0},{12,4},{16,24},{20,28},{24,16},{28,20},{1,9},{5... | collective-permute-start | bytes 393224 | tf_op jit(solution)/shard_map/ppermute | solution.py:227
  21.2 1.5 %collective-permute-start.4 = (bf16[128,512]{1,0:T(8,128)(2,1)S(1)}, bf16[128,512]{1,0:T(8,128)(2,1)S(1)}, u32[]{:S(2)}, u32[]{:S(2)}) collective-permute-start(bf16[128,512]{1,0:T(8,128)(2,1)S(1)} %get-tuple-element.37), channel_id=1, source_target_pairs={{0,16},{4,20},{8,24},{12,28},{16,0},{20,4},{24,8},{28,12},{1,17},{... | collective-permute-start | bytes 393224 | tf_op jit(solution)/shard_map/ppermute | solution.py:227
  22.7 0.0 collective-permute-done.7.refs_1_
  22.7 1.4 %collective-permute-start.5 = (bf16[128,512]{1,0:T(8,128)(2,1)S(1)}, bf16[128,512]{1,0:T(8,128)(2,1)S(1)}, u32[]{:S(2)}, u32[]{:S(2)}) collective-permute-start(bf16[128,512]{1,0:T(8,128)(2,1)S(1)} %get-tuple-element.38), channel_id=1, source_target_pairs={{0,24},{4,28},{8,16},{12,20},{16,8},{20,12},{24,0},{28,4},{1,25},{... | collective-permute-start | bytes 393224 | tf_op jit(solution)/shard_map/ppermute | solution.py:227
  24.1 3.7 %collective-permute-done.8.refs_2_ = bf16[128,512]{1,0:T(8,128)(2,1)S(1)} collective-permute-done((bf16[128,512]{1,0:T(8,128)(2,1)S(1)}, bf16[128,512]{1,0:T(8,128)(2,1)S(1)}, u32[]{:S(2)}, u32[]{:S(2)}) %collective-permute-start.8) | collective-permute-done | bytes 131104 | tf_op jit(solution)/shard_map/ppermute | solution.py:227
  27.8 0.0 collective-permute-done.9.refs_3_
  27.8 0.4 shard_map.44
  28.2 1.6 %collective-permute-start.10 = (bf16[128,512]{1,0:T(8,128)(2,1)S(1)}, bf16[128,512]{1,0:T(8,128)(2,1)S(1)}, u32[]{:S(2)}, u32[]{:S(2)}) collective-permute-start(bf16[128,512]{1,0:T(8,128)(2,1)S(1)} %get-tuple-element.45), channel_id=1, source_target_pairs={{0,16},{4,20},{8,24},{12,28},{16,0},{20,4},{24,8},{28,12},{1,17},{... | collective-permute-start | bytes 393224 | tf_op jit(solution)/shard_map/ppermute | solution.py:227
  29.8 1.4 %collective-permute-start.11 = (bf16[128,512]{1,0:T(8,128)(2,1)S(1)}, bf16[128,512]{1,0:T(8,128)(2,1)S(1)}, u32[]{:S(2)}, u32[]{:S(2)}) collective-permute-start(bf16[128,512]{1,0:T(8,128)(2,1)S(1)} %get-tuple-element.46), channel_id=1, source_target_pairs={{0,24},{4,28},{8,16},{12,20},{16,8},{20,12},{24,0},{28,4},{1,25},{... | collective-permute-start | bytes 393224 | tf_op jit(solution)/shard_map/ppermute | solution.py:227
  31.2 0.3 shard_map.45
  31.5 0.0 collective-permute-done.3.refs_1_
  31.5 0.6 %collective-permute-start.12 = (bf16[64,512]{1,0:T(8,128)(2,1)S(1)}, bf16[64,512]{1,0:T(8,128)(2,1)S(1)}, u32[]{:S(2)}, u32[]{:S(2)}) collective-permute-start(bf16[64,512]{1,0:T(8,128)(2,1)S(1)} %get-tuple-element.47), channel_id=1, source_target_pairs={{0,8},{4,12},{8,0},{12,4},{16,24},{20,28},{24,16},{28,20},{1,9},{5... | collective-permute-start | bytes 196616 | tf_op jit(solution)/shard_map/ppermute | solution.py:227
  32.1 0.0 collective-permute-done.4.refs_2_
  32.1 0.0 collective-permute-start.13
  32.1 0.0 collective-permute-done.5.refs_3_
  32.1 1.7 %collective-permute-start.6 = (bf16[256,512]{1,0:T(8,128)(2,1)S(1)}, bf16[256,512]{1,0:T(8,128)(2,1)S(1)}, u32[]{:S(2)}, u32[]{:S(2)}) collective-permute-start(bf16[256,512]{1,0:T(8,128)(2,1)S(1)} %shard_map.41), channel_id=1, source_target_pairs={{0,4},{4,0},{8,12},{12,8},{16,20},{20,16},{24,28},{28,24},{1,5},{5... | collective-permute-start | bytes 786440 | tf_op jit(solution)/shard_map/ppermute | solution.py:227
  33.8 0.0 collective-permute-done.10.refs_1_
  33.8 1.8 %collective-permute-done.11.refs_2_ = bf16[128,512]{1,0:T(8,128)(2,1)S(1)} collective-permute-done((bf16[128,512]{1,0:T(8,128)(2,1)S(1)}, bf16[128,512]{1,0:T(8,128)(2,1)S(1)}, u32[]{:S(2)}, u32[]{:S(2)}) %collective-permute-start.11) | collective-permute-done | bytes 131104 | tf_op jit(solution)/shard_map/ppermute | solution.py:227
  35.7 0.1 collective-permute-start.14
  35.7 0.7 %collective-permute-done.12.refs_3_ = bf16[64,512]{1,0:T(8,128)(2,1)S(1)} collective-permute-done((bf16[64,512]{1,0:T(8,128)(2,1)S(1)}, bf16[64,512]{1,0:T(8,128)(2,1)S(1)}, u32[]{:S(2)}, u32[]{:S(2)}) %collective-permute-start.12) | collective-permute-done | bytes 65568 | tf_op jit(solution)/shard_map/ppermute | solution.py:227
  36.5 0.0 collective-permute-done.13.refs_4_
  36.5 0.5 %shard_map.46.refs_1_ = f32[512,512]{1,0:T(8,128)S(1)} custom-call(bf16[512,512]{1,0:T(8,128)(2,1)S(1)} %get-tuple-element.27.form_ref, bf16[128,512]{1,0:T(8,128)(2,1)S(1)} %get-tuple-element.44.refs_0_, bf16[128,512]{1,0:T(8,128)(2,1)S(1)} %collective-permute-done.10.refs_1_, bf16[128,512]{1,0:T(8,128)(2,1)S(1)} %collective-permute-done.11.refs_2_, ...), custom_call_target="tpu_custom_call" | custom-call | flops 99999997952 | bytes 100000000 | tf_op jit(solution)/shard_map/pallas_call | solution.py:328
  37.0 0.0 collective-permute-done.6.refs_4_
  37.0 0.5 %shard_map.42.refs_0_ = bf16[2,512,256]{2,1,0:T(8,128)(2,1)S(1)} custom-call(bf16[512,512]{1,0:T(8,128)(2,1)S(1)} %get-tuple-element.27.form_ref, bf16[128,512]{1,0:T(8,128)(2,1)S(1)} %get-tuple-element.35.refs_0_, bf16[128,512]{1,0:T(8,128)(2,1)S(1)} %collective-permute-done.3.refs_1_, bf16[128,512]{1,0:T(8,128)(2,1)S(1)} %collective-permute-done.4.refs_2_, ...), custom_call_target="tpu_custom_call" | custom-call | flops 1 | bytes 1 | tf_op jit(solution)/shard_map/pallas_call | solution.py:338
  37.4 0.0 collective-permute-done.14.refs_2_
  37.4 1.1 %shard_map.48 = bf16[2,1,1,1024,256]{4,3,2,1,0:T(8,128)(2,1)} custom-call(bf16[512,512]{1,0:T(8,128)(2,1)S(1)} %get-tuple-element.27.form_ref, bf16[2,512,256]{2,1,0:T(8,128)(2,1)S(1)} %shard_map.42.refs_0_, f32[512,512]{1,0:T(8,128)S(1)} %shard_map.46.refs_1_, bf16[192,512]{1,0:T(8,128)(2,1)S(1)} %collective-permute-done.14.refs_2_), custom_call_target="tpu_custom_call" | custom-call | flops 1 | bytes 1 | tf_op jit(solution)/shard_map/pallas_call | solution.py:344
  (2 shorter events, 0.0 us)
Async XLA Ops:
  1.6 12.1 %collective-permute-start.1 = (bf16[128,512]{1,0:T(8,128)(2,1)S(1)}, bf16[128,512]{1,0:T(8,128)(2,1)S(1)}, u32[]{:S(2)}, u32[]{:S(2)}) collective-permute-start(bf16[128,512]{1,0:T(8,128)(2,1)S(1)} %get-tuple-element.33), channel_id=1, source_target_pairs={{0,2},{1,3},{2,0},{3,1},{4,6},{5,7},{6,4},{7,5},{8,10},{9,11},{10,... | collective-permute-start | bytes 393224 | tf_op jit(solution)/shard_map/ppermute | solution.py:227
  6.1 12.5 %collective-permute-start = (bf16[128,512]{1,0:T(8,128)(2,1)S(1)}, bf16[128,512]{1,0:T(8,128)(2,1)S(1)}, u32[]{:S(2)}, u32[]{:S(2)}) collective-permute-start(bf16[128,512]{1,0:T(8,128)(2,1)S(1)} %get-tuple-element.32), channel_id=1, source_target_pairs={{0,1},{1,0},{2,3},{3,2},{4,5},{5,4},{6,7},{7,6},{8,9},{9,8},{10,11... | collective-permute-start | bytes 393224 | tf_op jit(solution)/shard_map/ppermute | solution.py:227
  7.7 10.9 %collective-permute-start.2 = (bf16[128,512]{1,0:T(8,128)(2,1)S(1)}, bf16[128,512]{1,0:T(8,128)(2,1)S(1)}, u32[]{:S(2)}, u32[]{:S(2)}) collective-permute-start(bf16[128,512]{1,0:T(8,128)(2,1)S(1)} %get-tuple-element.34), channel_id=1, source_target_pairs={{0,3},{1,2},{2,1},{3,0},{4,7},{5,6},{6,5},{7,4},{8,11},{9,10},{10,... | collective-permute-start | bytes 393224 | tf_op jit(solution)/shard_map/ppermute | solution.py:227
  14.1 8.6 %collective-permute-start.7 = (bf16[128,512]{1,0:T(8,128)(2,1)S(1)}, bf16[128,512]{1,0:T(8,128)(2,1)S(1)}, u32[]{:S(2)}, u32[]{:S(2)}) collective-permute-start(bf16[128,512]{1,0:T(8,128)(2,1)S(1)} %get-tuple-element.41), channel_id=1, source_target_pairs={{0,1},{1,0},{2,3},{3,2},{4,5},{5,4},{6,7},{7,6},{8,9},{9,8},{10,11... | collective-permute-start | bytes 393224 | tf_op jit(solution)/shard_map/ppermute | solution.py:227
  14.2 13.6 %collective-permute-start.8 = (bf16[128,512]{1,0:T(8,128)(2,1)S(1)}, bf16[128,512]{1,0:T(8,128)(2,1)S(1)}, u32[]{:S(2)}, u32[]{:S(2)}) collective-permute-start(bf16[128,512]{1,0:T(8,128)(2,1)S(1)} %get-tuple-element.42), channel_id=1, source_target_pairs={{0,2},{1,3},{2,0},{3,1},{4,6},{5,7},{6,4},{7,5},{8,10},{9,11},{10,... | collective-permute-start | bytes 393224 | tf_op jit(solution)/shard_map/ppermute | solution.py:227
  17.8 10.0 %collective-permute-start.9 = (bf16[128,512]{1,0:T(8,128)(2,1)S(1)}, bf16[128,512]{1,0:T(8,128)(2,1)S(1)}, u32[]{:S(2)}, u32[]{:S(2)}) collective-permute-start(bf16[128,512]{1,0:T(8,128)(2,1)S(1)} %get-tuple-element.43), channel_id=1, source_target_pairs={{0,3},{1,2},{2,1},{3,0},{4,7},{5,6},{6,5},{7,4},{8,11},{9,10},{10,... | collective-permute-start | bytes 393224 | tf_op jit(solution)/shard_map/ppermute | solution.py:227
  19.0 12.5 %collective-permute-start.3 = (bf16[128,512]{1,0:T(8,128)(2,1)S(1)}, bf16[128,512]{1,0:T(8,128)(2,1)S(1)}, u32[]{:S(2)}, u32[]{:S(2)}) collective-permute-start(bf16[128,512]{1,0:T(8,128)(2,1)S(1)} %get-tuple-element.36), channel_id=1, source_target_pairs={{0,8},{4,12},{8,0},{12,4},{16,24},{20,28},{24,16},{28,20},{1,9},{5... | collective-permute-start | bytes 393224 | tf_op jit(solution)/shard_map/ppermute | solution.py:227
  21.2 10.9 %collective-permute-start.4 = (bf16[128,512]{1,0:T(8,128)(2,1)S(1)}, bf16[128,512]{1,0:T(8,128)(2,1)S(1)}, u32[]{:S(2)}, u32[]{:S(2)}) collective-permute-start(bf16[128,512]{1,0:T(8,128)(2,1)S(1)} %get-tuple-element.37), channel_id=1, source_target_pairs={{0,16},{4,20},{8,24},{12,28},{16,0},{20,4},{24,8},{28,12},{1,17},{... | collective-permute-start | bytes 393224 | tf_op jit(solution)/shard_map/ppermute | solution.py:227
  22.7 9.4 %collective-permute-start.5 = (bf16[128,512]{1,0:T(8,128)(2,1)S(1)}, bf16[128,512]{1,0:T(8,128)(2,1)S(1)}, u32[]{:S(2)}, u32[]{:S(2)}) collective-permute-start(bf16[128,512]{1,0:T(8,128)(2,1)S(1)} %get-tuple-element.38), channel_id=1, source_target_pairs={{0,24},{4,28},{8,16},{12,20},{16,8},{20,12},{24,0},{28,4},{1,25},{... | collective-permute-start | bytes 393224 | tf_op jit(solution)/shard_map/ppermute | solution.py:227
  28.2 5.7 %collective-permute-start.10 = (bf16[128,512]{1,0:T(8,128)(2,1)S(1)}, bf16[128,512]{1,0:T(8,128)(2,1)S(1)}, u32[]{:S(2)}, u32[]{:S(2)}) collective-permute-start(bf16[128,512]{1,0:T(8,128)(2,1)S(1)} %get-tuple-element.45), channel_id=1, source_target_pairs={{0,16},{4,20},{8,24},{12,28},{16,0},{20,4},{24,8},{28,12},{1,17},{... | collective-permute-start | bytes 393224 | tf_op jit(solution)/shard_map/ppermute | solution.py:227
  29.8 5.9 %collective-permute-start.11 = (bf16[128,512]{1,0:T(8,128)(2,1)S(1)}, bf16[128,512]{1,0:T(8,128)(2,1)S(1)}, u32[]{:S(2)}, u32[]{:S(2)}) collective-permute-start(bf16[128,512]{1,0:T(8,128)(2,1)S(1)} %get-tuple-element.46), channel_id=1, source_target_pairs={{0,24},{4,28},{8,16},{12,20},{16,8},{20,12},{24,0},{28,4},{1,25},{... | collective-permute-start | bytes 393224 | tf_op jit(solution)/shard_map/ppermute | solution.py:227
  31.5 5.0 %collective-permute-start.12 = (bf16[64,512]{1,0:T(8,128)(2,1)S(1)}, bf16[64,512]{1,0:T(8,128)(2,1)S(1)}, u32[]{:S(2)}, u32[]{:S(2)}) collective-permute-start(bf16[64,512]{1,0:T(8,128)(2,1)S(1)} %get-tuple-element.47), channel_id=1, source_target_pairs={{0,8},{4,12},{8,0},{12,4},{16,24},{20,28},{24,16},{28,20},{1,9},{5... | collective-permute-start | bytes 196616 | tf_op jit(solution)/shard_map/ppermute | solution.py:227
  32.1 4.4 %collective-permute-start.13 = (bf16[64,512]{1,0:T(8,128)(2,1)S(1)}, bf16[64,512]{1,0:T(8,128)(2,1)S(1)}, u32[]{:S(2)}, u32[]{:S(2)}) collective-permute-start(bf16[64,512]{1,0:T(8,128)(2,1)S(1)} %get-tuple-element.48), channel_id=1, source_target_pairs={{0,12},{4,8},{8,4},{12,0},{16,28},{20,24},{24,20},{28,16},{1,13},{... | collective-permute-start | bytes 196616 | tf_op jit(solution)/shard_map/ppermute | solution.py:227
  32.1 4.8 %collective-permute-start.6 = (bf16[256,512]{1,0:T(8,128)(2,1)S(1)}, bf16[256,512]{1,0:T(8,128)(2,1)S(1)}, u32[]{:S(2)}, u32[]{:S(2)}) collective-permute-start(bf16[256,512]{1,0:T(8,128)(2,1)S(1)} %shard_map.41), channel_id=1, source_target_pairs={{0,4},{4,0},{8,12},{12,8},{16,20},{20,16},{24,28},{28,24},{1,5},{5... | collective-permute-start | bytes 786440 | tf_op jit(solution)/shard_map/ppermute | solution.py:227
  35.7 1.8 %collective-permute-start.14 = (bf16[192,512]{1,0:T(8,128)(2,1)S(1)}, bf16[192,512]{1,0:T(8,128)(2,1)S(1)}, u32[]{:S(2)}, u32[]{:S(2)}) collective-permute-start(bf16[192,512]{1,0:T(8,128)(2,1)S(1)} %shard_map.47), channel_id=1, source_target_pairs={{0,4},{4,0},{8,12},{12,8},{16,20},{20,16},{24,28},{28,24},{1,5},{5... | collective-permute-start | bytes 589832 | tf_op jit(solution)/shard_map/ppermute | solution.py:227

commit v5 on v4

--- a/solution.py
+++ b/solution.py
@@ -162,19 +162,25 @@
 
 
 def third_part_kernel(places, size, form_ref, *refs):
-    joined = jnp.concatenate([ref[:size] for ref in refs[:-1]], axis=0)
-    refs[-1][...] = dot(joined, form_rows(form_ref, size, places), 0, 0)
-
-
-def third_block_kernel(n_in, form_ref, *refs):
-    ins, out_ref = refs[:n_in], refs[-1]
-    if n_in > 1:
-        size = ins[0].shape[0] // 2
-        ins = sum(
-            [[ref.at[:size], ins[-1].at[slot * size : (slot + 1) * size]] for slot, ref in enumerate(ins[:-1])], []
-        )
-    result = dot(gathered(ins), form_ref[...], 0, 0).astype(BF16)
+    joined = jnp.concatenate([ref[:size] for ref in refs[: len(places)]], axis=0)
+    total = dot(joined, form_rows(form_ref, size, places), 0, 0)
+    for before in refs[len(places) : -1]:
+        total = total + before[...]
+    refs[-1][...] = total
+
+
+def block_result(places, form_ref, refs, rows):
+    joined, form = refs[-1][:, rows], form_ref[...]
+    if places:
+        form = form_rows(form_ref, joined.shape[0] // len(places), places)
+    result = dot(joined, form, 0, 0)
+    return (result + refs[0][rows] if places else result).astype(BF16)
+
+
+def block_kernel(places, form_ref, *refs):
+    out_ref = refs[-1]
     width = out_ref.shape[2]
+    result = block_result(places, form_ref, refs[:-1], slice(None))
     for c in range(2):
         out_ref[c] = result[:, c * width : (c + 1) * width]
 
@@ -184,20 +190,16 @@
     width, rows = held.shape[2], held.shape[1]
     copies, lo = [], 0
 
-    def write(source, lo, rows):
-        copies.append(pltpu.make_async_copy(source, out_ref.at[:, 0, 0, pl.ds(lo, rows)], sem.at[len(copies)]))
+    def write(source, at, count):
+        copies.append(pltpu.make_async_copy(source, out_ref.at[:, 0, 0, pl.ds(at, count)], sem.at[len(copies)]))
         copies[-1].start()
 
     for ref in done:
         write(ref, lo, ref.shape[1])
         lo += ref.shape[1]
-    joined, form = ins[-1][...], form_ref[...]
-    if places:
-        form = form_rows(form_ref, joined.shape[0] // len(places), places)
     cut = rows // WRITE_CUT
     for at in range(0, rows, cut):
-        result = dot(joined[:, at : at + cut], form, 0, 0)
-        result = (result + ins[0][at : at + cut] if places else result).astype(BF16)
+        result = block_result(places, form_ref, ins, slice(at, at + cut))
         for c in range(2):
             held[c, at : at + cut] = result[:, c * width : (c + 1) * width]
         write(held.at[:, pl.ds(at, cut)], lo + at, cut)
@@ -304,47 +306,51 @@
         )(form1, *ins)
         return dict(zip(slots, made))
 
+    def third_part(n, blocks, cost, *before):
+        return call(
+            functools.partial(third_part_kernel, tuple(blocks), full // outer),
+            [VM] * (1 + len(blocks) + len(before)), jax.ShapeDtypeStruct((sizes[n], full), F32), VM, cost,
+        )(form2, *blocks.values(), *before)
+
+    def pass_on(n, came, after=()):
+        given = call(
+            functools.partial(pass_kernel, len(came)),
+            [VM] * len(came) + [ANY] * len(after), shape(len(came) * full // outer, sizes[n]), VM,
+        )(*came.values(), *after)
+        return swap(given, "grp", outer, 1), tuple(2 * q + 1 for q in came)
+
     def outer_exchange(n):
-        if not rel2:
-            return [whole_exchange(second(n, (0,), full, LONG if n == last else FREE)[0], "grp", outer)]
         slots = tuple(range(pairs))
         made = second(n, slots, full // pairs, FREE)
-        came = [made[0]] + [swap(made[q], "grp", outer, 2 * q) for q in slots[1:]]
-        passed = call(functools.partial(pass_kernel, pairs), [VM] * pairs, shape(full // 2, sizes[n]), VM)(*came)
-        return came + [swap(passed, "grp", outer, 1)]
-
-    def last_exchange(done):
+        came = {q: swap(made[q], "grp", outer, 2 * q) if q else made[q] for q in slots}
+        total = third_part(n, {2 * q: came[q] for q in slots}, FREE)
+        passed, places = pass_on(n, came, (total,))
+        return [total, passed], places
+
+    def last_exchange(n):
         slots = (0,) + tuple(range(2, pairs))
-        made = second(last, slots, full // pairs, LONG)
+        made = second(n, slots[:1], full // pairs, FREE) | second(n, slots[1:], full // pairs, LONG)
         came = {q: swap(made[q], "grp", outer, 2 * q) if q else made[q] for q in slots}
-        direct = second(last, (2, 3), full // outer, FREE)
+        direct = second(n, (2, 3), full // outer, FREE)
         direct = {k: swap(direct[k], "grp", outer, k) for k in direct}
-        passed = call(
-            functools.partial(pass_kernel, len(slots)),
-            [VM] * len(slots), shape(len(slots) * full // outer, sizes[last]), VM,
-        )(*[came[q] for q in slots])
-        passed = swap(passed, "grp", outer, 1)
-        ins = {2 * q: came[q] for q in slots} | direct
-        total = call(
-            functools.partial(third_part_kernel, tuple(ins), full // outer),
-            [VM] * (1 + len(ins)), jax.ShapeDtypeStruct((sizes[last], full), F32), VM, LONG,
-        )(form2, *ins.values())
-        return [total, passed], tuple(2 * q + 1 for q in slots)
+        passed, places = pass_on(n, came)
+        total = third_part(n, {2 * q: came[q] for q in slots}, FREE)
+        return [third_part(n, direct, LONG, total), passed], places
 
     done = []
-    for n, rows in enumerate(sizes[:-1]):
-        ins = outer_exchange(n)
-        done.append(
-            call(
-                functools.partial(third_block_kernel, len(ins)),
-                [VM] * (1 + len(ins)), shape(2, rows, width), VM,
-            )(form2, *ins)
-        )
-    ins, places = last_exchange(done) if rel2 else (outer_exchange(last), ())
+    for n, rows in enumerate(sizes):
+        if not rel2:
+            whole = second(n, (0,), full, LONG if n == last else FREE)[0]
+            ins, places = [whole_exchange(whole, "grp", outer)], ()
+        else:
+            ins, places = last_exchange(n) if n == last else outer_exchange(n)
+        if n < last:
+            kernel = functools.partial(block_kernel, places)
+            done.append(call(kernel, [VM] * (1 + len(ins)), shape(2, rows, width), VM)(form2, *ins))
     return call(
         functools.partial(closing_kernel, last, places),
         [VM] * (1 + last + len(ins)), shape(*stem.shape), ANY, FREE,
-        [pltpu.VMEM((2, sizes[-1], width), BF16), pltpu.SemaphoreType.DMA((last + WRITE_CUT,))],
+        [pltpu.VMEM((2, sizes[last], width), BF16), pltpu.SemaphoreType.DMA((last + WRITE_CUT,))],
     )(form2, *done, *ins)
 
 

time: 39.1 us -> 38.8 us (level)
  waiting for transfers between devices: 9.85 us -> 8.97 us
  Pallas kernels: 7.89 us -> 8.41 us
    ppermute x15, waiting for transfers between devices: 9.85 us -> 8.97 us  [swap(): return lax.ppermute(piece, axis, [(i, i ^ k) for i in range(count)])]
    pallas_call x4 -> x6, Pallas kernels: 0.96 us -> 1.32 us  [the longest x3 0.96 us: third_part(): call(functools.partial(third_part_kernel, tuple(blocks), full // outer),...]
    pallas_call x3 -> x4, Pallas kernels: 1.11 us -> 1.27 us  [second(): call(functools.partial(second_kernel, len(ins), slots), [VM] * (1 + len(i...]
  transfers between devices with their start and end apart: 15 -> 15, of which waited for: 4 -> 4; matrix products, arithmetic and copies ran while one was open for 0% -> 0% of each run, Pallas kernels for 14% -> 15%
where the time goes in v5:
time: 38.8 us; the launch traced here: 38.2 us
  starting transfers between devices  20.7 us (53%)
  waiting for transfers between devices  8.97 us (23%)
  Pallas kernels  8.41 us (22%)
    ppermute x15, starting transfers between devices, swap(): return lax.ppermute(piece, axis, [(i, i ^ k) for i in range(count)])  20.7 us
    ppermute x15, waiting for transfers between devices, swap(): return lax.ppermute(piece, axis, [(i, i ^ k) for i in range(count)])  8.97 us
    pallas_call x1, Pallas kernels, local(): call(functools.partial(forms_kernel, sizes, part1, rel1, part2, rel2), [H...  2.31 us
    pallas_call x1, Pallas kernels, local(): call(functools.partial(opening_kernel, part1, rel1, opening), [HBM] * 3,...  1.57 us
    pallas_call x4, Pallas kernels, second(): call(functools.partial(second_kernel, len(ins), slots), [VM] * (1 + len(i...  1.27 us
    pallas_call x1, Pallas kernels, local(): call(functools.partial(closing_kernel, last, places), [VM] * (1 + last +...  1.08 us
    pallas_call x3, Pallas kernels, third_part(): call(functools.partial(third_part_kernel, tuple(blocks), full // outer),...  0.96 us
    pallas_call x2, Pallas kernels, first_pieces(): call(functools.partial(first_kernel, part1, rel1, owners, len(shapes)), [...  0.86 us
  transfers between devices with their start and end apart: 15, of which 4 were waited for; matrix products, arithmetic and copies ran while one was open for 0% of the time, Pallas kernels for 15%

profile of v5, /device:TPU:0, one launch (start us, length us, event | category | flops | bytes accessed | tf_op | source)
XLA Modules:
  0.0 38.2 jit_solution(13773829677106747648)
XLA Ops:
  0.0 1.6 %shard_map.38 = (bf16[512,512]{1,0:T(8,128)(2,1)S(1)}, bf16[2,512,256]{2,1,0:T(8,128)(2,1)S(1)}, bf16[128,512]{1,0:T(8,128)(2,1)S(1)}) custom-call(bf16[2,1,1,1024,256]{4,3,2,1,0:T(8,128)(2,1)} %stem_ref.3, bf16[3,2,256,256]{3,2,1,0:T(8,128)(2,1)} %branches_ref.3, s32[3,256]{1,0:T(4,128)} %order_ref.3), custom_call_target="tpu_custom_call" | custom-call | flops 1 | bytes 1 | tf_op jit(solution)/shard_map/pallas_call | solution.py:281
  1.6 4.1 %collective-permute-start.1 = (bf16[128,512]{1,0:T(8,128)(2,1)S(1)}, bf16[128,512]{1,0:T(8,128)(2,1)S(1)}, u32[]{:S(2)}, u32[]{:S(2)}) collective-permute-start(bf16[128,512]{1,0:T(8,128)(2,1)S(1)} %get-tuple-element.32), channel_id=1, source_target_pairs={{0,2},{1,3},{2,0},{3,1},{4,6},{5,7},{6,4},{7,5},{8,10},{9,11},{10,... | collective-permute-start | bytes 393224 | tf_op jit(solution)/shard_map/ppermute | solution.py:229
  5.7 0.4 %shard_map.39 = (bf16[128,512]{1,0:T(8,128)(2,1)S(1)}, bf16[128,512]{1,0:T(8,128)(2,1)S(1)}, bf16[128,512]{1,0:T(8,128)(2,1)S(1)}) custom-call(bf16[2,512,256]{2,1,0:T(8,128)(2,1)S(1)} %get-tuple-element.28.block_ref, bf16[512,512]{1,0:T(8,128)(2,1)S(1)} %get-tuple-element.29.form_ref), custom_call_target="tpu_custom_call" | custom-call | flops 1 | bytes 1 | tf_op jit(solution)/shard_map/pallas_call | solution.py:267
  6.1 1.7 %collective-permute-start = (bf16[128,512]{1,0:T(8,128)(2,1)S(1)}, bf16[128,512]{1,0:T(8,128)(2,1)S(1)}, u32[]{:S(2)}, u32[]{:S(2)}) collective-permute-start(bf16[128,512]{1,0:T(8,128)(2,1)S(1)} %get-tuple-element.31), channel_id=1, source_target_pairs={{0,1},{1,0},{2,3},{3,2},{4,5},{5,4},{6,7},{7,6},{8,9},{9,8},{10,11... | collective-permute-start | bytes 393224 | tf_op jit(solution)/shard_map/ppermute | solution.py:229
  7.7 0.0 collective-permute-start.2
  7.7 2.3 %shard_map.37 = (bf16[512,512]{1,0:T(8,128)(2,1)S(1)}, bf16[512,512]{1,0:T(8,128)(2,1)S(1)}, bf16[2,512,256]{2,1,0:T(8,128)(2,1)S(1)}) custom-call(bf16[2,1,1,1024,256]{4,3,2,1,0:T(8,128)(2,1)} %stem_ref.3, bf16[3,2,256,256]{3,2,1,0:T(8,128)(2,1)} %branches_ref.3, s32[3,256]{1,0:T(4,128)} %order_ref.3), custom_call_target="tpu_custom_call" | custom-call | flops 1 | bytes 1 | tf_op jit(solution)/shard_map/pallas_call | solution.py:290
  10.1 3.6 %collective-permute-done.1.refs_2_.rest_1_ = bf16[128,512]{1,0:T(8,128)(2,1)S(1)} collective-permute-done((bf16[128,512]{1,0:T(8,128)(2,1)S(1)}, bf16[128,512]{1,0:T(8,128)(2,1)S(1)}, u32[]{:S(2)}, u32[]{:S(2)}) %collective-permute-start.1) | collective-permute-done | bytes 131104 | tf_op jit(solution)/shard_map/ppermute | solution.py:229
  13.6 0.5 %shard_map.44 = (bf16[128,512]{1,0:T(8,128)(2,1)S(1)}, bf16[128,512]{1,0:T(8,128)(2,1)S(1)}, bf16[128,512]{1,0:T(8,128)(2,1)S(1)}, bf16[128,512]{1,0:T(8,128)(2,1)S(1)}) custom-call(bf16[2,512,256]{2,1,0:T(8,128)(2,1)S(1)} %get-tuple-element.38.block_ref, bf16[512,512]{1,0:T(8,128)(2,1)S(1)} %get-tuple-element.29.form_ref, ...), custom_call_target="tpu_custom_call" | custom-call | flops 1 | bytes 1 | tf_op jit(solution)/shard_map/pallas_call | solution.py:267
  14.1 0.1 collective-permute-start.7
  14.2 3.6 %collective-permute-start.8 = (bf16[128,512]{1,0:T(8,128)(2,1)S(1)}, bf16[128,512]{1,0:T(8,128)(2,1)S(1)}, u32[]{:S(2)}, u32[]{:S(2)}) collective-permute-start(bf16[128,512]{1,0:T(8,128)(2,1)S(1)} %get-tuple-element.41), channel_id=1, source_target_pairs={{0,2},{1,3},{2,0},{3,1},{4,6},{5,7},{6,4},{7,5},{8,10},{9,11},{10,... | collective-permute-start | bytes 393224 | tf_op jit(solution)/shard_map/ppermute | solution.py:229
  17.8 0.8 %collective-permute-start.9 = (bf16[128,512]{1,0:T(8,128)(2,1)S(1)}, bf16[128,512]{1,0:T(8,128)(2,1)S(1)}, u32[]{:S(2)}, u32[]{:S(2)}) collective-permute-start(bf16[128,512]{1,0:T(8,128)(2,1)S(1)} %get-tuple-element.42), channel_id=1, source_target_pairs={{0,3},{1,2},{2,1},{3,0},{4,7},{5,6},{6,5},{7,4},{8,11},{9,10},{10,... | collective-permute-start | bytes 393224 | tf_op jit(solution)/shard_map/ppermute | solution.py:229
  18.6 0.0 collective-permute-done.refs_1_
  18.6 0.0 collective-permute-done.2.refs_3_
  18.6 0.4 %shard_map.40 = (bf16[128,512]{1,0:T(8,128)(2,1)S(1)}, bf16[128,512]{1,0:T(8,128)(2,1)S(1)}, bf16[128,512]{1,0:T(8,128)(2,1)S(1)}, bf16[128,512]{1,0:T(8,128)(2,1)S(1)}) custom-call(bf16[512,512]{1,0:T(8,128)(2,1)S(1)} %get-tuple-element.27.form_ref.rest_0_, bf16[128,512]{1,0:T(8,128)(2,1)S(1)} %get-tuple-element.30.refs_0_, ...), custom_call_target="tpu_custom_call" | custom-call | flops 1 | bytes 1 | tf_op jit(solution)/shard_map/pallas_call | solution.py:304
  19.0 2.2 %collective-permute-start.3 = (bf16[128,512]{1,0:T(8,128)(2,1)S(1)}, bf16[128,512]{1,0:T(8,128)(2,1)S(1)}, u32[]{:S(2)}, u32[]{:S(2)}) collective-permute-start(bf16[128,512]{1,0:T(8,128)(2,1)S(1)} %get-tuple-element.35), channel_id=1, source_target_pairs={{0,8},{4,12},{8,0},{12,4},{16,24},{20,28},{24,16},{28,20},{1,9},{5... | collective-permute-start | bytes 393224 | tf_op jit(solution)/shard_map/ppermute | solution.py:229
  21.2 1.5 %collective-permute-start.4 = (bf16[128,512]{1,0:T(8,128)(2,1)S(1)}, bf16[128,512]{1,0:T(8,128)(2,1)S(1)}, u32[]{:S(2)}, u32[]{:S(2)}) collective-permute-start(bf16[128,512]{1,0:T(8,128)(2,1)S(1)} %get-tuple-element.36), channel_id=1, source_target_pairs={{0,16},{4,20},{8,24},{12,28},{16,0},{20,4},{24,8},{28,12},{1,17},{... | collective-permute-start | bytes 393224 | tf_op jit(solution)/shard_map/ppermute | solution.py:229
  22.7 0.0 collective-permute-done.7.refs_1_
  22.7 1.4 %collective-permute-start.5 = (bf16[128,512]{1,0:T(8,128)(2,1)S(1)}, bf16[128,512]{1,0:T(8,128)(2,1)S(1)}, u32[]{:S(2)}, u32[]{:S(2)}) collective-permute-start(bf16[128,512]{1,0:T(8,128)(2,1)S(1)} %get-tuple-element.37), channel_id=1, source_target_pairs={{0,24},{4,28},{8,16},{12,20},{16,8},{20,12},{24,0},{28,4},{1,25},{... | collective-permute-start | bytes 393224 | tf_op jit(solution)/shard_map/ppermute | solution.py:229
  24.1 3.7 %collective-permute-done.8.refs_2_ = bf16[128,512]{1,0:T(8,128)(2,1)S(1)} collective-permute-done((bf16[128,512]{1,0:T(8,128)(2,1)S(1)}, bf16[128,512]{1,0:T(8,128)(2,1)S(1)}, u32[]{:S(2)}, u32[]{:S(2)}) %collective-permute-start.8) | collective-permute-done | bytes 131104 | tf_op jit(solution)/shard_map/ppermute | solution.py:229
  27.8 0.0 collective-permute-done.9.refs_3_
  27.8 0.3 shard_map.47
  28.1 1.6 %collective-permute-start.12 = (bf16[128,512]{1,0:T(8,128)(2,1)S(1)}, bf16[128,512]{1,0:T(8,128)(2,1)S(1)}, u32[]{:S(2)}, u32[]{:S(2)}) collective-permute-start(bf16[128,512]{1,0:T(8,128)(2,1)S(1)} %get-tuple-element.45), channel_id=1, source_target_pairs={{0,16},{4,20},{8,24},{12,28},{16,0},{20,4},{24,8},{28,12},{1,17},{... | collective-permute-start | bytes 393224 | tf_op jit(solution)/shard_map/ppermute | solution.py:229
  29.7 1.4 %collective-permute-start.13 = (bf16[128,512]{1,0:T(8,128)(2,1)S(1)}, bf16[128,512]{1,0:T(8,128)(2,1)S(1)}, u32[]{:S(2)}, u32[]{:S(2)}) collective-permute-start(bf16[128,512]{1,0:T(8,128)(2,1)S(1)} %get-tuple-element.46), channel_id=1, source_target_pairs={{0,24},{4,28},{8,16},{12,20},{16,8},{20,12},{24,0},{28,4},{1,25},{... | collective-permute-start | bytes 393224 | tf_op jit(solution)/shard_map/ppermute | solution.py:229
  31.1 0.3 shard_map.45
  31.4 0.0 collective-permute-done.3.refs_1_
  31.4 0.6 %collective-permute-start.10 = (bf16[64,512]{1,0:T(8,128)(2,1)S(1)}, bf16[64,512]{1,0:T(8,128)(2,1)S(1)}, u32[]{:S(2)}, u32[]{:S(2)}) collective-permute-start(bf16[64,512]{1,0:T(8,128)(2,1)S(1)} %get-tuple-element.43), channel_id=1, source_target_pairs={{0,8},{4,12},{8,0},{12,4},{16,24},{20,28},{24,16},{28,20},{1,9},{5... | collective-permute-start | bytes 196616 | tf_op jit(solution)/shard_map/ppermute | solution.py:229
  32.0 0.0 collective-permute-done.4.refs_2_
  32.0 0.0 collective-permute-start.11
  32.0 0.0 collective-permute-done.5.refs_3_
  32.0 0.3 shard_map.41.refs_4_.refs_0_
  32.4 1.7 %collective-permute-start.6 = (bf16[256,512]{1,0:T(8,128)(2,1)S(1)}, bf16[256,512]{1,0:T(8,128)(2,1)S(1)}, u32[]{:S(2)}, u32[]{:S(2)}) collective-permute-start(bf16[256,512]{1,0:T(8,128)(2,1)S(1)} %shard_map.42), channel_id=1, source_target_pairs={{0,4},{4,0},{8,12},{12,8},{16,20},{20,16},{24,28},{28,24},{1,5},{5... | collective-permute-start | bytes 786440 | tf_op jit(solution)/shard_map/ppermute | solution.py:229
  34.1 0.2 shard_map.46.refs_0_
  34.3 0.0 collective-permute-done.12.refs_1_
  34.3 1.3 %collective-permute-done.13.refs_2_ = bf16[128,512]{1,0:T(8,128)(2,1)S(1)} collective-permute-done((bf16[128,512]{1,0:T(8,128)(2,1)S(1)}, bf16[128,512]{1,0:T(8,128)(2,1)S(1)}, u32[]{:S(2)}, u32[]{:S(2)}) %collective-permute-start.13) | collective-permute-done | bytes 131104 | tf_op jit(solution)/shard_map/ppermute | solution.py:229
  35.6 0.1 collective-permute-start.14
  35.7 0.3 shard_map.48.refs_2_
  36.0 0.4 %collective-permute-done.10.refs_0_ = bf16[64,512]{1,0:T(8,128)(2,1)S(1)} collective-permute-done((bf16[64,512]{1,0:T(8,128)(2,1)S(1)}, bf16[64,512]{1,0:T(8,128)(2,1)S(1)}, u32[]{:S(2)}, u32[]{:S(2)}) %collective-permute-start.10) | collective-permute-done | bytes 65568 | tf_op jit(solution)/shard_map/ppermute | solution.py:229
  36.4 0.0 collective-permute-done.11.refs_1_
  36.4 0.3 shard_map.49.refs_1_
  36.7 0.0 collective-permute-done.6.refs_1_
  36.8 0.3 shard_map.43.refs_0_
  37.1 0.0 collective-permute-done.14.refs_2_
  37.1 1.1 %shard_map.51 = bf16[2,1,1,1024,256]{4,3,2,1,0:T(8,128)(2,1)} custom-call(bf16[512,512]{1,0:T(8,128)(2,1)S(1)} %get-tuple-element.26.form_ref, bf16[2,512,256]{2,1,0:T(8,128)(2,1)S(1)} %shard_map.43.refs_0_, f32[512,512]{1,0:T(8,128)S(1)} %shard_map.49.refs_1_, bf16[192,512]{1,0:T(8,128)(2,1)S(1)} %collective-permute-done.14.refs_2_), custom_call_target="tpu_custom_call" | custom-call | flops 1 | bytes 1 | tf_op jit(solution)/shard_map/pallas_call | solution.py:350
  (2 shorter events, 0.0 us)
Async XLA Ops:
  1.6 12.1 %collective-permute-start.1 = (bf16[128,512]{1,0:T(8,128)(2,1)S(1)}, bf16[128,512]{1,0:T(8,128)(2,1)S(1)}, u32[]{:S(2)}, u32[]{:S(2)}) collective-permute-start(bf16[128,512]{1,0:T(8,128)(2,1)S(1)} %get-tuple-element.32), channel_id=1, source_target_pairs={{0,2},{1,3},{2,0},{3,1},{4,6},{5,7},{6,4},{7,5},{8,10},{9,11},{10,... | collective-permute-start | bytes 393224 | tf_op jit(solution)/shard_map/ppermute | solution.py:229
  6.1 12.5 %collective-permute-start = (bf16[128,512]{1,0:T(8,128)(2,1)S(1)}, bf16[128,512]{1,0:T(8,128)(2,1)S(1)}, u32[]{:S(2)}, u32[]{:S(2)}) collective-permute-start(bf16[128,512]{1,0:T(8,128)(2,1)S(1)} %get-tuple-element.31), channel_id=1, source_target_pairs={{0,1},{1,0},{2,3},{3,2},{4,5},{5,4},{6,7},{7,6},{8,9},{9,8},{10,11... | collective-permute-start | bytes 393224 | tf_op jit(solution)/shard_map/ppermute | solution.py:229
  7.7 10.9 %collective-permute-start.2 = (bf16[128,512]{1,0:T(8,128)(2,1)S(1)}, bf16[128,512]{1,0:T(8,128)(2,1)S(1)}, u32[]{:S(2)}, u32[]{:S(2)}) collective-permute-start(bf16[128,512]{1,0:T(8,128)(2,1)S(1)} %get-tuple-element.33), channel_id=1, source_target_pairs={{0,3},{1,2},{2,1},{3,0},{4,7},{5,6},{6,5},{7,4},{8,11},{9,10},{10,... | collective-permute-start | bytes 393224 | tf_op jit(solution)/shard_map/ppermute | solution.py:229
  14.1 8.6 %collective-permute-start.7 = (bf16[128,512]{1,0:T(8,128)(2,1)S(1)}, bf16[128,512]{1,0:T(8,128)(2,1)S(1)}, u32[]{:S(2)}, u32[]{:S(2)}) collective-permute-start(bf16[128,512]{1,0:T(8,128)(2,1)S(1)} %get-tuple-element.40), channel_id=1, source_target_pairs={{0,1},{1,0},{2,3},{3,2},{4,5},{5,4},{6,7},{7,6},{8,9},{9,8},{10,11... | collective-permute-start | bytes 393224 | tf_op jit(solution)/shard_map/ppermute | solution.py:229
  14.2 13.6 %collective-permute-start.8 = (bf16[128,512]{1,0:T(8,128)(2,1)S(1)}, bf16[128,512]{1,0:T(8,128)(2,1)S(1)}, u32[]{:S(2)}, u32[]{:S(2)}) collective-permute-start(bf16[128,512]{1,0:T(8,128)(2,1)S(1)} %get-tuple-element.41), channel_id=1, source_target_pairs={{0,2},{1,3},{2,0},{3,1},{4,6},{5,7},{6,4},{7,5},{8,10},{9,11},{10,... | collective-permute-start | bytes 393224 | tf_op jit(solution)/shard_map/ppermute | solution.py:229
  17.8 10.0 %collective-permute-start.9 = (bf16[128,512]{1,0:T(8,128)(2,1)S(1)}, bf16[128,512]{1,0:T(8,128)(2,1)S(1)}, u32[]{:S(2)}, u32[]{:S(2)}) collective-permute-start(bf16[128,512]{1,0:T(8,128)(2,1)S(1)} %get-tuple-element.42), channel_id=1, source_target_pairs={{0,3},{1,2},{2,1},{3,0},{4,7},{5,6},{6,5},{7,4},{8,11},{9,10},{10,... | collective-permute-start | bytes 393224 | tf_op jit(solution)/shard_map/ppermute | solution.py:229
  19.0 12.4 %collective-permute-start.3 = (bf16[128,512]{1,0:T(8,128)(2,1)S(1)}, bf16[128,512]{1,0:T(8,128)(2,1)S(1)}, u32[]{:S(2)}, u32[]{:S(2)}) collective-permute-start(bf16[128,512]{1,0:T(8,128)(2,1)S(1)} %get-tuple-element.35), channel_id=1, source_target_pairs={{0,8},{4,12},{8,0},{12,4},{16,24},{20,28},{24,16},{28,20},{1,9},{5... | collective-permute-start | bytes 393224 | tf_op jit(solution)/shard_map/ppermute | solution.py:229
  21.2 10.8 %collective-permute-start.4 = (bf16[128,512]{1,0:T(8,128)(2,1)S(1)}, bf16[128,512]{1,0:T(8,128)(2,1)S(1)}, u32[]{:S(2)}, u32[]{:S(2)}) collective-permute-start(bf16[128,512]{1,0:T(8,128)(2,1)S(1)} %get-tuple-element.36), channel_id=1, source_target_pairs={{0,16},{4,20},{8,24},{12,28},{16,0},{20,4},{24,8},{28,12},{1,17},{... | collective-permute-start | bytes 393224 | tf_op jit(solution)/shard_map/ppermute | solution.py:229
  22.7 9.3 %collective-permute-start.5 = (bf16[128,512]{1,0:T(8,128)(2,1)S(1)}, bf16[128,512]{1,0:T(8,128)(2,1)S(1)}, u32[]{:S(2)}, u32[]{:S(2)}) collective-permute-start(bf16[128,512]{1,0:T(8,128)(2,1)S(1)} %get-tuple-element.37), channel_id=1, source_target_pairs={{0,24},{4,28},{8,16},{12,20},{16,8},{20,12},{24,0},{28,4},{1,25},{... | collective-permute-start | bytes 393224 | tf_op jit(solution)/shard_map/ppermute | solution.py:229
  28.1 6.2 %collective-permute-start.12 = (bf16[128,512]{1,0:T(8,128)(2,1)S(1)}, bf16[128,512]{1,0:T(8,128)(2,1)S(1)}, u32[]{:S(2)}, u32[]{:S(2)}) collective-permute-start(bf16[128,512]{1,0:T(8,128)(2,1)S(1)} %get-tuple-element.45), channel_id=1, source_target_pairs={{0,16},{4,20},{8,24},{12,28},{16,0},{20,4},{24,8},{28,12},{1,17},{... | collective-permute-start | bytes 393224 | tf_op jit(solution)/shard_map/ppermute | solution.py:229
  29.7 5.9 %collective-permute-start.13 = (bf16[128,512]{1,0:T(8,128)(2,1)S(1)}, bf16[128,512]{1,0:T(8,128)(2,1)S(1)}, u32[]{:S(2)}, u32[]{:S(2)}) collective-permute-start(bf16[128,512]{1,0:T(8,128)(2,1)S(1)} %get-tuple-element.46), channel_id=1, source_target_pairs={{0,24},{4,28},{8,16},{12,20},{16,8},{20,12},{24,0},{28,4},{1,25},{... | collective-permute-start | bytes 393224 | tf_op jit(solution)/shard_map/ppermute | solution.py:229
  31.4 5.0 %collective-permute-start.10 = (bf16[64,512]{1,0:T(8,128)(2,1)S(1)}, bf16[64,512]{1,0:T(8,128)(2,1)S(1)}, u32[]{:S(2)}, u32[]{:S(2)}) collective-permute-start(bf16[64,512]{1,0:T(8,128)(2,1)S(1)} %get-tuple-element.43), channel_id=1, source_target_pairs={{0,8},{4,12},{8,0},{12,4},{16,24},{20,28},{24,16},{28,20},{1,9},{5... | collective-permute-start | bytes 196616 | tf_op jit(solution)/shard_map/ppermute | solution.py:229
  32.0 4.4 %collective-permute-start.11 = (bf16[64,512]{1,0:T(8,128)(2,1)S(1)}, bf16[64,512]{1,0:T(8,128)(2,1)S(1)}, u32[]{:S(2)}, u32[]{:S(2)}) collective-permute-start(bf16[64,512]{1,0:T(8,128)(2,1)S(1)} %get-tuple-element.44), channel_id=1, source_target_pairs={{0,12},{4,8},{8,4},{12,0},{16,28},{20,24},{24,20},{28,16},{1,13},{... | collective-permute-start | bytes 196616 | tf_op jit(solution)/shard_map/ppermute | solution.py:229
  32.4 4.4 %collective-permute-start.6 = (bf16[256,512]{1,0:T(8,128)(2,1)S(1)}, bf16[256,512]{1,0:T(8,128)(2,1)S(1)}, u32[]{:S(2)}, u32[]{:S(2)}) collective-permute-start(bf16[256,512]{1,0:T(8,128)(2,1)S(1)} %shard_map.42), channel_id=1, source_target_pairs={{0,4},{4,0},{8,12},{12,8},{16,20},{20,16},{24,28},{28,24},{1,5},{5... | collective-permute-start | bytes 786440 | tf_op jit(solution)/shard_map/ppermute | solution.py:229
  35.6 1.5 %collective-permute-start.14 = (bf16[192,512]{1,0:T(8,128)(2,1)S(1)}, bf16[192,512]{1,0:T(8,128)(2,1)S(1)}, u32[]{:S(2)}, u32[]{:S(2)}) collective-permute-start(bf16[192,512]{1,0:T(8,128)(2,1)S(1)} %shard_map.50), channel_id=1, source_target_pairs={{0,4},{4,0},{8,12},{12,8},{16,20},{20,16},{24,28},{28,24},{1,5},{5... | collective-permute-start | bytes 589832 | tf_op jit(solution)/shard_map/ppermute | solution.py:229

commit v6 on v5

--- a/solution.py
+++ b/solution.py
@@ -144,11 +144,21 @@
 
 
 def second_kernel(n_in, slots, form_ref, *refs):
-    ins, outs = refs[:n_in], refs[n_in:]
+    ins, total, outs = refs[:n_in], refs[n_in : -len(slots)], refs[-len(slots) :]
     joined = gathered(ins)
+    ahead = form_ref.shape[1] - joined.shape[0]
     for slot, out in zip(slots, outs):
         rows = out.shape[0]
-        out[...] = dot(form_ref[rows * slot : rows * (slot + 1)], joined, 1, 0).astype(BF16)
+        here = slice(rows * slot, rows * (slot + 1))
+        result = dot(form_ref[here, ahead:], joined, 1, 0)
+        for before in total:
+            result = result + before[here]
+        out[...] = result.astype(BF16)
+
+
+def second_part_kernel(form_ref, *refs):
+    joined = gathered(refs[:-1])
+    refs[-1][...] = dot(form_ref[:, : joined.shape[0]], joined, 1, 0)
 
 
 def pass_kernel(count, *refs):
@@ -298,12 +308,13 @@
 
     pairs = outer // 2
 
-    def second(n, slots, rows_each, cost):
-        ins = arrived[n]
+    def second(n, slots, rows_each, cost, total=()):
+        ins = arrived[n][half:] if total else arrived[n]
         shapes = [shape(rows_each, sizes[n])] * len(slots)
         made = call(
-            functools.partial(second_kernel, len(ins), slots), [VM] * (1 + len(ins)), shapes, [VM] * len(slots), cost
-        )(form1, *ins)
+            functools.partial(second_kernel, len(ins), slots),
+            [VM] * (1 + len(ins) + len(total)), shapes, [VM] * len(slots), cost,
+        )(form1, *ins, *total)
         return dict(zip(slots, made))
 
     def third_part(n, blocks, cost, *before):
@@ -329,9 +340,16 @@
 
     def last_exchange(n):
         slots = (0,) + tuple(range(2, pairs))
-        made = second(n, slots[:1], full // pairs, FREE) | second(n, slots[1:], full // pairs, LONG)
+        near = ()
+        if rel1:
+            near = (
+                call(
+                    second_part_kernel, [VM] * (1 + half), jax.ShapeDtypeStruct((full, sizes[n]), F32), VM, FREE
+                )(form1, *arrived[n][:half]),
+            )
+        made = second(n, slots[:1], full // pairs, FREE, near) | second(n, slots[1:], full // pairs, LONG, near)
         came = {q: swap(made[q], "grp", outer, 2 * q) if q else made[q] for q in slots}
-        direct = second(n, (2, 3), full // outer, FREE)
+        direct = second(n, (2, 3), full // outer, FREE, near)
         direct = {k: swap(direct[k], "grp", outer, k) for k in direct}
         passed, places = pass_on(n, came)
         total = third_part(n, {2 * q: came[q] for q in slots}, FREE)

time: 38.8 us -> 38.6 us (level)
  transfers between devices with their start and end apart: 15 -> 15, of which waited for: 4 -> 5; matrix products, arithmetic and copies ran while one was open for 0% -> 0% of each run, Pallas kernels for 15% -> 15%
where the time goes in v6:
time: 38.6 us; the launch traced here: 38.1 us
  starting transfers between devices  20.7 us (54%)
  waiting for transfers between devices  8.81 us (23%)
  Pallas kernels  8.5 us (22%)
    ppermute x15, starting transfers between devices, swap(): return lax.ppermute(piece, axis, [(i, i ^ k) for i in range(count)])  20.7 us
    ppermute x15, waiting for transfers between devices, swap(): return lax.ppermute(piece, axis, [(i, i ^ k) for i in range(count)])  8.81 us
    pallas_call x1, Pallas kernels, local(): call(functools.partial(forms_kernel, sizes, part1, rel1, part2, rel2), [H...  2.31 us
    pallas_call x1, Pallas kernels, local(): call(functools.partial(opening_kernel, part1, rel1, opening), [HBM] * 3,...  1.57 us
    pallas_call x1, Pallas kernels, local(): call(functools.partial(closing_kernel, last, places), [VM] * (1 + last +...  1.08 us
    pallas_call x4, Pallas kernels, second(): call(functools.partial(second_kernel, len(ins), slots), [VM] * (1 + len(i...  1.06 us
    pallas_call x3, Pallas kernels, third_part(): call(functools.partial(third_part_kernel, tuple(blocks), full // outer),...  0.97 us
    pallas_call x2, Pallas kernels, first_pieces(): call(functools.partial(first_kernel, part1, rel1, owners, len(shapes)), [...  0.86 us
  transfers between devices with their start and end apart: 15, of which 5 were waited for; matrix products, arithmetic and copies ran while one was open for 0% of the time, Pallas kernels for 15%

profile of v6, /device:TPU:0, one launch (start us, length us, event | category | flops | bytes accessed | tf_op | source)
XLA Modules:
  0.0 38.1 jit_solution(173490298919644713)
XLA Ops:
  0.0 1.6 %shard_map.38 = (bf16[512,512]{1,0:T(8,128)(2,1)S(1)}, bf16[2,512,256]{2,1,0:T(8,128)(2,1)S(1)}, bf16[128,512]{1,0:T(8,128)(2,1)S(1)}) custom-call(bf16[2,1,1,1024,256]{4,3,2,1,0:T(8,128)(2,1)} %stem_ref.3, bf16[3,2,256,256]{3,2,1,0:T(8,128)(2,1)} %branches_ref.3, s32[3,256]{1,0:T(4,128)} %order_ref.3), custom_call_target="tpu_custom_call" | custom-call | flops 1 | bytes 1 | tf_op jit(solution)/shard_map/pallas_call | solution.py:291
  1.6 4.1 %collective-permute-start.1 = (bf16[128,512]{1,0:T(8,128)(2,1)S(1)}, bf16[128,512]{1,0:T(8,128)(2,1)S(1)}, u32[]{:S(2)}, u32[]{:S(2)}) collective-permute-start(bf16[128,512]{1,0:T(8,128)(2,1)S(1)} %get-tuple-element.32), channel_id=1, source_target_pairs={{0,2},{1,3},{2,0},{3,1},{4,6},{5,7},{6,4},{7,5},{8,10},{9,11},{10,... | collective-permute-start | bytes 393224 | tf_op jit(solution)/shard_map/ppermute | solution.py:239
  5.7 0.4 %shard_map.39 = (bf16[128,512]{1,0:T(8,128)(2,1)S(1)}, bf16[128,512]{1,0:T(8,128)(2,1)S(1)}, bf16[128,512]{1,0:T(8,128)(2,1)S(1)}) custom-call(bf16[2,512,256]{2,1,0:T(8,128)(2,1)S(1)} %get-tuple-element.28.block_ref, bf16[512,512]{1,0:T(8,128)(2,1)S(1)} %get-tuple-element.29.form_ref), custom_call_target="tpu_custom_call" | custom-call | flops 1 | bytes 1 | tf_op jit(solution)/shard_map/pallas_call | solution.py:277
  6.1 1.7 %collective-permute-start = (bf16[128,512]{1,0:T(8,128)(2,1)S(1)}, bf16[128,512]{1,0:T(8,128)(2,1)S(1)}, u32[]{:S(2)}, u32[]{:S(2)}) collective-permute-start(bf16[128,512]{1,0:T(8,128)(2,1)S(1)} %get-tuple-element.31), channel_id=1, source_target_pairs={{0,1},{1,0},{2,3},{3,2},{4,5},{5,4},{6,7},{7,6},{8,9},{9,8},{10,11... | collective-permute-start | bytes 393224 | tf_op jit(solution)/shard_map/ppermute | solution.py:239
  7.7 0.0 collective-permute-start.2
  7.7 2.3 %shard_map.37 = (bf16[512,512]{1,0:T(8,128)(2,1)S(1)}, bf16[512,512]{1,0:T(8,128)(2,1)S(1)}, bf16[2,512,256]{2,1,0:T(8,128)(2,1)S(1)}) custom-call(bf16[2,1,1,1024,256]{4,3,2,1,0:T(8,128)(2,1)} %stem_ref.3, bf16[3,2,256,256]{3,2,1,0:T(8,128)(2,1)} %branches_ref.3, s32[3,256]{1,0:T(4,128)} %order_ref.3), custom_call_target="tpu_custom_call" | custom-call | flops 1 | bytes 1 | tf_op jit(solution)/shard_map/pallas_call | solution.py:300
  10.1 3.6 %collective-permute-done.1.refs_2_.rest_1_ = bf16[128,512]{1,0:T(8,128)(2,1)S(1)} collective-permute-done((bf16[128,512]{1,0:T(8,128)(2,1)S(1)}, bf16[128,512]{1,0:T(8,128)(2,1)S(1)}, u32[]{:S(2)}, u32[]{:S(2)}) %collective-permute-start.1) | collective-permute-done | bytes 131104 | tf_op jit(solution)/shard_map/ppermute | solution.py:239
  13.6 0.5 %shard_map.44 = (bf16[128,512]{1,0:T(8,128)(2,1)S(1)}, bf16[128,512]{1,0:T(8,128)(2,1)S(1)}, bf16[128,512]{1,0:T(8,128)(2,1)S(1)}, bf16[128,512]{1,0:T(8,128)(2,1)S(1)}) custom-call(bf16[2,512,256]{2,1,0:T(8,128)(2,1)S(1)} %get-tuple-element.38.block_ref, bf16[512,512]{1,0:T(8,128)(2,1)S(1)} %get-tuple-element.29.form_ref, ...), custom_call_target="tpu_custom_call" | custom-call | flops 1 | bytes 1 | tf_op jit(solution)/shard_map/pallas_call | solution.py:277
  14.1 0.1 collective-permute-start.9
  14.2 3.6 %collective-permute-start.7 = (bf16[128,512]{1,0:T(8,128)(2,1)S(1)}, bf16[128,512]{1,0:T(8,128)(2,1)S(1)}, u32[]{:S(2)}, u32[]{:S(2)}) collective-permute-start(bf16[128,512]{1,0:T(8,128)(2,1)S(1)} %get-tuple-element.39), channel_id=1, source_target_pairs={{0,2},{1,3},{2,0},{3,1},{4,6},{5,7},{6,4},{7,5},{8,10},{9,11},{10,... | collective-permute-start | bytes 393224 | tf_op jit(solution)/shard_map/ppermute | solution.py:239
  17.8 0.8 %collective-permute-start.8 = (bf16[128,512]{1,0:T(8,128)(2,1)S(1)}, bf16[128,512]{1,0:T(8,128)(2,1)S(1)}, u32[]{:S(2)}, u32[]{:S(2)}) collective-permute-start(bf16[128,512]{1,0:T(8,128)(2,1)S(1)} %get-tuple-element.40), channel_id=1, source_target_pairs={{0,3},{1,2},{2,1},{3,0},{4,7},{5,6},{6,5},{7,4},{8,11},{9,10},{10,... | collective-permute-start | bytes 393224 | tf_op jit(solution)/shard_map/ppermute | solution.py:239
  18.6 0.0 collective-permute-done.refs_1_
  18.6 0.0 collective-permute-done.2.refs_3_
  18.6 0.4 %shard_map.40 = (bf16[128,512]{1,0:T(8,128)(2,1)S(1)}, bf16[128,512]{1,0:T(8,128)(2,1)S(1)}, bf16[128,512]{1,0:T(8,128)(2,1)S(1)}, bf16[128,512]{1,0:T(8,128)(2,1)S(1)}) custom-call(bf16[512,512]{1,0:T(8,128)(2,1)S(1)} %get-tuple-element.27.form_ref.rest_0_, bf16[128,512]{1,0:T(8,128)(2,1)S(1)} %get-tuple-element.30.refs_0_, ...), custom_call_target="tpu_custom_call" | custom-call | flops 1 | bytes 1 | tf_op jit(solution)/shard_map/pallas_call | solution.py:314
  19.0 2.2 %collective-permute-start.3 = (bf16[128,512]{1,0:T(8,128)(2,1)S(1)}, bf16[128,512]{1,0:T(8,128)(2,1)S(1)}, u32[]{:S(2)}, u32[]{:S(2)}) collective-permute-start(bf16[128,512]{1,0:T(8,128)(2,1)S(1)} %get-tuple-element.35), channel_id=1, source_target_pairs={{0,8},{4,12},{8,0},{12,4},{16,24},{20,28},{24,16},{28,20},{1,9},{5... | collective-permute-start | bytes 393224 | tf_op jit(solution)/shard_map/ppermute | solution.py:239
  21.2 1.5 %collective-permute-start.4 = (bf16[128,512]{1,0:T(8,128)(2,1)S(1)}, bf16[128,512]{1,0:T(8,128)(2,1)S(1)}, u32[]{:S(2)}, u32[]{:S(2)}) collective-permute-start(bf16[128,512]{1,0:T(8,128)(2,1)S(1)} %get-tuple-element.36), channel_id=1, source_target_pairs={{0,16},{4,20},{8,24},{12,28},{16,0},{20,4},{24,8},{28,12},{1,17},{... | collective-permute-start | bytes 393224 | tf_op jit(solution)/shard_map/ppermute | solution.py:239
  22.7 0.0 collective-permute-done.9.refs_1_
  22.7 1.4 %collective-permute-start.5 = (bf16[128,512]{1,0:T(8,128)(2,1)S(1)}, bf16[128,512]{1,0:T(8,128)(2,1)S(1)}, u32[]{:S(2)}, u32[]{:S(2)}) collective-permute-start(bf16[128,512]{1,0:T(8,128)(2,1)S(1)} %get-tuple-element.37), channel_id=1, source_target_pairs={{0,24},{4,28},{8,16},{12,20},{16,8},{20,12},{24,0},{28,4},{1,25},{... | collective-permute-start | bytes 393224 | tf_op jit(solution)/shard_map/ppermute | solution.py:239
  24.1 0.3 shard_map.45.refs_2_
  24.4 3.4 %collective-permute-done.7.refs_0_ = bf16[128,512]{1,0:T(8,128)(2,1)S(1)} collective-permute-done((bf16[128,512]{1,0:T(8,128)(2,1)S(1)}, bf16[128,512]{1,0:T(8,128)(2,1)S(1)}, u32[]{:S(2)}, u32[]{:S(2)}) %collective-permute-start.7) | collective-permute-done | bytes 131104 | tf_op jit(solution)/shard_map/ppermute | solution.py:239
  27.8 0.0 collective-permute-done.8.refs_1_
  27.8 0.2 shard_map.48
  28.0 1.6 %collective-permute-start.12 = (bf16[128,512]{1,0:T(8,128)(2,1)S(1)}, bf16[128,512]{1,0:T(8,128)(2,1)S(1)}, u32[]{:S(2)}, u32[]{:S(2)}) collective-permute-start(bf16[128,512]{1,0:T(8,128)(2,1)S(1)} %get-tuple-element.45), channel_id=1, source_target_pairs={{0,16},{4,20},{8,24},{12,28},{16,0},{20,4},{24,8},{28,12},{1,17},{... | collective-permute-start | bytes 393224 | tf_op jit(solution)/shard_map/ppermute | solution.py:239
  29.6 1.4 %collective-permute-start.13 = (bf16[128,512]{1,0:T(8,128)(2,1)S(1)}, bf16[128,512]{1,0:T(8,128)(2,1)S(1)}, u32[]{:S(2)}, u32[]{:S(2)}) collective-permute-start(bf16[128,512]{1,0:T(8,128)(2,1)S(1)} %get-tuple-element.46), channel_id=1, source_target_pairs={{0,24},{4,28},{8,16},{12,20},{16,8},{20,12},{24,0},{28,4},{1,25},{... | collective-permute-start | bytes 393224 | tf_op jit(solution)/shard_map/ppermute | solution.py:239
  31.1 0.2 shard_map.46
  31.3 0.0 collective-permute-done.3.refs_1_
  31.3 0.6 %collective-permute-start.10 = (bf16[64,512]{1,0:T(8,128)(2,1)S(1)}, bf16[64,512]{1,0:T(8,128)(2,1)S(1)}, u32[]{:S(2)}, u32[]{:S(2)}) collective-permute-start(bf16[64,512]{1,0:T(8,128)(2,1)S(1)} %get-tuple-element.43), channel_id=1, source_target_pairs={{0,8},{4,12},{8,0},{12,4},{16,24},{20,28},{24,16},{28,20},{1,9},{5... | collective-permute-start | bytes 196616 | tf_op jit(solution)/shard_map/ppermute | solution.py:239
  31.9 0.0 collective-permute-done.4.refs_2_
  31.9 0.0 collective-permute-start.11
  31.9 0.0 collective-permute-done.5.refs_3_
  31.9 0.3 shard_map.41.refs_4_.refs_0_
  32.2 1.7 %collective-permute-start.6 = (bf16[256,512]{1,0:T(8,128)(2,1)S(1)}, bf16[256,512]{1,0:T(8,128)(2,1)S(1)}, u32[]{:S(2)}, u32[]{:S(2)}) collective-permute-start(bf16[256,512]{1,0:T(8,128)(2,1)S(1)} %shard_map.42), channel_id=1, source_target_pairs={{0,4},{4,0},{8,12},{12,8},{16,20},{20,16},{24,28},{28,24},{1,5},{5... | collective-permute-start | bytes 786440 | tf_op jit(solution)/shard_map/ppermute | solution.py:239
  33.9 0.2 shard_map.47.refs_0_
  34.1 0.0 collective-permute-done.12.refs_1_
  34.1 1.4 %collective-permute-done.13.refs_2_ = bf16[128,512]{1,0:T(8,128)(2,1)S(1)} collective-permute-done((bf16[128,512]{1,0:T(8,128)(2,1)S(1)}, bf16[128,512]{1,0:T(8,128)(2,1)S(1)}, u32[]{:S(2)}, u32[]{:S(2)}) %collective-permute-start.13) | collective-permute-done | bytes 131104 | tf_op jit(solution)/shard_map/ppermute | solution.py:239
  35.5 0.1 collective-permute-start.14
  35.6 0.3 shard_map.49.refs_2_
  35.9 0.3 collective-permute-done.10.refs_0_
  36.3 0.0 collective-permute-done.11.refs_1_
  36.3 0.3 shard_map.50.refs_1_
  36.6 0.0 collective-permute-done.6.refs_1_
  36.6 0.3 shard_map.43.refs_0_
  36.9 0.1 collective-permute-done.14.refs_2_
  37.0 1.1 %shard_map.52 = bf16[2,1,1,1024,256]{4,3,2,1,0:T(8,128)(2,1)} custom-call(bf16[512,512]{1,0:T(8,128)(2,1)S(1)} %get-tuple-element.26.form_ref, bf16[2,512,256]{2,1,0:T(8,128)(2,1)S(1)} %shard_map.43.refs_0_, f32[512,512]{1,0:T(8,128)S(1)} %shard_map.50.refs_1_, bf16[192,512]{1,0:T(8,128)(2,1)S(1)} %collective-permute-done.14.refs_2_), custom_call_target="tpu_custom_call" | custom-call | flops 1 | bytes 1 | tf_op jit(solution)/shard_map/pallas_call | solution.py:368
  (2 shorter events, 0.0 us)
Async XLA Ops:
  1.6 12.1 %collective-permute-start.1 = (bf16[128,512]{1,0:T(8,128)(2,1)S(1)}, bf16[128,512]{1,0:T(8,128)(2,1)S(1)}, u32[]{:S(2)}, u32[]{:S(2)}) collective-permute-start(bf16[128,512]{1,0:T(8,128)(2,1)S(1)} %get-tuple-element.32), channel_id=1, source_target_pairs={{0,2},{1,3},{2,0},{3,1},{4,6},{5,7},{6,4},{7,5},{8,10},{9,11},{10,... | collective-permute-start | bytes 393224 | tf_op jit(solution)/shard_map/ppermute | solution.py:239
  6.1 12.5 %collective-permute-start = (bf16[128,512]{1,0:T(8,128)(2,1)S(1)}, bf16[128,512]{1,0:T(8,128)(2,1)S(1)}, u32[]{:S(2)}, u32[]{:S(2)}) collective-permute-start(bf16[128,512]{1,0:T(8,128)(2,1)S(1)} %get-tuple-element.31), channel_id=1, source_target_pairs={{0,1},{1,0},{2,3},{3,2},{4,5},{5,4},{6,7},{7,6},{8,9},{9,8},{10,11... | collective-permute-start | bytes 393224 | tf_op jit(solution)/shard_map/ppermute | solution.py:239
  7.7 10.9 %collective-permute-start.2 = (bf16[128,512]{1,0:T(8,128)(2,1)S(1)}, bf16[128,512]{1,0:T(8,128)(2,1)S(1)}, u32[]{:S(2)}, u32[]{:S(2)}) collective-permute-start(bf16[128,512]{1,0:T(8,128)(2,1)S(1)} %get-tuple-element.33), channel_id=1, source_target_pairs={{0,3},{1,2},{2,1},{3,0},{4,7},{5,6},{6,5},{7,4},{8,11},{9,10},{10,... | collective-permute-start | bytes 393224 | tf_op jit(solution)/shard_map/ppermute | solution.py:239
  14.1 8.6 %collective-permute-start.9 = (bf16[128,512]{1,0:T(8,128)(2,1)S(1)}, bf16[128,512]{1,0:T(8,128)(2,1)S(1)}, u32[]{:S(2)}, u32[]{:S(2)}) collective-permute-start(bf16[128,512]{1,0:T(8,128)(2,1)S(1)} %get-tuple-element.42), channel_id=1, source_target_pairs={{0,1},{1,0},{2,3},{3,2},{4,5},{5,4},{6,7},{7,6},{8,9},{9,8},{10,11... | collective-permute-start | bytes 393224 | tf_op jit(solution)/shard_map/ppermute | solution.py:239
  14.2 13.6 %collective-permute-start.7 = (bf16[128,512]{1,0:T(8,128)(2,1)S(1)}, bf16[128,512]{1,0:T(8,128)(2,1)S(1)}, u32[]{:S(2)}, u32[]{:S(2)}) collective-permute-start(bf16[128,512]{1,0:T(8,128)(2,1)S(1)} %get-tuple-element.39), channel_id=1, source_target_pairs={{0,2},{1,3},{2,0},{3,1},{4,6},{5,7},{6,4},{7,5},{8,10},{9,11},{10,... | collective-permute-start | bytes 393224 | tf_op jit(solution)/shard_map/ppermute | solution.py:239
  17.8 10.0 %collective-permute-start.8 = (bf16[128,512]{1,0:T(8,128)(2,1)S(1)}, bf16[128,512]{1,0:T(8,128)(2,1)S(1)}, u32[]{:S(2)}, u32[]{:S(2)}) collective-permute-start(bf16[128,512]{1,0:T(8,128)(2,1)S(1)} %get-tuple-element.40), channel_id=1, source_target_pairs={{0,3},{1,2},{2,1},{3,0},{4,7},{5,6},{6,5},{7,4},{8,11},{9,10},{10,... | collective-permute-start | bytes 393224 | tf_op jit(solution)/shard_map/ppermute | solution.py:239
  19.0 12.2 %collective-permute-start.3 = (bf16[128,512]{1,0:T(8,128)(2,1)S(1)}, bf16[128,512]{1,0:T(8,128)(2,1)S(1)}, u32[]{:S(2)}, u32[]{:S(2)}) collective-permute-start(bf16[128,512]{1,0:T(8,128)(2,1)S(1)} %get-tuple-element.35), channel_id=1, source_target_pairs={{0,8},{4,12},{8,0},{12,4},{16,24},{20,28},{24,16},{28,20},{1,9},{5... | collective-permute-start | bytes 393224 | tf_op jit(solution)/shard_map/ppermute | solution.py:239
  21.2 10.6 %collective-permute-start.4 = (bf16[128,512]{1,0:T(8,128)(2,1)S(1)}, bf16[128,512]{1,0:T(8,128)(2,1)S(1)}, u32[]{:S(2)}, u32[]{:S(2)}) collective-permute-start(bf16[128,512]{1,0:T(8,128)(2,1)S(1)} %get-tuple-element.36), channel_id=1, source_target_pairs={{0,16},{4,20},{8,24},{12,28},{16,0},{20,4},{24,8},{28,12},{1,17},{... | collective-permute-start | bytes 393224 | tf_op jit(solution)/shard_map/ppermute | solution.py:239
  22.7 9.1 %collective-permute-start.5 = (bf16[128,512]{1,0:T(8,128)(2,1)S(1)}, bf16[128,512]{1,0:T(8,128)(2,1)S(1)}, u32[]{:S(2)}, u32[]{:S(2)}) collective-permute-start(bf16[128,512]{1,0:T(8,128)(2,1)S(1)} %get-tuple-element.37), channel_id=1, source_target_pairs={{0,24},{4,28},{8,16},{12,20},{16,8},{20,12},{24,0},{28,4},{1,25},{... | collective-permute-start | bytes 393224 | tf_op jit(solution)/shard_map/ppermute | solution.py:239
  28.0 6.1 %collective-permute-start.12 = (bf16[128,512]{1,0:T(8,128)(2,1)S(1)}, bf16[128,512]{1,0:T(8,128)(2,1)S(1)}, u32[]{:S(2)}, u32[]{:S(2)}) collective-permute-start(bf16[128,512]{1,0:T(8,128)(2,1)S(1)} %get-tuple-element.45), channel_id=1, source_target_pairs={{0,16},{4,20},{8,24},{12,28},{16,0},{20,4},{24,8},{28,12},{1,17},{... | collective-permute-start | bytes 393224 | tf_op jit(solution)/shard_map/ppermute | solution.py:239
  29.6 5.9 %collective-permute-start.13 = (bf16[128,512]{1,0:T(8,128)(2,1)S(1)}, bf16[128,512]{1,0:T(8,128)(2,1)S(1)}, u32[]{:S(2)}, u32[]{:S(2)}) collective-permute-start(bf16[128,512]{1,0:T(8,128)(2,1)S(1)} %get-tuple-element.46), channel_id=1, source_target_pairs={{0,24},{4,28},{8,16},{12,20},{16,8},{20,12},{24,0},{28,4},{1,25},{... | collective-permute-start | bytes 393224 | tf_op jit(solution)/shard_map/ppermute | solution.py:239
  31.3 5.0 %collective-permute-start.10 = (bf16[64,512]{1,0:T(8,128)(2,1)S(1)}, bf16[64,512]{1,0:T(8,128)(2,1)S(1)}, u32[]{:S(2)}, u32[]{:S(2)}) collective-permute-start(bf16[64,512]{1,0:T(8,128)(2,1)S(1)} %get-tuple-element.43), channel_id=1, source_target_pairs={{0,8},{4,12},{8,0},{12,4},{16,24},{20,28},{24,16},{28,20},{1,9},{5... | collective-permute-start | bytes 196616 | tf_op jit(solution)/shard_map/ppermute | solution.py:239
  31.9 4.4 %collective-permute-start.11 = (bf16[64,512]{1,0:T(8,128)(2,1)S(1)}, bf16[64,512]{1,0:T(8,128)(2,1)S(1)}, u32[]{:S(2)}, u32[]{:S(2)}) collective-permute-start(bf16[64,512]{1,0:T(8,128)(2,1)S(1)} %get-tuple-element.44), channel_id=1, source_target_pairs={{0,12},{4,8},{8,4},{12,0},{16,28},{20,24},{24,20},{28,16},{1,13},{... | collective-permute-start | bytes 196616 | tf_op jit(solution)/shard_map/ppermute | solution.py:239
  32.2 4.4 %collective-permute-start.6 = (bf16[256,512]{1,0:T(8,128)(2,1)S(1)}, bf16[256,512]{1,0:T(8,128)(2,1)S(1)}, u32[]{:S(2)}, u32[]{:S(2)}) collective-permute-start(bf16[256,512]{1,0:T(8,128)(2,1)S(1)} %shard_map.42), channel_id=1, source_target_pairs={{0,4},{4,0},{8,12},{12,8},{16,20},{20,16},{24,28},{28,24},{1,5},{5... | collective-permute-start | bytes 786440 | tf_op jit(solution)/shard_map/ppermute | solution.py:239
  35.5 1.5 %collective-permute-start.14 = (bf16[192,512]{1,0:T(8,128)(2,1)S(1)}, bf16[192,512]{1,0:T(8,128)(2,1)S(1)}, u32[]{:S(2)}, u32[]{:S(2)}) collective-permute-start(bf16[192,512]{1,0:T(8,128)(2,1)S(1)} %shard_map.51), channel_id=1, source_target_pairs={{0,4},{4,0},{8,12},{12,8},{16,20},{20,16},{24,28},{28,24},{1,5},{5... | collective-permute-start | bytes 589832 | tf_op jit(solution)/shard_map/ppermute | solution.py:239

commit v7 on v6

--- a/solution.py
+++ b/solution.py
@@ -105,7 +105,7 @@
         pltpu.make_async_copy(branches_ref.at[0], branch, sem.at[1]),
         pltpu.make_async_copy(stem_ref.at[:, 0, 0, pl.ds(0, block_ref.shape[1])], block_ref, sem.at[2]),
     ]
-    for copy in copies:
+    for copy in (copies[1], copies[0], copies[2]):
         copy.start()
     copies[0].wait()
     copies[1].wait()
@@ -317,6 +317,12 @@
         )(form1, *ins, *total)
         return dict(zip(slots, made))
 
+    def near_sum(n):
+        if not rel1:
+            return ()
+        total = jax.ShapeDtypeStruct((full, sizes[n]), F32)
+        return (call(second_part_kernel, [VM] * (1 + half), total, VM)(form1, *arrived[n][:half]),)
+
     def third_part(n, blocks, cost, *before):
         return call(
             functools.partial(third_part_kernel, tuple(blocks), full // outer),
@@ -332,7 +338,7 @@
 
     def outer_exchange(n):
         slots = tuple(range(pairs))
-        made = second(n, slots, full // pairs, FREE)
+        made = second(n, slots, full // pairs, FREE, near_sum(n))
         came = {q: swap(made[q], "grp", outer, 2 * q) if q else made[q] for q in slots}
         total = third_part(n, {2 * q: came[q] for q in slots}, FREE)
         passed, places = pass_on(n, came, (total,))
@@ -340,13 +346,7 @@
 
     def last_exchange(n):
         slots = (0,) + tuple(range(2, pairs))
-        near = ()
-        if rel1:
-            near = (
-                call(
-                    second_part_kernel, [VM] * (1 + half), jax.ShapeDtypeStruct((full, sizes[n]), F32), VM, FREE
-                )(form1, *arrived[n][:half]),
-            )
+        near = near_sum(n)
         made = second(n, slots[:1], full // pairs, FREE, near) | second(n, slots[1:], full // pairs, LONG, near)
         came = {q: swap(made[q], "grp", outer, 2 * q) if q else made[q] for q in slots}
         direct = second(n, (2, 3), full // outer, FREE, near)

time: 38.6 us -> 38.6 us (level)
  transfers between devices with their start and end apart: 15 -> 15, of which waited for: 5 -> 5; matrix products, arithmetic and copies ran while one was open for 0% -> 0% of each run, Pallas kernels for 15% -> 16%
where the time goes in v7:
time: 38.6 us; the launch traced here: 38.1 us
  starting transfers between devices  20.5 us (53%)
  waiting for transfers between devices  8.79 us (23%)
  Pallas kernels  8.63 us (22%)
    ppermute x15, starting transfers between devices, swap(): return lax.ppermute(piece, axis, [(i, i ^ k) for i in range(count)])  20.5 us
    ppermute x15, waiting for transfers between devices, swap(): return lax.ppermute(piece, axis, [(i, i ^ k) for i in range(count)])  8.79 us
    pallas_call x1, Pallas kernels, local(): call(functools.partial(forms_kernel, sizes, part1, rel1, part2, rel2), [H...  2.31 us
    pallas_call x1, Pallas kernels, local(): call(functools.partial(opening_kernel, part1, rel1, opening), [HBM] * 3,...  1.55 us
    pallas_call x1, Pallas kernels, local(): call(functools.partial(closing_kernel, last, places), [VM] * (1 + last +...  1.08 us
    pallas_call x3, Pallas kernels, third_part(): call(functools.partial(third_part_kernel, tuple(blocks), full // outer),...  0.96 us
    pallas_call x4, Pallas kernels, second(): call(functools.partial(second_kernel, len(ins), slots), [VM] * (1 + len(i...  0.92 us
    pallas_call x2, Pallas kernels, first_pieces(): call(functools.partial(first_kernel, part1, rel1, owners, len(shapes)), [...  0.86 us
  transfers between devices with their start and end apart: 15, of which 5 were waited for; matrix products, arithmetic and copies ran while one was open for 0% of the time, Pallas kernels for 16%

profile of v7, /device:TPU:0, one launch (start us, length us, event | category | flops | bytes accessed | tf_op | source)
XLA Modules:
  0.0 38.1 jit_solution(10339055303790159711)
XLA Ops:
  0.0 1.5 %shard_map.38 = (bf16[512,512]{1,0:T(8,128)(2,1)S(1)}, bf16[2,512,256]{2,1,0:T(8,128)(2,1)S(1)}, bf16[128,512]{1,0:T(8,128)(2,1)S(1)}) custom-call(bf16[2,1,1,1024,256]{4,3,2,1,0:T(8,128)(2,1)} %stem_ref.3, bf16[3,2,256,256]{3,2,1,0:T(8,128)(2,1)} %branches_ref.3, s32[3,256]{1,0:T(4,128)} %order_ref.3), custom_call_target="tpu_custom_call" | custom-call | flops 1 | bytes 1 | tf_op jit(solution)/shard_map/pallas_call | solution.py:291
  1.6 4.1 %collective-permute-start = (bf16[128,512]{1,0:T(8,128)(2,1)S(1)}, bf16[128,512]{1,0:T(8,128)(2,1)S(1)}, u32[]{:S(2)}, u32[]{:S(2)}) collective-permute-start(bf16[128,512]{1,0:T(8,128)(2,1)S(1)} %get-tuple-element.28), channel_id=1, source_target_pairs={{0,2},{1,3},{2,0},{3,1},{4,6},{5,7},{6,4},{7,5},{8,10},{9,11},{10,... | collective-permute-start | bytes 393224 | tf_op jit(solution)/shard_map/ppermute | solution.py:239
  5.7 0.4 %shard_map.39 = (bf16[128,512]{1,0:T(8,128)(2,1)S(1)}, bf16[128,512]{1,0:T(8,128)(2,1)S(1)}, bf16[128,512]{1,0:T(8,128)(2,1)S(1)}) custom-call(bf16[2,512,256]{2,1,0:T(8,128)(2,1)S(1)} %get-tuple-element.29.block_ref, bf16[512,512]{1,0:T(8,128)(2,1)S(1)} %get-tuple-element.30.form_ref), custom_call_target="tpu_custom_call" | custom-call | flops 1 | bytes 1 | tf_op jit(solution)/shard_map/pallas_call | solution.py:277
  6.1 1.6 %collective-permute-start.2 = (bf16[128,512]{1,0:T(8,128)(2,1)S(1)}, bf16[128,512]{1,0:T(8,128)(2,1)S(1)}, u32[]{:S(2)}, u32[]{:S(2)}) collective-permute-start(bf16[128,512]{1,0:T(8,128)(2,1)S(1)} %get-tuple-element.33), channel_id=1, source_target_pairs={{0,1},{1,0},{2,3},{3,2},{4,5},{5,4},{6,7},{7,6},{8,9},{9,8},{10,11... | collective-permute-start | bytes 393224 | tf_op jit(solution)/shard_map/ppermute | solution.py:239
  7.7 0.0 collective-permute-start.1
  7.7 2.3 %shard_map.37 = (bf16[512,512]{1,0:T(8,128)(2,1)S(1)}, bf16[512,512]{1,0:T(8,128)(2,1)S(1)}, bf16[2,512,256]{2,1,0:T(8,128)(2,1)S(1)}) custom-call(bf16[2,1,1,1024,256]{4,3,2,1,0:T(8,128)(2,1)} %stem_ref.3, bf16[3,2,256,256]{3,2,1,0:T(8,128)(2,1)} %branches_ref.3, s32[3,256]{1,0:T(4,128)} %order_ref.3), custom_call_target="tpu_custom_call" | custom-call | flops 1 | bytes 1 | tf_op jit(solution)/shard_map/pallas_call | solution.py:300
  10.0 3.6 %collective-permute-done.refs_0_.rest_1_ = bf16[128,512]{1,0:T(8,128)(2,1)S(1)} collective-permute-done((bf16[128,512]{1,0:T(8,128)(2,1)S(1)}, bf16[128,512]{1,0:T(8,128)(2,1)S(1)}, u32[]{:S(2)}, u32[]{:S(2)}) %collective-permute-start) | collective-permute-done | bytes 131104 | tf_op jit(solution)/shard_map/ppermute | solution.py:239
  13.6 0.5 %shard_map.45 = (bf16[128,512]{1,0:T(8,128)(2,1)S(1)}, bf16[128,512]{1,0:T(8,128)(2,1)S(1)}, bf16[128,512]{1,0:T(8,128)(2,1)S(1)}, bf16[128,512]{1,0:T(8,128)(2,1)S(1)}) custom-call(bf16[2,512,256]{2,1,0:T(8,128)(2,1)S(1)} %get-tuple-element.38.block_ref, bf16[512,512]{1,0:T(8,128)(2,1)S(1)} %get-tuple-element.30.form_ref, ...), custom_call_target="tpu_custom_call" | custom-call | flops 1 | bytes 1 | tf_op jit(solution)/shard_map/pallas_call | solution.py:277
  14.1 0.1 collective-permute-start.9
  14.2 3.6 %collective-permute-start.7 = (bf16[128,512]{1,0:T(8,128)(2,1)S(1)}, bf16[128,512]{1,0:T(8,128)(2,1)S(1)}, u32[]{:S(2)}, u32[]{:S(2)}) collective-permute-start(bf16[128,512]{1,0:T(8,128)(2,1)S(1)} %get-tuple-element.39), channel_id=1, source_target_pairs={{0,2},{1,3},{2,0},{3,1},{4,6},{5,7},{6,4},{7,5},{8,10},{9,11},{10,... | collective-permute-start | bytes 393224 | tf_op jit(solution)/shard_map/ppermute | solution.py:239
  17.8 0.7 %collective-permute-start.8 = (bf16[128,512]{1,0:T(8,128)(2,1)S(1)}, bf16[128,512]{1,0:T(8,128)(2,1)S(1)}, u32[]{:S(2)}, u32[]{:S(2)}) collective-permute-start(bf16[128,512]{1,0:T(8,128)(2,1)S(1)} %get-tuple-element.40), channel_id=1, source_target_pairs={{0,3},{1,2},{2,1},{3,0},{4,7},{5,6},{6,5},{7,4},{8,11},{9,10},{10,... | collective-permute-start | bytes 393224 | tf_op jit(solution)/shard_map/ppermute | solution.py:239
  18.6 0.0 collective-permute-done.2.refs_1_
  18.6 0.3 shard_map.40.refs_2_
  18.9 0.0 collective-permute-done.1.refs_1_
  18.9 0.3 shard_map.41
  19.2 2.2 %collective-permute-start.3 = (bf16[128,512]{1,0:T(8,128)(2,1)S(1)}, bf16[128,512]{1,0:T(8,128)(2,1)S(1)}, u32[]{:S(2)}, u32[]{:S(2)}) collective-permute-start(bf16[128,512]{1,0:T(8,128)(2,1)S(1)} %get-tuple-element.35), channel_id=1, source_target_pairs={{0,8},{4,12},{8,0},{12,4},{16,24},{20,28},{24,16},{28,20},{1,9},{5... | collective-permute-start | bytes 393224 | tf_op jit(solution)/shard_map/ppermute | solution.py:239
  21.4 1.5 %collective-permute-start.4 = (bf16[128,512]{1,0:T(8,128)(2,1)S(1)}, bf16[128,512]{1,0:T(8,128)(2,1)S(1)}, u32[]{:S(2)}, u32[]{:S(2)}) collective-permute-start(bf16[128,512]{1,0:T(8,128)(2,1)S(1)} %get-tuple-element.36), channel_id=1, source_target_pairs={{0,16},{4,20},{8,24},{12,28},{16,0},{20,4},{24,8},{28,12},{1,17},{... | collective-permute-start | bytes 393224 | tf_op jit(solution)/shard_map/ppermute | solution.py:239
  22.9 0.0 collective-permute-done.9.refs_1_
  22.9 1.3 %collective-permute-start.5 = (bf16[128,512]{1,0:T(8,128)(2,1)S(1)}, bf16[128,512]{1,0:T(8,128)(2,1)S(1)}, u32[]{:S(2)}, u32[]{:S(2)}) collective-permute-start(bf16[128,512]{1,0:T(8,128)(2,1)S(1)} %get-tuple-element.37), channel_id=1, source_target_pairs={{0,24},{4,28},{8,16},{12,20},{16,8},{20,12},{24,0},{28,4},{1,25},{... | collective-permute-start | bytes 393224 | tf_op jit(solution)/shard_map/ppermute | solution.py:239
  24.2 0.3 shard_map.46.refs_2_
  24.4 3.4 %collective-permute-done.7.refs_0_ = bf16[128,512]{1,0:T(8,128)(2,1)S(1)} collective-permute-done((bf16[128,512]{1,0:T(8,128)(2,1)S(1)}, bf16[128,512]{1,0:T(8,128)(2,1)S(1)}, u32[]{:S(2)}, u32[]{:S(2)}) %collective-permute-start.7) | collective-permute-done | bytes 131104 | tf_op jit(solution)/shard_map/ppermute | solution.py:239
  27.8 0.0 collective-permute-done.8.refs_1_
  27.8 0.2 shard_map.49
  28.0 1.6 %collective-permute-start.12 = (bf16[128,512]{1,0:T(8,128)(2,1)S(1)}, bf16[128,512]{1,0:T(8,128)(2,1)S(1)}, u32[]{:S(2)}, u32[]{:S(2)}) collective-permute-start(bf16[128,512]{1,0:T(8,128)(2,1)S(1)} %get-tuple-element.45), channel_id=1, source_target_pairs={{0,16},{4,20},{8,24},{12,28},{16,0},{20,4},{24,8},{28,12},{1,17},{... | collective-permute-start | bytes 393224 | tf_op jit(solution)/shard_map/ppermute | solution.py:239
  29.6 1.4 %collective-permute-start.13 = (bf16[128,512]{1,0:T(8,128)(2,1)S(1)}, bf16[128,512]{1,0:T(8,128)(2,1)S(1)}, u32[]{:S(2)}, u32[]{:S(2)}) collective-permute-start(bf16[128,512]{1,0:T(8,128)(2,1)S(1)} %get-tuple-element.46), channel_id=1, source_target_pairs={{0,24},{4,28},{8,16},{12,20},{16,8},{20,12},{24,0},{28,4},{1,25},{... | collective-permute-start | bytes 393224 | tf_op jit(solution)/shard_map/ppermute | solution.py:239
  31.0 0.2 shard_map.47
  31.3 0.0 collective-permute-done.3.refs_1_
  31.3 0.6 %collective-permute-start.10 = (bf16[64,512]{1,0:T(8,128)(2,1)S(1)}, bf16[64,512]{1,0:T(8,128)(2,1)S(1)}, u32[]{:S(2)}, u32[]{:S(2)}) collective-permute-start(bf16[64,512]{1,0:T(8,128)(2,1)S(1)} %get-tuple-element.43), channel_id=1, source_target_pairs={{0,8},{4,12},{8,0},{12,4},{16,24},{20,28},{24,16},{28,20},{1,9},{5... | collective-permute-start | bytes 196616 | tf_op jit(solution)/shard_map/ppermute | solution.py:239
  31.9 0.0 collective-permute-done.4.refs_2_
  31.9 0.0 collective-permute-start.11
  31.9 0.0 collective-permute-done.5.refs_3_
  31.9 0.3 shard_map.42.refs_4_.refs_0_
  32.2 1.7 %collective-permute-start.6 = (bf16[256,512]{1,0:T(8,128)(2,1)S(1)}, bf16[256,512]{1,0:T(8,128)(2,1)S(1)}, u32[]{:S(2)}, u32[]{:S(2)}) collective-permute-start(bf16[256,512]{1,0:T(8,128)(2,1)S(1)} %shard_map.43), channel_id=1, source_target_pairs={{0,4},{4,0},{8,12},{12,8},{16,20},{20,16},{24,28},{28,24},{1,5},{5... | collective-permute-start | bytes 786440 | tf_op jit(solution)/shard_map/ppermute | solution.py:239
  33.9 0.2 shard_map.48.refs_0_
  34.1 0.0 collective-permute-done.12.refs_1_
  34.1 1.4 %collective-permute-done.13.refs_2_ = bf16[128,512]{1,0:T(8,128)(2,1)S(1)} collective-permute-done((bf16[128,512]{1,0:T(8,128)(2,1)S(1)}, bf16[128,512]{1,0:T(8,128)(2,1)S(1)}, u32[]{:S(2)}, u32[]{:S(2)}) %collective-permute-start.13) | collective-permute-done | bytes 131104 | tf_op jit(solution)/shard_map/ppermute | solution.py:239
  35.5 0.1 collective-permute-start.14
  35.6 0.3 shard_map.50.refs_2_
  35.9 0.4 collective-permute-done.10.refs_0_
  36.3 0.0 collective-permute-done.11.refs_1_
  36.3 0.3 shard_map.51.refs_1_
  36.6 0.0 collective-permute-done.6.refs_1_
  36.6 0.3 shard_map.44.refs_0_
  36.9 0.1 collective-permute-done.14.refs_2_
  37.0 1.1 %shard_map.53 = bf16[2,1,1,1024,256]{4,3,2,1,0:T(8,128)(2,1)} custom-call(bf16[512,512]{1,0:T(8,128)(2,1)S(1)} %get-tuple-element.26.form_ref, bf16[2,512,256]{2,1,0:T(8,128)(2,1)S(1)} %shard_map.44.refs_0_, f32[512,512]{1,0:T(8,128)S(1)} %shard_map.51.refs_1_, bf16[192,512]{1,0:T(8,128)(2,1)S(1)} %collective-permute-done.14.refs_2_), custom_call_target="tpu_custom_call" | custom-call | flops 1 | bytes 1 | tf_op jit(solution)/shard_map/pallas_call | solution.py:368
  (2 shorter events, 0.0 us)
Async XLA Ops:
  1.6 12.1 %collective-permute-start = (bf16[128,512]{1,0:T(8,128)(2,1)S(1)}, bf16[128,512]{1,0:T(8,128)(2,1)S(1)}, u32[]{:S(2)}, u32[]{:S(2)}) collective-permute-start(bf16[128,512]{1,0:T(8,128)(2,1)S(1)} %get-tuple-element.28), channel_id=1, source_target_pairs={{0,2},{1,3},{2,0},{3,1},{4,6},{5,7},{6,4},{7,5},{8,10},{9,11},{10,... | collective-permute-start | bytes 393224 | tf_op jit(solution)/shard_map/ppermute | solution.py:239
  6.1 12.5 %collective-permute-start.2 = (bf16[128,512]{1,0:T(8,128)(2,1)S(1)}, bf16[128,512]{1,0:T(8,128)(2,1)S(1)}, u32[]{:S(2)}, u32[]{:S(2)}) collective-permute-start(bf16[128,512]{1,0:T(8,128)(2,1)S(1)} %get-tuple-element.33), channel_id=1, source_target_pairs={{0,1},{1,0},{2,3},{3,2},{4,5},{5,4},{6,7},{7,6},{8,9},{9,8},{10,11... | collective-permute-start | bytes 393224 | tf_op jit(solution)/shard_map/ppermute | solution.py:239
  7.7 11.2 %collective-permute-start.1 = (bf16[128,512]{1,0:T(8,128)(2,1)S(1)}, bf16[128,512]{1,0:T(8,128)(2,1)S(1)}, u32[]{:S(2)}, u32[]{:S(2)}) collective-permute-start(bf16[128,512]{1,0:T(8,128)(2,1)S(1)} %get-tuple-element.31), channel_id=1, source_target_pairs={{0,3},{1,2},{2,1},{3,0},{4,7},{5,6},{6,5},{7,4},{8,11},{9,10},{10,... | collective-permute-start | bytes 393224 | tf_op jit(solution)/shard_map/ppermute | solution.py:239
  14.1 8.8 %collective-permute-start.9 = (bf16[128,512]{1,0:T(8,128)(2,1)S(1)}, bf16[128,512]{1,0:T(8,128)(2,1)S(1)}, u32[]{:S(2)}, u32[]{:S(2)}) collective-permute-start(bf16[128,512]{1,0:T(8,128)(2,1)S(1)} %get-tuple-element.42), channel_id=1, source_target_pairs={{0,1},{1,0},{2,3},{3,2},{4,5},{5,4},{6,7},{7,6},{8,9},{9,8},{10,11... | collective-permute-start | bytes 393224 | tf_op jit(solution)/shard_map/ppermute | solution.py:239
  14.2 13.6 %collective-permute-start.7 = (bf16[128,512]{1,0:T(8,128)(2,1)S(1)}, bf16[128,512]{1,0:T(8,128)(2,1)S(1)}, u32[]{:S(2)}, u32[]{:S(2)}) collective-permute-start(bf16[128,512]{1,0:T(8,128)(2,1)S(1)} %get-tuple-element.39), channel_id=1, source_target_pairs={{0,2},{1,3},{2,0},{3,1},{4,6},{5,7},{6,4},{7,5},{8,10},{9,11},{10,... | collective-permute-start | bytes 393224 | tf_op jit(solution)/shard_map/ppermute | solution.py:239
  17.8 10.0 %collective-permute-start.8 = (bf16[128,512]{1,0:T(8,128)(2,1)S(1)}, bf16[128,512]{1,0:T(8,128)(2,1)S(1)}, u32[]{:S(2)}, u32[]{:S(2)}) collective-permute-start(bf16[128,512]{1,0:T(8,128)(2,1)S(1)} %get-tuple-element.40), channel_id=1, source_target_pairs={{0,3},{1,2},{2,1},{3,0},{4,7},{5,6},{6,5},{7,4},{8,11},{9,10},{10,... | collective-permute-start | bytes 393224 | tf_op jit(solution)/shard_map/ppermute | solution.py:239
  19.2 12.1 %collective-permute-start.3 = (bf16[128,512]{1,0:T(8,128)(2,1)S(1)}, bf16[128,512]{1,0:T(8,128)(2,1)S(1)}, u32[]{:S(2)}, u32[]{:S(2)}) collective-permute-start(bf16[128,512]{1,0:T(8,128)(2,1)S(1)} %get-tuple-element.35), channel_id=1, source_target_pairs={{0,8},{4,12},{8,0},{12,4},{16,24},{20,28},{24,16},{28,20},{1,9},{5... | collective-permute-start | bytes 393224 | tf_op jit(solution)/shard_map/ppermute | solution.py:239
  21.4 10.5 %collective-permute-start.4 = (bf16[128,512]{1,0:T(8,128)(2,1)S(1)}, bf16[128,512]{1,0:T(8,128)(2,1)S(1)}, u32[]{:S(2)}, u32[]{:S(2)}) collective-permute-start(bf16[128,512]{1,0:T(8,128)(2,1)S(1)} %get-tuple-element.36), channel_id=1, source_target_pairs={{0,16},{4,20},{8,24},{12,28},{16,0},{20,4},{24,8},{28,12},{1,17},{... | collective-permute-start | bytes 393224 | tf_op jit(solution)/shard_map/ppermute | solution.py:239
  22.9 9.0 %collective-permute-start.5 = (bf16[128,512]{1,0:T(8,128)(2,1)S(1)}, bf16[128,512]{1,0:T(8,128)(2,1)S(1)}, u32[]{:S(2)}, u32[]{:S(2)}) collective-permute-start(bf16[128,512]{1,0:T(8,128)(2,1)S(1)} %get-tuple-element.37), channel_id=1, source_target_pairs={{0,24},{4,28},{8,16},{12,20},{16,8},{20,12},{24,0},{28,4},{1,25},{... | collective-permute-start | bytes 393224 | tf_op jit(solution)/shard_map/ppermute | solution.py:239
  28.0 6.1 %collective-permute-start.12 = (bf16[128,512]{1,0:T(8,128)(2,1)S(1)}, bf16[128,512]{1,0:T(8,128)(2,1)S(1)}, u32[]{:S(2)}, u32[]{:S(2)}) collective-permute-start(bf16[128,512]{1,0:T(8,128)(2,1)S(1)} %get-tuple-element.45), channel_id=1, source_target_pairs={{0,16},{4,20},{8,24},{12,28},{16,0},{20,4},{24,8},{28,12},{1,17},{... | collective-permute-start | bytes 393224 | tf_op jit(solution)/shard_map/ppermute | solution.py:239
  29.6 5.9 %collective-permute-start.13 = (bf16[128,512]{1,0:T(8,128)(2,1)S(1)}, bf16[128,512]{1,0:T(8,128)(2,1)S(1)}, u32[]{:S(2)}, u32[]{:S(2)}) collective-permute-start(bf16[128,512]{1,0:T(8,128)(2,1)S(1)} %get-tuple-element.46), channel_id=1, source_target_pairs={{0,24},{4,28},{8,16},{12,20},{16,8},{20,12},{24,0},{28,4},{1,25},{... | collective-permute-start | bytes 393224 | tf_op jit(solution)/shard_map/ppermute | solution.py:239
  31.3 5.0 %collective-permute-start.10 = (bf16[64,512]{1,0:T(8,128)(2,1)S(1)}, bf16[64,512]{1,0:T(8,128)(2,1)S(1)}, u32[]{:S(2)}, u32[]{:S(2)}) collective-permute-start(bf16[64,512]{1,0:T(8,128)(2,1)S(1)} %get-tuple-element.43), channel_id=1, source_target_pairs={{0,8},{4,12},{8,0},{12,4},{16,24},{20,28},{24,16},{28,20},{1,9},{5... | collective-permute-start | bytes 196616 | tf_op jit(solution)/shard_map/ppermute | solution.py:239
  31.9 4.4 %collective-permute-start.11 = (bf16[64,512]{1,0:T(8,128)(2,1)S(1)}, bf16[64,512]{1,0:T(8,128)(2,1)S(1)}, u32[]{:S(2)}, u32[]{:S(2)}) collective-permute-start(bf16[64,512]{1,0:T(8,128)(2,1)S(1)} %get-tuple-element.44), channel_id=1, source_target_pairs={{0,12},{4,8},{8,4},{12,0},{16,28},{20,24},{24,20},{28,16},{1,13},{... | collective-permute-start | bytes 196616 | tf_op jit(solution)/shard_map/ppermute | solution.py:239
  32.2 4.4 %collective-permute-start.6 = (bf16[256,512]{1,0:T(8,128)(2,1)S(1)}, bf16[256,512]{1,0:T(8,128)(2,1)S(1)}, u32[]{:S(2)}, u32[]{:S(2)}) collective-permute-start(bf16[256,512]{1,0:T(8,128)(2,1)S(1)} %shard_map.43), channel_id=1, source_target_pairs={{0,4},{4,0},{8,12},{12,8},{16,20},{20,16},{24,28},{28,24},{1,5},{5... | collective-permute-start | bytes 786440 | tf_op jit(solution)/shard_map/ppermute | solution.py:239
  35.5 1.5 %collective-permute-start.14 = (bf16[192,512]{1,0:T(8,128)(2,1)S(1)}, bf16[192,512]{1,0:T(8,128)(2,1)S(1)}, u32[]{:S(2)}, u32[]{:S(2)}) collective-permute-start(bf16[192,512]{1,0:T(8,128)(2,1)S(1)} %shard_map.52), channel_id=1, source_target_pairs={{0,4},{4,0},{8,12},{12,8},{16,20},{20,16},{24,28},{28,24},{1,5},{5... | collective-permute-start | bytes 589832 | tf_op jit(solution)/shard_map/ppermute | solution.py:239

commit v8 on v6

--- a/solution.py
+++ b/solution.py
@@ -352,8 +352,8 @@
         direct = second(n, (2, 3), full // outer, FREE, near)
         direct = {k: swap(direct[k], "grp", outer, k) for k in direct}
         passed, places = pass_on(n, came)
-        total = third_part(n, {2 * q: came[q] for q in slots}, FREE)
-        return [third_part(n, direct, LONG, total), passed], places
+        total = third_part(n, {2 * q: came[q] for q in slots[1:]}, FREE)
+        return [third_part(n, {0: came[0]} | direct, LONG, total), passed], places
 
     done = []
     for n, rows in enumerate(sizes):

time: 38.6 us -> 38.6 us (level)
  no operation moved by 1% of the time
where the time goes in v8:
time: 38.6 us; the launch traced here: 38.1 us
  starting transfers between devices  20.7 us (54%)
  waiting for transfers between devices  8.81 us (23%)
  Pallas kernels  8.5 us (22%)
    ppermute x15, starting transfers between devices, swap(): return lax.ppermute(piece, axis, [(i, i ^ k) for i in range(count)])  20.7 us
    ppermute x15, waiting for transfers between devices, swap(): return lax.ppermute(piece, axis, [(i, i ^ k) for i in range(count)])  8.81 us
    pallas_call x1, Pallas kernels, local(): call(functools.partial(forms_kernel, sizes, part1, rel1, part2, rel2), [H...  2.31 us
    pallas_call x1, Pallas kernels, local(): call(functools.partial(opening_kernel, part1, rel1, opening), [HBM] * 3,...  1.57 us
    pallas_call x1, Pallas kernels, local(): call(functools.partial(closing_kernel, last, places), [VM] * (1 + last +...  1.08 us
    pallas_call x4, Pallas kernels, second(): call(functools.partial(second_kernel, len(ins), slots), [VM] * (1 + len(i...  1.06 us
    pallas_call x3, Pallas kernels, third_part(): call(functools.partial(third_part_kernel, tuple(blocks), full // outer),...  0.97 us
    pallas_call x2, Pallas kernels, first_pieces(): call(functools.partial(first_kernel, part1, rel1, owners, len(shapes)), [...  0.86 us
  transfers between devices with their start and end apart: 15, of which 5 were waited for; matrix products, arithmetic and copies ran while one was open for 0% of the time, Pallas kernels for 15%

profile of v8, /device:TPU:0, one launch (start us, length us, event | category | flops | bytes accessed | tf_op | source)
XLA Modules:
  0.0 38.1 jit_solution(6710877288202100639)
XLA Ops:
  0.0 1.6 %shard_map.38 = (bf16[512,512]{1,0:T(8,128)(2,1)S(1)}, bf16[2,512,256]{2,1,0:T(8,128)(2,1)S(1)}, bf16[128,512]{1,0:T(8,128)(2,1)S(1)}) custom-call(bf16[2,1,1,1024,256]{4,3,2,1,0:T(8,128)(2,1)} %stem_ref.3, bf16[3,2,256,256]{3,2,1,0:T(8,128)(2,1)} %branches_ref.3, s32[3,256]{1,0:T(4,128)} %order_ref.3), custom_call_target="tpu_custom_call" | custom-call | flops 1 | bytes 1 | tf_op jit(solution)/shard_map/pallas_call | solution.py:291
  1.6 4.1 %collective-permute-start.1 = (bf16[128,512]{1,0:T(8,128)(2,1)S(1)}, bf16[128,512]{1,0:T(8,128)(2,1)S(1)}, u32[]{:S(2)}, u32[]{:S(2)}) collective-permute-start(bf16[128,512]{1,0:T(8,128)(2,1)S(1)} %get-tuple-element.32), channel_id=1, source_target_pairs={{0,2},{1,3},{2,0},{3,1},{4,6},{5,7},{6,4},{7,5},{8,10},{9,11},{10,... | collective-permute-start | bytes 393224 | tf_op jit(solution)/shard_map/ppermute | solution.py:239
  5.7 0.4 %shard_map.39 = (bf16[128,512]{1,0:T(8,128)(2,1)S(1)}, bf16[128,512]{1,0:T(8,128)(2,1)S(1)}, bf16[128,512]{1,0:T(8,128)(2,1)S(1)}) custom-call(bf16[2,512,256]{2,1,0:T(8,128)(2,1)S(1)} %get-tuple-element.28.block_ref, bf16[512,512]{1,0:T(8,128)(2,1)S(1)} %get-tuple-element.29.form_ref), custom_call_target="tpu_custom_call" | custom-call | flops 1 | bytes 1 | tf_op jit(solution)/shard_map/pallas_call | solution.py:277
  6.1 1.7 %collective-permute-start = (bf16[128,512]{1,0:T(8,128)(2,1)S(1)}, bf16[128,512]{1,0:T(8,128)(2,1)S(1)}, u32[]{:S(2)}, u32[]{:S(2)}) collective-permute-start(bf16[128,512]{1,0:T(8,128)(2,1)S(1)} %get-tuple-element.31), channel_id=1, source_target_pairs={{0,1},{1,0},{2,3},{3,2},{4,5},{5,4},{6,7},{7,6},{8,9},{9,8},{10,11... | collective-permute-start | bytes 393224 | tf_op jit(solution)/shard_map/ppermute | solution.py:239
  7.7 0.0 collective-permute-start.2
  7.7 2.3 %shard_map.37 = (bf16[512,512]{1,0:T(8,128)(2,1)S(1)}, bf16[512,512]{1,0:T(8,128)(2,1)S(1)}, bf16[2,512,256]{2,1,0:T(8,128)(2,1)S(1)}) custom-call(bf16[2,1,1,1024,256]{4,3,2,1,0:T(8,128)(2,1)} %stem_ref.3, bf16[3,2,256,256]{3,2,1,0:T(8,128)(2,1)} %branches_ref.3, s32[3,256]{1,0:T(4,128)} %order_ref.3), custom_call_target="tpu_custom_call" | custom-call | flops 1 | bytes 1 | tf_op jit(solution)/shard_map/pallas_call | solution.py:300
  10.1 3.6 %collective-permute-done.1.refs_2_.rest_1_ = bf16[128,512]{1,0:T(8,128)(2,1)S(1)} collective-permute-done((bf16[128,512]{1,0:T(8,128)(2,1)S(1)}, bf16[128,512]{1,0:T(8,128)(2,1)S(1)}, u32[]{:S(2)}, u32[]{:S(2)}) %collective-permute-start.1) | collective-permute-done | bytes 131104 | tf_op jit(solution)/shard_map/ppermute | solution.py:239
  13.6 0.5 %shard_map.44 = (bf16[128,512]{1,0:T(8,128)(2,1)S(1)}, bf16[128,512]{1,0:T(8,128)(2,1)S(1)}, bf16[128,512]{1,0:T(8,128)(2,1)S(1)}, bf16[128,512]{1,0:T(8,128)(2,1)S(1)}) custom-call(bf16[2,512,256]{2,1,0:T(8,128)(2,1)S(1)} %get-tuple-element.38.block_ref, bf16[512,512]{1,0:T(8,128)(2,1)S(1)} %get-tuple-element.29.form_ref, ...), custom_call_target="tpu_custom_call" | custom-call | flops 1 | bytes 1 | tf_op jit(solution)/shard_map/pallas_call | solution.py:277
  14.1 0.1 collective-permute-start.9
  14.2 3.6 %collective-permute-start.7 = (bf16[128,512]{1,0:T(8,128)(2,1)S(1)}, bf16[128,512]{1,0:T(8,128)(2,1)S(1)}, u32[]{:S(2)}, u32[]{:S(2)}) collective-permute-start(bf16[128,512]{1,0:T(8,128)(2,1)S(1)} %get-tuple-element.39), channel_id=1, source_target_pairs={{0,2},{1,3},{2,0},{3,1},{4,6},{5,7},{6,4},{7,5},{8,10},{9,11},{10,... | collective-permute-start | bytes 393224 | tf_op jit(solution)/shard_map/ppermute | solution.py:239
  17.8 0.8 %collective-permute-start.8 = (bf16[128,512]{1,0:T(8,128)(2,1)S(1)}, bf16[128,512]{1,0:T(8,128)(2,1)S(1)}, u32[]{:S(2)}, u32[]{:S(2)}) collective-permute-start(bf16[128,512]{1,0:T(8,128)(2,1)S(1)} %get-tuple-element.40), channel_id=1, source_target_pairs={{0,3},{1,2},{2,1},{3,0},{4,7},{5,6},{6,5},{7,4},{8,11},{9,10},{10,... | collective-permute-start | bytes 393224 | tf_op jit(solution)/shard_map/ppermute | solution.py:239
  18.6 0.0 collective-permute-done.refs_1_
  18.6 0.0 collective-permute-done.2.refs_3_
  18.6 0.4 %shard_map.40 = (bf16[128,512]{1,0:T(8,128)(2,1)S(1)}, bf16[128,512]{1,0:T(8,128)(2,1)S(1)}, bf16[128,512]{1,0:T(8,128)(2,1)S(1)}, bf16[128,512]{1,0:T(8,128)(2,1)S(1)}) custom-call(bf16[512,512]{1,0:T(8,128)(2,1)S(1)} %get-tuple-element.27.form_ref.rest_0_, bf16[128,512]{1,0:T(8,128)(2,1)S(1)} %get-tuple-element.30.refs_0_, ...), custom_call_target="tpu_custom_call" | custom-call | flops 1 | bytes 1 | tf_op jit(solution)/shard_map/pallas_call | solution.py:314
  19.0 2.2 %collective-permute-start.3 = (bf16[128,512]{1,0:T(8,128)(2,1)S(1)}, bf16[128,512]{1,0:T(8,128)(2,1)S(1)}, u32[]{:S(2)}, u32[]{:S(2)}) collective-permute-start(bf16[128,512]{1,0:T(8,128)(2,1)S(1)} %get-tuple-element.35), channel_id=1, source_target_pairs={{0,8},{4,12},{8,0},{12,4},{16,24},{20,28},{24,16},{28,20},{1,9},{5... | collective-permute-start | bytes 393224 | tf_op jit(solution)/shard_map/ppermute | solution.py:239
  21.2 1.5 %collective-permute-start.4 = (bf16[128,512]{1,0:T(8,128)(2,1)S(1)}, bf16[128,512]{1,0:T(8,128)(2,1)S(1)}, u32[]{:S(2)}, u32[]{:S(2)}) collective-permute-start(bf16[128,512]{1,0:T(8,128)(2,1)S(1)} %get-tuple-element.36), channel_id=1, source_target_pairs={{0,16},{4,20},{8,24},{12,28},{16,0},{20,4},{24,8},{28,12},{1,17},{... | collective-permute-start | bytes 393224 | tf_op jit(solution)/shard_map/ppermute | solution.py:239
  22.7 0.0 collective-permute-done.9.refs_1_
  22.7 1.4 %collective-permute-start.5 = (bf16[128,512]{1,0:T(8,128)(2,1)S(1)}, bf16[128,512]{1,0:T(8,128)(2,1)S(1)}, u32[]{:S(2)}, u32[]{:S(2)}) collective-permute-start(bf16[128,512]{1,0:T(8,128)(2,1)S(1)} %get-tuple-element.37), channel_id=1, source_target_pairs={{0,24},{4,28},{8,16},{12,20},{16,8},{20,12},{24,0},{28,4},{1,25},{... | collective-permute-start | bytes 393224 | tf_op jit(solution)/shard_map/ppermute | solution.py:239
  24.1 0.3 shard_map.45.refs_2_
  24.4 3.4 %collective-permute-done.7.refs_0_ = bf16[128,512]{1,0:T(8,128)(2,1)S(1)} collective-permute-done((bf16[128,512]{1,0:T(8,128)(2,1)S(1)}, bf16[128,512]{1,0:T(8,128)(2,1)S(1)}, u32[]{:S(2)}, u32[]{:S(2)}) %collective-permute-start.7) | collective-permute-done | bytes 131104 | tf_op jit(solution)/shard_map/ppermute | solution.py:239
  27.8 0.0 collective-permute-done.8.refs_1_
  27.8 0.2 shard_map.48
  28.0 1.6 %collective-permute-start.12 = (bf16[128,512]{1,0:T(8,128)(2,1)S(1)}, bf16[128,512]{1,0:T(8,128)(2,1)S(1)}, u32[]{:S(2)}, u32[]{:S(2)}) collective-permute-start(bf16[128,512]{1,0:T(8,128)(2,1)S(1)} %get-tuple-element.45), channel_id=1, source_target_pairs={{0,16},{4,20},{8,24},{12,28},{16,0},{20,4},{24,8},{28,12},{1,17},{... | collective-permute-start | bytes 393224 | tf_op jit(solution)/shard_map/ppermute | solution.py:239
  29.6 1.4 %collective-permute-start.13 = (bf16[128,512]{1,0:T(8,128)(2,1)S(1)}, bf16[128,512]{1,0:T(8,128)(2,1)S(1)}, u32[]{:S(2)}, u32[]{:S(2)}) collective-permute-start(bf16[128,512]{1,0:T(8,128)(2,1)S(1)} %get-tuple-element.46), channel_id=1, source_target_pairs={{0,24},{4,28},{8,16},{12,20},{16,8},{20,12},{24,0},{28,4},{1,25},{... | collective-permute-start | bytes 393224 | tf_op jit(solution)/shard_map/ppermute | solution.py:239
  31.1 0.2 shard_map.47
  31.3 0.0 collective-permute-done.3.refs_1_
  31.3 0.6 %collective-permute-start.10 = (bf16[64,512]{1,0:T(8,128)(2,1)S(1)}, bf16[64,512]{1,0:T(8,128)(2,1)S(1)}, u32[]{:S(2)}, u32[]{:S(2)}) collective-permute-start(bf16[64,512]{1,0:T(8,128)(2,1)S(1)} %get-tuple-element.43), channel_id=1, source_target_pairs={{0,8},{4,12},{8,0},{12,4},{16,24},{20,28},{24,16},{28,20},{1,9},{5... | collective-permute-start | bytes 196616 | tf_op jit(solution)/shard_map/ppermute | solution.py:239
  31.9 0.0 collective-permute-done.4.refs_2_
  31.9 0.0 collective-permute-start.11
  31.9 0.0 collective-permute-done.5.refs_3_
  31.9 0.3 shard_map.41.refs_4_.refs_0_
  32.2 1.7 %collective-permute-start.6 = (bf16[256,512]{1,0:T(8,128)(2,1)S(1)}, bf16[256,512]{1,0:T(8,128)(2,1)S(1)}, u32[]{:S(2)}, u32[]{:S(2)}) collective-permute-start(bf16[256,512]{1,0:T(8,128)(2,1)S(1)} %shard_map.42), channel_id=1, source_target_pairs={{0,4},{4,0},{8,12},{12,8},{16,20},{20,16},{24,28},{28,24},{1,5},{5... | collective-permute-start | bytes 786440 | tf_op jit(solution)/shard_map/ppermute | solution.py:239
  33.9 0.2 shard_map.46.refs_0_
  34.1 0.0 collective-permute-done.12.refs_0_.refs_1_
  34.1 1.4 %collective-permute-done.13.refs_1_.refs_2_ = bf16[128,512]{1,0:T(8,128)(2,1)S(1)} collective-permute-done((bf16[128,512]{1,0:T(8,128)(2,1)S(1)}, bf16[128,512]{1,0:T(8,128)(2,1)S(1)}, u32[]{:S(2)}, u32[]{:S(2)}) %collective-permute-start.13) | collective-permute-done | bytes 131104 | tf_op jit(solution)/shard_map/ppermute | solution.py:239
  35.5 0.1 collective-permute-start.14
  35.6 0.3 shard_map.49.refs_3_
  35.9 0.3 collective-permute-done.10.refs_1_
  36.3 0.0 collective-permute-done.11.refs_2_
  36.3 0.3 shard_map.50.refs_1_
  36.6 0.0 collective-permute-done.6.refs_1_
  36.6 0.3 shard_map.43.refs_0_
  36.9 0.1 collective-permute-done.14.refs_2_
  37.0 1.1 %shard_map.52 = bf16[2,1,1,1024,256]{4,3,2,1,0:T(8,128)(2,1)} custom-call(bf16[512,512]{1,0:T(8,128)(2,1)S(1)} %get-tuple-element.26.form_ref, bf16[2,512,256]{2,1,0:T(8,128)(2,1)S(1)} %shard_map.43.refs_0_, f32[512,512]{1,0:T(8,128)S(1)} %shard_map.50.refs_1_, bf16[192,512]{1,0:T(8,128)(2,1)S(1)} %collective-permute-done.14.refs_2_), custom_call_target="tpu_custom_call" | custom-call | flops 1 | bytes 1 | tf_op jit(solution)/shard_map/pallas_call | solution.py:368
  (2 shorter events, 0.0 us)
Async XLA Ops:
  1.6 12.1 %collective-permute-start.1 = (bf16[128,512]{1,0:T(8,128)(2,1)S(1)}, bf16[128,512]{1,0:T(8,128)(2,1)S(1)}, u32[]{:S(2)}, u32[]{:S(2)}) collective-permute-start(bf16[128,512]{1,0:T(8,128)(2,1)S(1)} %get-tuple-element.32), channel_id=1, source_target_pairs={{0,2},{1,3},{2,0},{3,1},{4,6},{5,7},{6,4},{7,5},{8,10},{9,11},{10,... | collective-permute-start | bytes 393224 | tf_op jit(solution)/shard_map/ppermute | solution.py:239
  6.1 12.5 %collective-permute-start = (bf16[128,512]{1,0:T(8,128)(2,1)S(1)}, bf16[128,512]{1,0:T(8,128)(2,1)S(1)}, u32[]{:S(2)}, u32[]{:S(2)}) collective-permute-start(bf16[128,512]{1,0:T(8,128)(2,1)S(1)} %get-tuple-element.31), channel_id=1, source_target_pairs={{0,1},{1,0},{2,3},{3,2},{4,5},{5,4},{6,7},{7,6},{8,9},{9,8},{10,11... | collective-permute-start | bytes 393224 | tf_op jit(solution)/shard_map/ppermute | solution.py:239
  7.7 10.9 %collective-permute-start.2 = (bf16[128,512]{1,0:T(8,128)(2,1)S(1)}, bf16[128,512]{1,0:T(8,128)(2,1)S(1)}, u32[]{:S(2)}, u32[]{:S(2)}) collective-permute-start(bf16[128,512]{1,0:T(8,128)(2,1)S(1)} %get-tuple-element.33), channel_id=1, source_target_pairs={{0,3},{1,2},{2,1},{3,0},{4,7},{5,6},{6,5},{7,4},{8,11},{9,10},{10,... | collective-permute-start | bytes 393224 | tf_op jit(solution)/shard_map/ppermute | solution.py:239
  14.1 8.6 %collective-permute-start.9 = (bf16[128,512]{1,0:T(8,128)(2,1)S(1)}, bf16[128,512]{1,0:T(8,128)(2,1)S(1)}, u32[]{:S(2)}, u32[]{:S(2)}) collective-permute-start(bf16[128,512]{1,0:T(8,128)(2,1)S(1)} %get-tuple-element.42), channel_id=1, source_target_pairs={{0,1},{1,0},{2,3},{3,2},{4,5},{5,4},{6,7},{7,6},{8,9},{9,8},{10,11... | collective-permute-start | bytes 393224 | tf_op jit(solution)/shard_map/ppermute | solution.py:239
  14.2 13.6 %collective-permute-start.7 = (bf16[128,512]{1,0:T(8,128)(2,1)S(1)}, bf16[128,512]{1,0:T(8,128)(2,1)S(1)}, u32[]{:S(2)}, u32[]{:S(2)}) collective-permute-start(bf16[128,512]{1,0:T(8,128)(2,1)S(1)} %get-tuple-element.39), channel_id=1, source_target_pairs={{0,2},{1,3},{2,0},{3,1},{4,6},{5,7},{6,4},{7,5},{8,10},{9,11},{10,... | collective-permute-start | bytes 393224 | tf_op jit(solution)/shard_map/ppermute | solution.py:239
  17.8 10.0 %collective-permute-start.8 = (bf16[128,512]{1,0:T(8,128)(2,1)S(1)}, bf16[128,512]{1,0:T(8,128)(2,1)S(1)}, u32[]{:S(2)}, u32[]{:S(2)}) collective-permute-start(bf16[128,512]{1,0:T(8,128)(2,1)S(1)} %get-tuple-element.40), channel_id=1, source_target_pairs={{0,3},{1,2},{2,1},{3,0},{4,7},{5,6},{6,5},{7,4},{8,11},{9,10},{10,... | collective-permute-start | bytes 393224 | tf_op jit(solution)/shard_map/ppermute | solution.py:239
  19.0 12.2 %collective-permute-start.3 = (bf16[128,512]{1,0:T(8,128)(2,1)S(1)}, bf16[128,512]{1,0:T(8,128)(2,1)S(1)}, u32[]{:S(2)}, u32[]{:S(2)}) collective-permute-start(bf16[128,512]{1,0:T(8,128)(2,1)S(1)} %get-tuple-element.35), channel_id=1, source_target_pairs={{0,8},{4,12},{8,0},{12,4},{16,24},{20,28},{24,16},{28,20},{1,9},{5... | collective-permute-start | bytes 393224 | tf_op jit(solution)/shard_map/ppermute | solution.py:239
  21.2 10.6 %collective-permute-start.4 = (bf16[128,512]{1,0:T(8,128)(2,1)S(1)}, bf16[128,512]{1,0:T(8,128)(2,1)S(1)}, u32[]{:S(2)}, u32[]{:S(2)}) collective-permute-start(bf16[128,512]{1,0:T(8,128)(2,1)S(1)} %get-tuple-element.36), channel_id=1, source_target_pairs={{0,16},{4,20},{8,24},{12,28},{16,0},{20,4},{24,8},{28,12},{1,17},{... | collective-permute-start | bytes 393224 | tf_op jit(solution)/shard_map/ppermute | solution.py:239
  22.7 9.1 %collective-permute-start.5 = (bf16[128,512]{1,0:T(8,128)(2,1)S(1)}, bf16[128,512]{1,0:T(8,128)(2,1)S(1)}, u32[]{:S(2)}, u32[]{:S(2)}) collective-permute-start(bf16[128,512]{1,0:T(8,128)(2,1)S(1)} %get-tuple-element.37), channel_id=1, source_target_pairs={{0,24},{4,28},{8,16},{12,20},{16,8},{20,12},{24,0},{28,4},{1,25},{... | collective-permute-start | bytes 393224 | tf_op jit(solution)/shard_map/ppermute | solution.py:239
  28.0 6.1 %collective-permute-start.12 = (bf16[128,512]{1,0:T(8,128)(2,1)S(1)}, bf16[128,512]{1,0:T(8,128)(2,1)S(1)}, u32[]{:S(2)}, u32[]{:S(2)}) collective-permute-start(bf16[128,512]{1,0:T(8,128)(2,1)S(1)} %get-tuple-element.45), channel_id=1, source_target_pairs={{0,16},{4,20},{8,24},{12,28},{16,0},{20,4},{24,8},{28,12},{1,17},{... | collective-permute-start | bytes 393224 | tf_op jit(solution)/shard_map/ppermute | solution.py:239
  29.6 5.9 %collective-permute-start.13 = (bf16[128,512]{1,0:T(8,128)(2,1)S(1)}, bf16[128,512]{1,0:T(8,128)(2,1)S(1)}, u32[]{:S(2)}, u32[]{:S(2)}) collective-permute-start(bf16[128,512]{1,0:T(8,128)(2,1)S(1)} %get-tuple-element.46), channel_id=1, source_target_pairs={{0,24},{4,28},{8,16},{12,20},{16,8},{20,12},{24,0},{28,4},{1,25},{... | collective-permute-start | bytes 393224 | tf_op jit(solution)/shard_map/ppermute | solution.py:239
  31.3 5.0 %collective-permute-start.10 = (bf16[64,512]{1,0:T(8,128)(2,1)S(1)}, bf16[64,512]{1,0:T(8,128)(2,1)S(1)}, u32[]{:S(2)}, u32[]{:S(2)}) collective-permute-start(bf16[64,512]{1,0:T(8,128)(2,1)S(1)} %get-tuple-element.43), channel_id=1, source_target_pairs={{0,8},{4,12},{8,0},{12,4},{16,24},{20,28},{24,16},{28,20},{1,9},{5... | collective-permute-start | bytes 196616 | tf_op jit(solution)/shard_map/ppermute | solution.py:239
  31.9 4.4 %collective-permute-start.11 = (bf16[64,512]{1,0:T(8,128)(2,1)S(1)}, bf16[64,512]{1,0:T(8,128)(2,1)S(1)}, u32[]{:S(2)}, u32[]{:S(2)}) collective-permute-start(bf16[64,512]{1,0:T(8,128)(2,1)S(1)} %get-tuple-element.44), channel_id=1, source_target_pairs={{0,12},{4,8},{8,4},{12,0},{16,28},{20,24},{24,20},{28,16},{1,13},{... | collective-permute-start | bytes 196616 | tf_op jit(solution)/shard_map/ppermute | solution.py:239
  32.2 4.4 %collective-permute-start.6 = (bf16[256,512]{1,0:T(8,128)(2,1)S(1)}, bf16[256,512]{1,0:T(8,128)(2,1)S(1)}, u32[]{:S(2)}, u32[]{:S(2)}) collective-permute-start(bf16[256,512]{1,0:T(8,128)(2,1)S(1)} %shard_map.42), channel_id=1, source_target_pairs={{0,4},{4,0},{8,12},{12,8},{16,20},{20,16},{24,28},{28,24},{1,5},{5... | collective-permute-start | bytes 786440 | tf_op jit(solution)/shard_map/ppermute | solution.py:239
  35.5 1.5 %collective-permute-start.14 = (bf16[192,512]{1,0:T(8,128)(2,1)S(1)}, bf16[192,512]{1,0:T(8,128)(2,1)S(1)}, u32[]{:S(2)}, u32[]{:S(2)}) collective-permute-start(bf16[192,512]{1,0:T(8,128)(2,1)S(1)} %shard_map.51), channel_id=1, source_target_pairs={{0,4},{4,0},{8,12},{12,8},{16,20},{20,16},{24,28},{28,24},{1,5},{5... | collective-permute-start | bytes 589832 | tf_op jit(solution)/shard_map/ppermute | solution.py:239

commit v9 on v6

--- a/solution.py
+++ b/solution.py
@@ -102,15 +102,17 @@
     outs, (branch, order, sem) = rest[:-3], rest[-3:]
     copies = [
         pltpu.make_async_copy(order_ref, order, sem.at[0]),
-        pltpu.make_async_copy(branches_ref.at[0], branch, sem.at[1]),
+        pltpu.make_async_copy(branches_ref.at[0, 0], branch.at[0], sem.at[1]),
+        pltpu.make_async_copy(branches_ref.at[0, 1], branch.at[1], sem.at[3]),
         pltpu.make_async_copy(stem_ref.at[:, 0, 0, pl.ds(0, block_ref.shape[1])], block_ref, sem.at[2]),
     ]
     for copy in copies:
         copy.start()
     copies[0].wait()
     copies[1].wait()
+    copies[2].wait()
     form_ref[...] = first_form(branch, order[0:1, :])
-    copies[2].wait()
+    copies[3].wait()
     put_first(form_ref, block_ref, part, place_of("mem", relative), owners, outs)
 
 
@@ -291,7 +293,7 @@
     form0, block, *made = call(
         functools.partial(opening_kernel, part1, rel1, opening),
         [HBM] * 3, [form_shape, shape(2, sizes[0], width)] + shapes, [VM] * (2 + len(shapes)), FREE,
-        [pltpu.VMEM(branches.shape[1:], BF16), order_scratch, pltpu.SemaphoreType.DMA((3,))],
+        [pltpu.VMEM(branches.shape[1:], BF16), order_scratch, pltpu.SemaphoreType.DMA((4,))],
     )(stem, branches, mode_order)
     pieces = dict(zip(opening, made))
     if rel1:

time: 38.6 us -> 38.7 us (level)
  no operation moved by 1% of the time
where the time goes in v9:
time: 38.7 us; the launch traced here: 38.1 us
  starting transfers between devices  20.7 us (53%)
  waiting for transfers between devices  8.8 us (23%)
  Pallas kernels  8.53 us (22%)
    ppermute x15, starting transfers between devices, swap(): return lax.ppermute(piece, axis, [(i, i ^ k) for i in range(count)])  20.7 us
    ppermute x15, waiting for transfers between devices, swap(): return lax.ppermute(piece, axis, [(i, i ^ k) for i in range(count)])  8.8 us
    pallas_call x1, Pallas kernels, local(): call(functools.partial(forms_kernel, sizes, part1, rel1, part2, rel2), [H...  2.31 us
    pallas_call x1, Pallas kernels, local(): call(functools.partial(opening_kernel, part1, rel1, opening), [HBM] * 3,...  1.59 us
    pallas_call x1, Pallas kernels, local(): call(functools.partial(closing_kernel, last, places), [VM] * (1 + last +...  1.08 us
    pallas_call x4, Pallas kernels, second(): call(functools.partial(second_kernel, len(ins), slots), [VM] * (1 + len(i...  1.06 us
    pallas_call x3, Pallas kernels, third_part(): call(functools.partial(third_part_kernel, tuple(blocks), full // outer),...  0.97 us
    pallas_call x2, Pallas kernels, first_pieces(): call(functools.partial(first_kernel, part1, rel1, owners, len(shapes)), [...  0.86 us
  transfers between devices with their start and end apart: 15, of which 5 were waited for; matrix products, arithmetic and copies ran while one was open for 0% of the time, Pallas kernels for 15%

profile of v9, /device:TPU:0, one launch (start us, length us, event | category | flops | bytes accessed | tf_op | source)
XLA Modules:
  0.0 38.1 jit_solution(11865124058519069686)
XLA Ops:
  0.0 1.6 %shard_map.38 = (bf16[512,512]{1,0:T(8,128)(2,1)S(1)}, bf16[2,512,256]{2,1,0:T(8,128)(2,1)S(1)}, bf16[128,512]{1,0:T(8,128)(2,1)S(1)}) custom-call(bf16[2,1,1,1024,256]{4,3,2,1,0:T(8,128)(2,1)} %stem_ref.3, bf16[3,2,256,256]{3,2,1,0:T(8,128)(2,1)} %branches_ref.3, s32[3,256]{1,0:T(4,128)} %order_ref.3), custom_call_target="tpu_custom_call" | custom-call | flops 1 | bytes 1 | tf_op jit(solution)/shard_map/pallas_call | solution.py:293
  1.6 4.1 %collective-permute-start.1 = (bf16[128,512]{1,0:T(8,128)(2,1)S(1)}, bf16[128,512]{1,0:T(8,128)(2,1)S(1)}, u32[]{:S(2)}, u32[]{:S(2)}) collective-permute-start(bf16[128,512]{1,0:T(8,128)(2,1)S(1)} %get-tuple-element.32), channel_id=1, source_target_pairs={{0,2},{1,3},{2,0},{3,1},{4,6},{5,7},{6,4},{7,5},{8,10},{9,11},{10,... | collective-permute-start | bytes 393224 | tf_op jit(solution)/shard_map/ppermute | solution.py:241
  5.7 0.4 %shard_map.39 = (bf16[128,512]{1,0:T(8,128)(2,1)S(1)}, bf16[128,512]{1,0:T(8,128)(2,1)S(1)}, bf16[128,512]{1,0:T(8,128)(2,1)S(1)}) custom-call(bf16[2,512,256]{2,1,0:T(8,128)(2,1)S(1)} %get-tuple-element.28.block_ref, bf16[512,512]{1,0:T(8,128)(2,1)S(1)} %get-tuple-element.29.form_ref), custom_call_target="tpu_custom_call" | custom-call | flops 1 | bytes 1 | tf_op jit(solution)/shard_map/pallas_call | solution.py:279
  6.1 1.7 %collective-permute-start = (bf16[128,512]{1,0:T(8,128)(2,1)S(1)}, bf16[128,512]{1,0:T(8,128)(2,1)S(1)}, u32[]{:S(2)}, u32[]{:S(2)}) collective-permute-start(bf16[128,512]{1,0:T(8,128)(2,1)S(1)} %get-tuple-element.31), channel_id=1, source_target_pairs={{0,1},{1,0},{2,3},{3,2},{4,5},{5,4},{6,7},{7,6},{8,9},{9,8},{10,11... | collective-permute-start | bytes 393224 | tf_op jit(solution)/shard_map/ppermute | solution.py:241
  7.8 0.0 collective-permute-start.2
  7.8 2.3 %shard_map.37 = (bf16[512,512]{1,0:T(8,128)(2,1)S(1)}, bf16[512,512]{1,0:T(8,128)(2,1)S(1)}, bf16[2,512,256]{2,1,0:T(8,128)(2,1)S(1)}) custom-call(bf16[2,1,1,1024,256]{4,3,2,1,0:T(8,128)(2,1)} %stem_ref.3, bf16[3,2,256,256]{3,2,1,0:T(8,128)(2,1)} %branches_ref.3, s32[3,256]{1,0:T(4,128)} %order_ref.3), custom_call_target="tpu_custom_call" | custom-call | flops 1 | bytes 1 | tf_op jit(solution)/shard_map/pallas_call | solution.py:302
  10.1 3.6 %collective-permute-done.1.refs_2_.rest_1_ = bf16[128,512]{1,0:T(8,128)(2,1)S(1)} collective-permute-done((bf16[128,512]{1,0:T(8,128)(2,1)S(1)}, bf16[128,512]{1,0:T(8,128)(2,1)S(1)}, u32[]{:S(2)}, u32[]{:S(2)}) %collective-permute-start.1) | collective-permute-done | bytes 131104 | tf_op jit(solution)/shard_map/ppermute | solution.py:241
  13.7 0.5 %shard_map.44 = (bf16[128,512]{1,0:T(8,128)(2,1)S(1)}, bf16[128,512]{1,0:T(8,128)(2,1)S(1)}, bf16[128,512]{1,0:T(8,128)(2,1)S(1)}, bf16[128,512]{1,0:T(8,128)(2,1)S(1)}) custom-call(bf16[2,512,256]{2,1,0:T(8,128)(2,1)S(1)} %get-tuple-element.38.block_ref, bf16[512,512]{1,0:T(8,128)(2,1)S(1)} %get-tuple-element.29.form_ref, ...), custom_call_target="tpu_custom_call" | custom-call | flops 1 | bytes 1 | tf_op jit(solution)/shard_map/pallas_call | solution.py:279
  14.1 0.1 collective-permute-start.9
  14.2 3.6 %collective-permute-start.7 = (bf16[128,512]{1,0:T(8,128)(2,1)S(1)}, bf16[128,512]{1,0:T(8,128)(2,1)S(1)}, u32[]{:S(2)}, u32[]{:S(2)}) collective-permute-start(bf16[128,512]{1,0:T(8,128)(2,1)S(1)} %get-tuple-element.39), channel_id=1, source_target_pairs={{0,2},{1,3},{2,0},{3,1},{4,6},{5,7},{6,4},{7,5},{8,10},{9,11},{10,... | collective-permute-start | bytes 393224 | tf_op jit(solution)/shard_map/ppermute | solution.py:241
  17.8 0.8 %collective-permute-start.8 = (bf16[128,512]{1,0:T(8,128)(2,1)S(1)}, bf16[128,512]{1,0:T(8,128)(2,1)S(1)}, u32[]{:S(2)}, u32[]{:S(2)}) collective-permute-start(bf16[128,512]{1,0:T(8,128)(2,1)S(1)} %get-tuple-element.40), channel_id=1, source_target_pairs={{0,3},{1,2},{2,1},{3,0},{4,7},{5,6},{6,5},{7,4},{8,11},{9,10},{10,... | collective-permute-start | bytes 393224 | tf_op jit(solution)/shard_map/ppermute | solution.py:241
  18.6 0.0 collective-permute-done.refs_1_
  18.6 0.0 collective-permute-done.2.refs_3_
  18.6 0.4 %shard_map.40 = (bf16[128,512]{1,0:T(8,128)(2,1)S(1)}, bf16[128,512]{1,0:T(8,128)(2,1)S(1)}, bf16[128,512]{1,0:T(8,128)(2,1)S(1)}, bf16[128,512]{1,0:T(8,128)(2,1)S(1)}) custom-call(bf16[512,512]{1,0:T(8,128)(2,1)S(1)} %get-tuple-element.27.form_ref.rest_0_, bf16[128,512]{1,0:T(8,128)(2,1)S(1)} %get-tuple-element.30.refs_0_, ...), custom_call_target="tpu_custom_call" | custom-call | flops 1 | bytes 1 | tf_op jit(solution)/shard_map/pallas_call | solution.py:316
  19.1 2.2 %collective-permute-start.3 = (bf16[128,512]{1,0:T(8,128)(2,1)S(1)}, bf16[128,512]{1,0:T(8,128)(2,1)S(1)}, u32[]{:S(2)}, u32[]{:S(2)}) collective-permute-start(bf16[128,512]{1,0:T(8,128)(2,1)S(1)} %get-tuple-element.35), channel_id=1, source_target_pairs={{0,8},{4,12},{8,0},{12,4},{16,24},{20,28},{24,16},{28,20},{1,9},{5... | collective-permute-start | bytes 393224 | tf_op jit(solution)/shard_map/ppermute | solution.py:241
  21.2 1.5 %collective-permute-start.4 = (bf16[128,512]{1,0:T(8,128)(2,1)S(1)}, bf16[128,512]{1,0:T(8,128)(2,1)S(1)}, u32[]{:S(2)}, u32[]{:S(2)}) collective-permute-start(bf16[128,512]{1,0:T(8,128)(2,1)S(1)} %get-tuple-element.36), channel_id=1, source_target_pairs={{0,16},{4,20},{8,24},{12,28},{16,0},{20,4},{24,8},{28,12},{1,17},{... | collective-permute-start | bytes 393224 | tf_op jit(solution)/shard_map/ppermute | solution.py:241
  22.8 0.0 collective-permute-done.9.refs_1_
  22.8 1.4 %collective-permute-start.5 = (bf16[128,512]{1,0:T(8,128)(2,1)S(1)}, bf16[128,512]{1,0:T(8,128)(2,1)S(1)}, u32[]{:S(2)}, u32[]{:S(2)}) collective-permute-start(bf16[128,512]{1,0:T(8,128)(2,1)S(1)} %get-tuple-element.37), channel_id=1, source_target_pairs={{0,24},{4,28},{8,16},{12,20},{16,8},{20,12},{24,0},{28,4},{1,25},{... | collective-permute-start | bytes 393224 | tf_op jit(solution)/shard_map/ppermute | solution.py:241
  24.1 0.3 shard_map.45.refs_2_
  24.4 3.4 %collective-permute-done.7.refs_0_ = bf16[128,512]{1,0:T(8,128)(2,1)S(1)} collective-permute-done((bf16[128,512]{1,0:T(8,128)(2,1)S(1)}, bf16[128,512]{1,0:T(8,128)(2,1)S(1)}, u32[]{:S(2)}, u32[]{:S(2)}) %collective-permute-start.7) | collective-permute-done | bytes 131104 | tf_op jit(solution)/shard_map/ppermute | solution.py:241
  27.8 0.0 collective-permute-done.8.refs_1_
  27.8 0.2 shard_map.48
  28.0 1.6 %collective-permute-start.12 = (bf16[128,512]{1,0:T(8,128)(2,1)S(1)}, bf16[128,512]{1,0:T(8,128)(2,1)S(1)}, u32[]{:S(2)}, u32[]{:S(2)}) collective-permute-start(bf16[128,512]{1,0:T(8,128)(2,1)S(1)} %get-tuple-element.45), channel_id=1, source_target_pairs={{0,16},{4,20},{8,24},{12,28},{16,0},{20,4},{24,8},{28,12},{1,17},{... | collective-permute-start | bytes 393224 | tf_op jit(solution)/shard_map/ppermute | solution.py:241
  29.7 1.4 %collective-permute-start.13 = (bf16[128,512]{1,0:T(8,128)(2,1)S(1)}, bf16[128,512]{1,0:T(8,128)(2,1)S(1)}, u32[]{:S(2)}, u32[]{:S(2)}) collective-permute-start(bf16[128,512]{1,0:T(8,128)(2,1)S(1)} %get-tuple-element.46), channel_id=1, source_target_pairs={{0,24},{4,28},{8,16},{12,20},{16,8},{20,12},{24,0},{28,4},{1,25},{... | collective-permute-start | bytes 393224 | tf_op jit(solution)/shard_map/ppermute | solution.py:241
  31.1 0.2 shard_map.46
  31.3 0.0 collective-permute-done.3.refs_1_
  31.3 0.6 %collective-permute-start.10 = (bf16[64,512]{1,0:T(8,128)(2,1)S(1)}, bf16[64,512]{1,0:T(8,128)(2,1)S(1)}, u32[]{:S(2)}, u32[]{:S(2)}) collective-permute-start(bf16[64,512]{1,0:T(8,128)(2,1)S(1)} %get-tuple-element.43), channel_id=1, source_target_pairs={{0,8},{4,12},{8,0},{12,4},{16,24},{20,28},{24,16},{28,20},{1,9},{5... | collective-permute-start | bytes 196616 | tf_op jit(solution)/shard_map/ppermute | solution.py:241
  31.9 0.0 collective-permute-done.4.refs_2_
  31.9 0.0 collective-permute-start.11
  31.9 0.0 collective-permute-done.5.refs_3_
  31.9 0.3 shard_map.41.refs_4_.refs_0_
  32.2 1.7 %collective-permute-start.6 = (bf16[256,512]{1,0:T(8,128)(2,1)S(1)}, bf16[256,512]{1,0:T(8,128)(2,1)S(1)}, u32[]{:S(2)}, u32[]{:S(2)}) collective-permute-start(bf16[256,512]{1,0:T(8,128)(2,1)S(1)} %shard_map.42), channel_id=1, source_target_pairs={{0,4},{4,0},{8,12},{12,8},{16,20},{20,16},{24,28},{28,24},{1,5},{5... | collective-permute-start | bytes 786440 | tf_op jit(solution)/shard_map/ppermute | solution.py:241
  33.9 0.2 shard_map.47.refs_0_
  34.1 0.0 collective-permute-done.12.refs_1_
  34.1 1.4 %collective-permute-done.13.refs_2_ = bf16[128,512]{1,0:T(8,128)(2,1)S(1)} collective-permute-done((bf16[128,512]{1,0:T(8,128)(2,1)S(1)}, bf16[128,512]{1,0:T(8,128)(2,1)S(1)}, u32[]{:S(2)}, u32[]{:S(2)}) %collective-permute-start.13) | collective-permute-done | bytes 131104 | tf_op jit(solution)/shard_map/ppermute | solution.py:241
  35.5 0.1 collective-permute-start.14
  35.6 0.3 shard_map.49.refs_2_
  36.0 0.3 collective-permute-done.10.refs_0_
  36.3 0.0 collective-permute-done.11.refs_1_
  36.3 0.3 shard_map.50.refs_1_
  36.6 0.0 collective-permute-done.6.refs_1_
  36.6 0.3 shard_map.43.refs_0_
  36.9 0.1 collective-permute-done.14.refs_2_
  37.1 1.1 %shard_map.52 = bf16[2,1,1,1024,256]{4,3,2,1,0:T(8,128)(2,1)} custom-call(bf16[512,512]{1,0:T(8,128)(2,1)S(1)} %get-tuple-element.26.form_ref, bf16[2,512,256]{2,1,0:T(8,128)(2,1)S(1)} %shard_map.43.refs_0_, f32[512,512]{1,0:T(8,128)S(1)} %shard_map.50.refs_1_, bf16[192,512]{1,0:T(8,128)(2,1)S(1)} %collective-permute-done.14.refs_2_), custom_call_target="tpu_custom_call" | custom-call | flops 1 | bytes 1 | tf_op jit(solution)/shard_map/pallas_call | solution.py:370
  (2 shorter events, 0.0 us)
Async XLA Ops:
  1.6 12.1 %collective-permute-start.1 = (bf16[128,512]{1,0:T(8,128)(2,1)S(1)}, bf16[128,512]{1,0:T(8,128)(2,1)S(1)}, u32[]{:S(2)}, u32[]{:S(2)}) collective-permute-start(bf16[128,512]{1,0:T(8,128)(2,1)S(1)} %get-tuple-element.32), channel_id=1, source_target_pairs={{0,2},{1,3},{2,0},{3,1},{4,6},{5,7},{6,4},{7,5},{8,10},{9,11},{10,... | collective-permute-start | bytes 393224 | tf_op jit(solution)/shard_map/ppermute | solution.py:241
  6.1 12.5 %collective-permute-start = (bf16[128,512]{1,0:T(8,128)(2,1)S(1)}, bf16[128,512]{1,0:T(8,128)(2,1)S(1)}, u32[]{:S(2)}, u32[]{:S(2)}) collective-permute-start(bf16[128,512]{1,0:T(8,128)(2,1)S(1)} %get-tuple-element.31), channel_id=1, source_target_pairs={{0,1},{1,0},{2,3},{3,2},{4,5},{5,4},{6,7},{7,6},{8,9},{9,8},{10,11... | collective-permute-start | bytes 393224 | tf_op jit(solution)/shard_map/ppermute | solution.py:241
  7.8 10.9 %collective-permute-start.2 = (bf16[128,512]{1,0:T(8,128)(2,1)S(1)}, bf16[128,512]{1,0:T(8,128)(2,1)S(1)}, u32[]{:S(2)}, u32[]{:S(2)}) collective-permute-start(bf16[128,512]{1,0:T(8,128)(2,1)S(1)} %get-tuple-element.33), channel_id=1, source_target_pairs={{0,3},{1,2},{2,1},{3,0},{4,7},{5,6},{6,5},{7,4},{8,11},{9,10},{10,... | collective-permute-start | bytes 393224 | tf_op jit(solution)/shard_map/ppermute | solution.py:241
  14.1 8.6 %collective-permute-start.9 = (bf16[128,512]{1,0:T(8,128)(2,1)S(1)}, bf16[128,512]{1,0:T(8,128)(2,1)S(1)}, u32[]{:S(2)}, u32[]{:S(2)}) collective-permute-start(bf16[128,512]{1,0:T(8,128)(2,1)S(1)} %get-tuple-element.42), channel_id=1, source_target_pairs={{0,1},{1,0},{2,3},{3,2},{4,5},{5,4},{6,7},{7,6},{8,9},{9,8},{10,11... | collective-permute-start | bytes 393224 | tf_op jit(solution)/shard_map/ppermute | solution.py:241
  14.2 13.6 %collective-permute-start.7 = (bf16[128,512]{1,0:T(8,128)(2,1)S(1)}, bf16[128,512]{1,0:T(8,128)(2,1)S(1)}, u32[]{:S(2)}, u32[]{:S(2)}) collective-permute-start(bf16[128,512]{1,0:T(8,128)(2,1)S(1)} %get-tuple-element.39), channel_id=1, source_target_pairs={{0,2},{1,3},{2,0},{3,1},{4,6},{5,7},{6,4},{7,5},{8,10},{9,11},{10,... | collective-permute-start | bytes 393224 | tf_op jit(solution)/shard_map/ppermute | solution.py:241
  17.8 10.0 %collective-permute-start.8 = (bf16[128,512]{1,0:T(8,128)(2,1)S(1)}, bf16[128,512]{1,0:T(8,128)(2,1)S(1)}, u32[]{:S(2)}, u32[]{:S(2)}) collective-permute-start(bf16[128,512]{1,0:T(8,128)(2,1)S(1)} %get-tuple-element.40), channel_id=1, source_target_pairs={{0,3},{1,2},{2,1},{3,0},{4,7},{5,6},{6,5},{7,4},{8,11},{9,10},{10,... | collective-permute-start | bytes 393224 | tf_op jit(solution)/shard_map/ppermute | solution.py:241
  19.1 12.2 %collective-permute-start.3 = (bf16[128,512]{1,0:T(8,128)(2,1)S(1)}, bf16[128,512]{1,0:T(8,128)(2,1)S(1)}, u32[]{:S(2)}, u32[]{:S(2)}) collective-permute-start(bf16[128,512]{1,0:T(8,128)(2,1)S(1)} %get-tuple-element.35), channel_id=1, source_target_pairs={{0,8},{4,12},{8,0},{12,4},{16,24},{20,28},{24,16},{28,20},{1,9},{5... | collective-permute-start | bytes 393224 | tf_op jit(solution)/shard_map/ppermute | solution.py:241
  21.2 10.6 %collective-permute-start.4 = (bf16[128,512]{1,0:T(8,128)(2,1)S(1)}, bf16[128,512]{1,0:T(8,128)(2,1)S(1)}, u32[]{:S(2)}, u32[]{:S(2)}) collective-permute-start(bf16[128,512]{1,0:T(8,128)(2,1)S(1)} %get-tuple-element.36), channel_id=1, source_target_pairs={{0,16},{4,20},{8,24},{12,28},{16,0},{20,4},{24,8},{28,12},{1,17},{... | collective-permute-start | bytes 393224 | tf_op jit(solution)/shard_map/ppermute | solution.py:241
  22.8 9.1 %collective-permute-start.5 = (bf16[128,512]{1,0:T(8,128)(2,1)S(1)}, bf16[128,512]{1,0:T(8,128)(2,1)S(1)}, u32[]{:S(2)}, u32[]{:S(2)}) collective-permute-start(bf16[128,512]{1,0:T(8,128)(2,1)S(1)} %get-tuple-element.37), channel_id=1, source_target_pairs={{0,24},{4,28},{8,16},{12,20},{16,8},{20,12},{24,0},{28,4},{1,25},{... | collective-permute-start | bytes 393224 | tf_op jit(solution)/shard_map/ppermute | solution.py:241
  28.0 6.1 %collective-permute-start.12 = (bf16[128,512]{1,0:T(8,128)(2,1)S(1)}, bf16[128,512]{1,0:T(8,128)(2,1)S(1)}, u32[]{:S(2)}, u32[]{:S(2)}) collective-permute-start(bf16[128,512]{1,0:T(8,128)(2,1)S(1)} %get-tuple-element.45), channel_id=1, source_target_pairs={{0,16},{4,20},{8,24},{12,28},{16,0},{20,4},{24,8},{28,12},{1,17},{... | collective-permute-start | bytes 393224 | tf_op jit(solution)/shard_map/ppermute | solution.py:241
  29.7 5.9 %collective-permute-start.13 = (bf16[128,512]{1,0:T(8,128)(2,1)S(1)}, bf16[128,512]{1,0:T(8,128)(2,1)S(1)}, u32[]{:S(2)}, u32[]{:S(2)}) collective-permute-start(bf16[128,512]{1,0:T(8,128)(2,1)S(1)} %get-tuple-element.46), channel_id=1, source_target_pairs={{0,24},{4,28},{8,16},{12,20},{16,8},{20,12},{24,0},{28,4},{1,25},{... | collective-permute-start | bytes 393224 | tf_op jit(solution)/shard_map/ppermute | solution.py:241
  31.3 5.0 %collective-permute-start.10 = (bf16[64,512]{1,0:T(8,128)(2,1)S(1)}, bf16[64,512]{1,0:T(8,128)(2,1)S(1)}, u32[]{:S(2)}, u32[]{:S(2)}) collective-permute-start(bf16[64,512]{1,0:T(8,128)(2,1)S(1)} %get-tuple-element.43), channel_id=1, source_target_pairs={{0,8},{4,12},{8,0},{12,4},{16,24},{20,28},{24,16},{28,20},{1,9},{5... | collective-permute-start | bytes 196616 | tf_op jit(solution)/shard_map/ppermute | solution.py:241
  31.9 4.4 %collective-permute-start.11 = (bf16[64,512]{1,0:T(8,128)(2,1)S(1)}, bf16[64,512]{1,0:T(8,128)(2,1)S(1)}, u32[]{:S(2)}, u32[]{:S(2)}) collective-permute-start(bf16[64,512]{1,0:T(8,128)(2,1)S(1)} %get-tuple-element.44), channel_id=1, source_target_pairs={{0,12},{4,8},{8,4},{12,0},{16,28},{20,24},{24,20},{28,16},{1,13},{... | collective-permute-start | bytes 196616 | tf_op jit(solution)/shard_map/ppermute | solution.py:241
  32.2 4.4 %collective-permute-start.6 = (bf16[256,512]{1,0:T(8,128)(2,1)S(1)}, bf16[256,512]{1,0:T(8,128)(2,1)S(1)}, u32[]{:S(2)}, u32[]{:S(2)}) collective-permute-start(bf16[256,512]{1,0:T(8,128)(2,1)S(1)} %shard_map.42), channel_id=1, source_target_pairs={{0,4},{4,0},{8,12},{12,8},{16,20},{20,16},{24,28},{28,24},{1,5},{5... | collective-permute-start | bytes 786440 | tf_op jit(solution)/shard_map/ppermute | solution.py:241
  35.5 1.5 %collective-permute-start.14 = (bf16[192,512]{1,0:T(8,128)(2,1)S(1)}, bf16[192,512]{1,0:T(8,128)(2,1)S(1)}, u32[]{:S(2)}, u32[]{:S(2)}) collective-permute-start(bf16[192,512]{1,0:T(8,128)(2,1)S(1)} %shard_map.51), channel_id=1, source_target_pairs={{0,4},{4,0},{8,12},{12,8},{16,20},{20,16},{24,28},{28,24},{1,5},{5... | collective-permute-start | bytes 589832 | tf_op jit(solution)/shard_map/ppermute | solution.py:241
